TPU v7x, 32 devices: a whole 2x2x4 slice. The times are simulated.
32 devices in a mesh: grp: 2 (over y), wide: 8 (over z, core), pair: 2 (over x).
Axes of the slice: x: 2, y: 2, z: 4, core: 2. Of those that a mesh axis runs over, the one named last changes fastest.
Arguments:
- amplitudes: bfloat16 [2048, 3584], P(('grp', 'wide', 'pair')), parts along dimension 0, may hold values from -6 to 6
- integrals: bfloat16 [7168, 3584], P(('grp', 'wide'), 'pair'), parts along dimension 0, may hold values from -0.1875 to 0.1875
- tile_list: int32 [32, 28], P('grp'), parts along dimension 0, may hold values from 0 to 55, all different within a row
- slab_order: int32 [32], P('grp'), parts along dimension 0, may hold values from 0 to 15, each once
- block_list: int32 [112, 2, 14], P('grp'), parts along dimension 0, may hold values from 0 to 27, all different within a row
Outputs:
- ladder: float32 [2048, 3584], P(('grp', 'wide', 'pair')), parts along dimension 0
There are 2 independent parts, one for each index of `grp`. A program takes and returns all parts, laid end to end along the dimension named above; each array names one. Nothing has to cross between parts.
Inputs may be any that keep to these rules, and one draw needn't show every extreme that they name: `tile_list`: each row names 28 different tiles, and every tile is named by some row. `slab_order`: each tile position holds a different occupied-pair tile. `block_list`: each last-dimension row names 14 different tiles of its group.
All inputs are finite; a program needn't handle non-finite values.
Results may differ from a plain program's by a relative error of at most 0.0003.
Values may be sent and summed in bfloat16 or wider, within the bound.
No kernel may reach another device: no remote copies, remote signals or barrier semaphores. Data moves between devices by JAX's collectives and lax.ppermute only.
A program may use at most 192 MiB of HBM per device.

v0:
```python
import jax
import jax.numpy as jnp
from jax import lax
from jax.sharding import PartitionSpec as P

BLK = 64


def body(amplitudes, integrals, tile_list, slab_order, block_list):
    rows_dev, virt_cols = amplitudes.shape
    virt_tiles = virt_cols // BLK
    own_count = rows_dev // BLK
    pair_count = lax.axis_size("pair")
    group_count = own_count * pair_count
    wide_index = lax.axis_index("wide")
    pair_index = lax.axis_index("pair")
    slab_ids = lax.dynamic_slice_in_dim(slab_order, wide_index * group_count, group_count)
    own_ids = lax.dynamic_slice_in_dim(slab_ids, pair_index * own_count, own_count)
    own_lists = jnp.take(tile_list, own_ids, axis=0)
    tiles_four = amplitudes.reshape(own_count, BLK, virt_tiles, BLK)
    tile_ids = jnp.arange(virt_tiles, dtype=jnp.int32)
    present = jnp.any(own_lists[:, :, None] == tile_ids[None, None, :], axis=1).astype(
        amplitudes.dtype
    )
    masked = (tiles_four * present[:, None, :, None]).reshape(rows_dev, virt_cols)
    slab_rows = lax.all_gather(masked, "pair", axis=0, tiled=True)
    group_tiles = integrals.shape[1] // BLK
    my_lists = lax.dynamic_index_in_dim(block_list, pair_index, 1, keepdims=False)
    group_ids = jnp.arange(group_tiles, dtype=jnp.int32)
    live = jnp.any(my_lists[:, :, None] == group_ids[None, None, :], axis=1).astype(integrals.dtype)
    shard_block = lax.all_gather(integrals, "wide", axis=0, tiled=True)
    qtiles = shard_block.shape[0] // BLK
    masked_block = shard_block.reshape(qtiles, BLK, group_tiles, BLK) * live[:, None, :, None]
    masked_block = masked_block.reshape(shard_block.shape)
    ladder_slab = jnp.dot(slab_rows, masked_block, preferred_element_type=jnp.float32)
    return lax.all_to_all(ladder_slab, "pair", split_axis=0, concat_axis=1, tiled=True)


def solution(mesh):
    placed = (
        P(("grp", "wide", "pair"), None),
        P(("grp", "wide"), "pair"),
        P("grp", None),
        P("grp"),
        P("grp", None, None),
    )
    return jax.shard_map(
        body,
        mesh=mesh,
        in_specs=placed,
        out_specs=P(("grp", "wide", "pair"), None),
        check_vma=False,
    )
```

profile of v0, /device:TPU:0, one launch (start us, length us, event | category | flops | bytes accessed | tf_op | source)
XLA Modules:
  0.0 182.3 jit_solution(8919941252359138682)
XLA Ops:
  6.5 0.0 copy-start
  6.5 0.0 all-gather.2.cloned.1.call-start
  6.5 0.7 all-gather.2.cloned.1.call-update
  7.3 1.2 dynamic_slice.11
  10.5 0.7 fusion.5
  11.2 0.1 fusion.4
  11.3 0.1 mul.30
  11.3 0.1 mul.31
  11.4 0.0 copy-done
  11.5 9.5 %mul.34 = bf16[56,64,28,64]{1,0,3,2:T(8,128)(2,1)} broadcast(bf16[56,28]{0,1:T(8,128)(2,1)S(1)} %convert_element_type.17), dimensions={0,2} | broadcast | bytes 12848192 | tf_op jit(solution)/shard_map/mul | solution.py:33
  21.0 0.0 copy-start.2
  21.0 31.0 %mul.35 = bf16[3584,1792]{0,1:T(8,128)(2,1)} reshape(bf16[56,64,28,64]{1,0,3,2:T(8,128)(2,1)} %mul.34) | data formatting | bytes 25690112 | tf_op jit(solution)/shard_map/mul | solution.py:33
  52.0 0.0 copy-done.2
  52.1 14.8 %all_gather.6 = bf16[128,3584]{1,0:T(8,128)(2,1)S(1)} all-gather(bf16[64,3584]{1,0:T(8,128)(2,1)S(1)} %broadcast_multiply_fusion), channel_id=1, replica_groups=mesh['grp'=2,'wide'=8,'pair'=2] {'pair'}, dimensions={0}, use_global_device_ids=true | all-gather | bytes 1376256 | tf_op jit(solution)/shard_map/all_gather | solution.py:26
  66.9 63.8 %all-gather.2.cloned.1.call-done = bf16[3584,1792]{1,0:T(8,128)(2,1)} async-done(((bf16[448,1792]{1,0:T(8,128)(2,1)}), bf16[3584,1792]{1,0:T(8,128)(2,1)}) %all-gather.2.cloned.1.call-update) | async-done | bytes 12845072 | tf_op jit(solution)/shard_map/all_gather | solution.py:31
  130.6 18.0 %copy.17 = bf16[3584,1792]{0,1:T(8,128)(2,1)} copy(bf16[3584,1792]{1,0:T(8,128)(2,1)} %all-gather.2.cloned.1.call-done) | data formatting | bytes 25690112 | tf_op jit(solution)/shard_map/all_gather | solution.py:31
  148.7 0.0 copy-start.1
  148.7 10.5 %fusion = f32[2,64,1792]{2,1,0:T(8,128)S(1)} fusion(bf16[2,64,3584]{2,1,0:T(8,128)(2,1)S(1)} %bitcast.19, bf16[3584,1792]{0,1:T(8,128)(2,1)} %copy.17, bf16[3584,1792]{0,1:T(8,128)(2,1)} %mul.35), kind=kOutput, calls=%fused_computation | convolution fusion | flops 1650589696 | bytes 27525120 | tf_op jit(solution)/shard_map/dot_general | solution.py:35
  159.1 15.3 %all_to_all.16 = f32[2,64,1792]{2,1,0:T(8,128)S(1)} all-to-all(f32[2,64,1792]{2,1,0:T(8,128)S(1)} %fusion), channel_id=1, replica_groups=mesh['grp'=2,'wide'=8,'pair'=2] {'pair'}, dimensions={0} | all-to-all | bytes 1835008 | tf_op jit(solution)/shard_map/all_to_all | solution.py:36
  174.5 1.0 copy.23
  175.5 0.0 copy-done.1
  (6 shorter events, 0.1 us)
Async XLA Ops:
  6.5 4.9 %copy-start = (s32[56,2,14]{0,1,2:T(2,128)S(1)}, s32[56,2,14]{0,1,2:T(2,128)}, u32[]{:S(2)}) copy-start(s32[56,2,14]{0,1,2:T(2,128)} %param.9) | copy-start | bytes 18820
  6.5 124.1 %all-gather.2.cloned.1.call-start = ((), (), s32[]{:S(2)}) async-start(), calls=%async_computation.1 | async-start | bytes 14450688 | tf_op jit(solution)/shard_map/all_gather | solution.py:31
  21.0 31.0 %copy-start.2 = (bf16[64,3584]{1,0:T(8,128)(2,1)S(1)}, bf16[64,3584]{1,0:T(8,128)(2,1)}, u32[]{:S(2)}) copy-start(bf16[64,3584]{1,0:T(8,128)(2,1)} %param.5) | copy-start | bytes 1376260
  148.7 26.8 %copy-start.1 = (s32[56,2,14]{0,1,2:T(2,128)S(1)}, s32[56,2,14]{0,1,2:T(2,128)}, u32[]{:S(2)}) copy-start(s32[56,2,14]{0,1,2:T(2,128)} %param.9) | copy-start | bytes 18820
Sparse Core Ops, SparseCore 0:
  9.0 121.5 all-gather.1
where the time goes:
time: 184 us; the launch traced here: 182 us
  waiting for transfers between devices  64.5 us (35%)
  local copies, waits for them, and re-layouts  60.9 us (33%)
  blocking collectives  30.1 us (16%)
  between operations  15.4 us (8%)
  matrix products  10.5 us (6%)
    all_gather x1, waiting for transfers between devices, body(): shard_block = lax.all_gather(integrals, 'wide', axis=0, tiled=True)  63.8 us
    mul x2, local copies, waits for them, and re-layouts, body(): shard_block.reshape(qtiles, BLK, group_tiles, BLK) * live[:, None, :, None]  40.5 us
    all_gather x1, local copies, waits for them, and re-layouts, body(): shard_block = lax.all_gather(integrals, 'wide', axis=0, tiled=True)  18 us
    all_to_all x1, blocking collectives, body(): lax.all_to_all(ladder_slab, 'pair', split_axis=0, concat_axis=1, tiled=True)  15.3 us
    all_gather x1, blocking collectives, body(): slab_rows = lax.all_gather(masked, 'pair', axis=0, tiled=True)  14.8 us
    dot_general x1, matrix products, body(): jnp.dot(slab_rows, masked_block, preferred_element_type=jnp.float32)  10.5 us
  transfers between devices with their start and end apart: 1, of which 1 were waited for; matrix products, arithmetic and copies ran while one was open for 23% of the time, Pallas kernels for 0%

commit v1 on v0

--- a/solution.py
+++ b/solution.py
@@ -1,12 +1,22 @@
+import functools
+
 import jax
 import jax.numpy as jnp
 from jax import lax
+from jax.experimental import pallas as pl
+from jax.experimental.pallas import tpu as pltpu
 from jax.sharding import PartitionSpec as P
 
 BLK = 64
-
-
-def body(amplitudes, integrals, tile_list, slab_order, block_list):
+LANES = 128
+GROUP = 256
+LOW_EXP = -100.0
+VMEM = pl.BlockSpec(memory_space=pltpu.VMEM)
+SMEM = pl.BlockSpec(memory_space=pltpu.SMEM)
+PARAMS = pltpu.CompilerParams(vmem_limit_bytes=48 * 1024 * 1024)
+
+
+def gather_body(amplitudes, integrals, tile_list, slab_order, block_list):
     rows_dev, virt_cols = amplitudes.shape
     virt_tiles = virt_cols // BLK
     own_count = rows_dev // BLK
@@ -36,6 +46,275 @@
     return lax.all_to_all(ladder_slab, "pair", split_axis=0, concat_axis=1, tiled=True)
 
 
+def low_lanes(rows):
+    return lax.broadcasted_iota(jnp.int32, (rows, LANES), 1) < BLK
+
+
+def half(index):
+    return pl.ds(pl.multiple_of((index // 2) * LANES, LANES), LANES)
+
+
+def pack_kernel(lists, block_ref, first_ref, second_ref):
+    wide, pair = lax.axis_index("wide"), lax.axis_index("pair")
+    tiles = block_ref.shape[0] // BLK
+    keep = first_ref.shape[1] // BLK
+    split = first_ref.shape[0] // BLK
+    low = low_lanes(BLK)
+    for i in range(tiles):
+        out, row = (first_ref, i) if i < split else (second_ref, i - split)
+        base = ((wide * tiles + i) * 2 + pair) * keep
+        rows = pl.ds(i * BLK, BLK)
+        for j in range(keep // 2):
+            even, odd = lists[base + 2 * j], lists[base + 2 * j + 1]
+            left = pltpu.roll(block_ref[rows, half(even)], (even % 2) * BLK, 1)
+            right = pltpu.roll(block_ref[rows, half(odd)], BLK - (odd % 2) * BLK, 1)
+            out[row * BLK : (row + 1) * BLK, j * LANES : (j + 1) * LANES] = jnp.where(
+                low, left, right
+            )
+
+
+def mask_kernel(tile_list, slab_order, amp_ref, own_ref, far_ref, present, masked):
+    wide, pair = lax.axis_index("wide"), lax.axis_index("pair")
+    count = amp_ref.shape[1] // BLK
+    keep = tile_list.shape[1]
+    tile = slab_order[wide * 2 + pair]
+    for t in range(count):
+        present[t] = 0
+    for k in range(keep):
+        present[tile_list[tile, k]] = 1
+    low = lax.broadcasted_iota(jnp.int32, (BLK, LANES), 1) < BLK
+    for s in range(count // 2):
+        cols = slice(s * LANES, (s + 1) * LANES)
+        flag = jnp.where(low, present[2 * s], present[2 * s + 1])
+        masked[:, cols] = jnp.where(flag > 0, amp_ref[:, cols], 0)
+    mine = wide // 4
+    part = amp_ref.shape[1] // 8
+    room = own_ref.shape[1] // 4
+    for side, out in ((mine, own_ref), (1 - mine, far_ref)):
+        rows = masked[:, pl.ds(pl.multiple_of(side * 4 * part, LANES), 4 * part)]
+        for w in range(4):
+            out[:, w * room : w * room + part] = rows[:, w * part : (w + 1) * part]
+            out[:, w * room + part : (w + 1) * room] = jnp.zeros((BLK, room - part), out.dtype)
+
+
+def gather_rows(amps, rows_ref, source, offset, depth, room):
+    cols = pl.ds(pl.multiple_of(source * room + offset, LANES), depth)
+    for n, amp in enumerate(amps):
+        rows_ref[n * BLK : (n + 1) * BLK, 0:depth] = amp[:, cols]
+
+
+def raw_kernel(place, own_ref, near_ref, a0, a1, a2, a3, acc_ref, dense, rows):
+    wide = lax.axis_index("wide")
+    tiles = own_ref.shape[0] // BLK
+    group = own_ref.shape[1] // BLK
+    depth = own_ref.shape[0]
+    room = a0.shape[1] // 4
+    low = low_lanes(BLK)
+    for n, (block, source) in enumerate(((own_ref, wide), (near_ref, wide ^ 1))):
+        for i in range(tiles):
+            here = slice(i * BLK, (i + 1) * BLK)
+            base = (source * tiles + i) * group
+            for s in range(group // 2):
+                cols = slice(s * LANES, (s + 1) * LANES)
+                flag = jnp.where(low, place[base + 2 * s], place[base + 2 * s + 1])
+                dense[here, cols] = jnp.where(flag >= 0, block[here, cols], 0)
+        gather_rows((a0, a1, a2, a3), rows, source % 4, 0, depth, room)
+        product = jnp.dot(rows[...], dense[...], preferred_element_type=jnp.float32)
+        if n == 0:
+            acc_ref[...] = product
+        else:
+            acc_ref[...] += product
+
+
+def spread(place, packed, swapped, dense, source_row):
+    tiles = packed.shape[0] // BLK
+    keep = packed.shape[1] // BLK
+    group = dense.shape[1] // BLK
+    low = low_lanes(BLK)
+    for j in range(keep // 2):
+        cols = slice(j * LANES, (j + 1) * LANES)
+        swapped[0, :, cols] = packed[:, cols]
+        swapped[1, :, cols] = pltpu.roll(packed[:, cols], BLK, 1)
+    for i in range(tiles):
+        here = slice(i * BLK, (i + 1) * BLK)
+        base = (source_row + i) * group
+        for s in range(group // 2):
+            even, odd = place[base + 2 * s], place[base + 2 * s + 1]
+            left_at, right_at = jnp.maximum(even, 0), jnp.maximum(odd, 0)
+            left = swapped[left_at % 2, here, half(left_at)]
+            right = swapped[1 - right_at % 2, here, half(right_at)]
+            flag = jnp.where(low, even, odd)
+            dense[here, s * LANES : (s + 1) * LANES] = jnp.where(
+                flag >= 0, jnp.where(low, left, right), 0
+            )
+
+
+def packed_product(place, blocks, amps, first_tile, swapped, dense, rows):
+    wide = lax.axis_index("wide")
+    depth = blocks[0].shape[0]
+    room = amps[0].shape[1] // 4
+    tiles = room // BLK - 1
+    total = None
+    for block, source in zip(blocks, (wide ^ 2, wide ^ 3)):
+        spread(place, block, swapped, dense, source * tiles + first_tile)
+        gather_rows(amps, rows, source % 4, first_tile * BLK, depth, room)
+        product = jnp.dot(rows[...], dense[...], preferred_element_type=jnp.float32)
+        total = product if total is None else total + product
+    return total
+
+
+def first_kernel(place, z_ref, y_ref, a0, a1, a2, a3, acc_ref, sum_ref, swapped, dense, rows):
+    product = packed_product(place, (z_ref, y_ref), (a0, a1, a2, a3), 0, swapped, dense, rows)
+    sum_ref[...] = acc_ref[...] + product
+
+
+def encode(values, out):
+    width = values.shape[1]
+    lane = lax.broadcasted_iota(jnp.int32, (BLK, LANES), 1)
+    exps = jnp.zeros((BLK, LANES), jnp.int32)
+    for g in range(width // GROUP):
+        part = values[:, g * GROUP : (g + 1) * GROUP]
+        top = jnp.max(jnp.abs(part), axis=1, keepdims=True)
+        exp = jnp.maximum(jnp.ceil(jnp.log2(jnp.maximum(top, 2.0**LOW_EXP))), LOW_EXP)
+        scaled = jnp.clip(jnp.round(part * jnp.exp2(15.0 - exp)), -32767.0, 32767.0)
+        out[:, g * GROUP : (g + 1) * GROUP] = scaled.astype(jnp.int32).astype(jnp.int16)
+        exps = jnp.where(lane == g, exp.astype(jnp.int32), exps)
+    out[:, width : width + LANES] = exps.astype(jnp.int16)
+
+
+def last_kernel(
+    place, z_ref, y_ref, a0, a1, a2, a3, acc_ref, keep_ref, send_ref, same_ref, cross_ref,
+    swapped, dense, rows,
+):
+    first_tile = a0.shape[1] // 4 // BLK - 1 - z_ref.shape[0] // BLK
+    product = packed_product(
+        place, (z_ref, y_ref), (a0, a1, a2, a3), first_tile, swapped, dense, rows
+    )
+    total = acc_ref[...] + product
+    keep_ref[...] = total[0 * BLK : 1 * BLK]
+    send_ref[...] = total[1 * BLK : 2 * BLK]
+    encode(total[2 * BLK : 3 * BLK], same_ref)
+    encode(total[3 * BLK : 4 * BLK], cross_ref)
+
+
+def join_kernel(keep_ref, got_ref, same_ref, cross_ref, out_ref):
+    pair = lax.axis_index("pair")
+    width = keep_ref.shape[1]
+    for side, base, coded in ((pair, keep_ref, same_ref), (1 - pair, got_ref, cross_ref)):
+        exps = coded[:, width : width + LANES].astype(jnp.int32).astype(jnp.float32)
+        for g in range(width // GROUP):
+            cols = slice(g * GROUP, (g + 1) * GROUP)
+            scale = jnp.exp2(exps[:, g : g + 1] - 15.0)
+            value = coded[:, cols].astype(jnp.int32).astype(jnp.float32) * scale
+            where = pl.ds(pl.multiple_of(side * width + g * GROUP, LANES), GROUP)
+            out_ref[:, where] = base[:, cols] + value
+
+
+def call(kernel, out, operands, smem, scratch=(), flops=0):
+    moved = sum(a.size * a.dtype.itemsize for a in operands)
+    return pl.pallas_call(
+        kernel,
+        out_shape=out,
+        in_specs=[SMEM] * smem + [VMEM] * (len(operands) - smem),
+        out_specs=jax.tree.map(lambda _: VMEM, out),
+        scratch_shapes=list(scratch),
+        compiler_params=PARAMS,
+        cost_estimate=pl.CostEstimate(flops=flops, bytes_accessed=moved, transcendentals=0),
+    )(*operands)
+
+
+def swap_body(amplitudes, integrals, tile_list, slab_order, block_list):
+    wide_count, pair_count = lax.axis_size("wide"), lax.axis_size("pair")
+    depth, width = integrals.shape
+    tiles, group = depth // BLK, width // BLK
+    keep = block_list.shape[2]
+    bf16, f32, i16 = jnp.bfloat16, jnp.float32, jnp.int16
+    sds = jax.ShapeDtypeStruct
+
+    def move(x, flip_wide, flip_pair=0):
+        if flip_wide and flip_pair:
+            n = wide_count * pair_count
+            flip = flip_wide * pair_count + flip_pair
+            return lax.ppermute(x, ("wide", "pair"), [(i, i ^ flip) for i in range(n)])
+        if flip_wide:
+            return lax.ppermute(x, "wide", [(i, i ^ flip_wide) for i in range(wide_count)])
+        return lax.ppermute(x, "pair", [(i, i ^ flip_pair) for i in range(pair_count)])
+
+    split = (tiles + 1) // 2
+    cut = split * BLK
+    first, second = call(
+        pack_kernel,
+        (sds((cut, keep * BLK), bf16), sds((depth - cut, keep * BLK), bf16)),
+        (block_list.reshape(-1), integrals),
+        1,
+    )
+    room = depth + BLK
+    own, far = call(
+        mask_kernel,
+        (sds((BLK, 4 * room), bf16),) * 2,
+        (tile_list, slab_order, amplitudes),
+        2,
+        [pltpu.SMEM((amplitudes.shape[1] // BLK,), jnp.int32), pltpu.VMEM(amplitudes.shape, bf16)],
+    )
+    near = move(integrals, 1)
+    z_first = move(first, 2)
+    z_second = move(second, 2)
+    far_same = move(far, 4)
+    own_cross = move(own, 0, 1)
+    far_cross = move(far_same, 0, 1)
+    amps = (own, own_cross, far_same, far_cross)
+
+    my_lists = lax.dynamic_index_in_dim(block_list, lax.axis_index("pair"), 1, keepdims=False)
+    hit = my_lists[:, :, None] == jnp.arange(group, dtype=jnp.int32)[None, None, :]
+    order = jnp.arange(1, keep + 1, dtype=jnp.int32)[None, :, None]
+    place = (jnp.sum(jnp.where(hit, order, 0), axis=1) - 1).reshape(-1)
+
+    rows = 4 * BLK
+    acc = call(
+        raw_kernel,
+        sds((rows, width), f32),
+        (place, integrals, near, *amps),
+        1,
+        [pltpu.VMEM((depth, width), bf16), pltpu.VMEM((rows, depth), bf16)],
+        2 * 2 * rows * depth * width,
+    )
+    y_first = move(z_first, 1)
+    y_second = move(z_second, 1)
+
+    def scratch(n):
+        return [
+            pltpu.VMEM((2, n, keep * BLK), bf16),
+            pltpu.VMEM((n, width), bf16),
+            pltpu.VMEM((rows, n), bf16),
+        ]
+
+    acc = call(
+        first_kernel,
+        sds((rows, width), f32),
+        (place, z_first, y_first, *amps, acc),
+        1,
+        scratch(cut),
+        2 * 2 * rows * cut * width,
+    )
+    keep_rows, send_rows, same, cross = call(
+        last_kernel,
+        (sds((BLK, width), f32),) * 2 + (sds((BLK, width + LANES), i16),) * 2,
+        (place, z_second, y_second, *amps, acc),
+        1,
+        scratch(depth - cut),
+        2 * 2 * rows * (depth - cut) * width,
+    )
+    same = move(same, 4)
+    cross = move(cross, 4, 1)
+    got = move(send_rows, 0, 1)
+    return call(
+        join_kernel,
+        sds((BLK, pair_count * width), f32),
+        (keep_rows, got, same, cross),
+        0,
+    )
+
+
 def solution(mesh):
     placed = (
         P(("grp", "wide", "pair"), None),
@@ -44,8 +323,9 @@
         P("grp"),
         P("grp", None, None),
     )
+    swapped = mesh.shape["wide"] == 8 and mesh.shape["pair"] == 2
     return jax.shard_map(
-        body,
+        swap_body if swapped else gather_body,
         mesh=mesh,
         in_specs=placed,
         out_specs=P(("grp", "wide", "pair"), None),

time: 184 us -> 70.8 us (0.38)
  local copies, waits for them, and re-layouts: 60.9 us -> 4.95 us
  blocking collectives: 30.1 us -> 0 us
  waiting for transfers between devices: 64.5 us -> 37 us
  between operations: 15.4 us -> 0.12 us
  Pallas kernels: 0 us -> 14.2 us
  starting transfers between devices: 0.01 us -> 14.1 us
  matrix products: 10.5 us -> 0 us
    all_gather x1 -> x0, waiting for transfers between devices: 63.8 us -> none  [body(): shard_block = lax.all_gather(integrals, 'wide', axis=0, tiled=True)]
    mul x4 -> x0, local copies, waits for them, and re-layouts: 40.7 us -> none  [the longest x2 40.5 us: body(): shard_block.reshape(qtiles, BLK, group_tiles, BLK) * live[:, None, :, None]]
    ppermute x0 -> x11, waiting for transfers between devices: none -> 37 us  [the longest x7 18.1 us: move(): lax.ppermute(x, 'wide', [(i, i ^ flip_wide) for i in range(wide_count)])]
    all_gather x1 -> x0, local copies, waits for them, and re-layouts: 18 us -> none  [body(): shard_block = lax.all_gather(integrals, 'wide', axis=0, tiled=True)]
    all_to_all x1 -> x0, blocking collectives: 15.3 us -> none  [body(): lax.all_to_all(ladder_slab, 'pair', split_axis=0, concat_axis=1, tiled=True)]
    all_gather x1 -> x0, blocking collectives: 14.8 us -> none  [body(): slab_rows = lax.all_gather(masked, 'pair', axis=0, tiled=True)]
    pallas_call x0 -> x6, Pallas kernels: none -> 14.2 us  [call(): pl.pallas_call(kernel, out_shape=out, in_specs=[SMEM] * smem + [VMEM] * (...]
    ppermute x0 -> x11, starting transfers between devices: none -> 14.1 us  [the longest x7 7.25 us: move(): lax.ppermute(x, 'wide', [(i, i ^ flip_wide) for i in range(wide_count)])]
  transfers between devices with their start and end apart: 1 -> 11, of which waited for: 1 -> 5; matrix products, arithmetic and copies ran while one was open for 23% -> 2% of each run, Pallas kernels for 0% -> 14%
where the time goes in v1:
time: 70.8 us; the launch traced here: 70.5 us
  waiting for transfers between devices  37 us (52%)
  Pallas kernels  14.2 us (20%)
  starting transfers between devices  14.1 us (20%)
  local copies, waits for them, and re-layouts  4.95 us (7%)
    ppermute x7, waiting for transfers between devices, move(): lax.ppermute(x, 'wide', [(i, i ^ flip_wide) for i in range(wide_count)])  18.1 us
    ppermute x1, waiting for transfers between devices, move(): return lax.ppermute(x, ('wide', 'pair'), [(i, i ^ flip) for i in range(n)])  17.3 us
    pallas_call x6, Pallas kernels, call(): pl.pallas_call(kernel, out_shape=out, in_specs=[SMEM] * smem + [VMEM] * (...  14.2 us
    ppermute x7, starting transfers between devices, move(): lax.ppermute(x, 'wide', [(i, i ^ flip_wide) for i in range(wide_count)])  7.25 us
    ppermute x3, starting transfers between devices, move(): lax.ppermute(x, 'pair', [(i, i ^ flip_pair) for i in range(pair_count)])  5.23 us
    unnamed x14, local copies, waits for them, and re-layouts  4.61 us
    ppermute x1, starting transfers between devices, move(): return lax.ppermute(x, ('wide', 'pair'), [(i, i ^ flip) for i in range(n)])  1.6 us
    ppermute x3, waiting for transfers between devices, move(): lax.ppermute(x, 'pair', [(i, i ^ flip_pair) for i in range(pair_count)])  1.58 us
  transfers between devices with their start and end apart: 11, of which 5 were waited for; matrix products, arithmetic and copies ran while one was open for 2% of the time, Pallas kernels for 14%

profile of v1, /device:TPU:0, one launch (start us, length us, event | category | flops | bytes accessed | tf_op | source)
XLA Modules:
  0.0 70.5 jit_solution(2675620143527916946)
XLA Ops:
  0.0 0.0 copy-start.5
  0.0 0.5 collective-permute-start.7
  0.5 0.8 %copy.11 = s32[56,2,14]{2,1,0:T(2,128)S(1)} copy(s32[56,2,14]{0,1,2:T(2,128)} %param.9) | data formatting | bytes 12544 | tf_op args[4]
  1.3 0.1 reshape.13.lists
  1.4 0.0 copy-start
  1.4 1.4 %copy-done = bf16[448,1792]{1,0:T(8,128)(2,1)S(1)} copy-done((bf16[448,1792]{1,0:T(8,128)(2,1)S(1)}, bf16[448,1792]{1,0:T(8,128)(2,1)}, u32[]{:S(2)}) %copy-start) | copy-done | bytes 1605656
  2.8 0.0 copy-start.1
  2.8 2.2 %shard_map.55 = (bf16[256,896]{1,0:T(8,128)(2,1)}, bf16[192,896]{1,0:T(8,128)(2,1)}) custom-call(s32[1568]{0:T(1024)S(1)} %reshape.13.lists, bf16[448,1792]{1,0:T(8,128)(2,1)S(1)} %copy-done), custom_call_target="tpu_custom_call" | custom-call | bytes 1611904 | tf_op jit(solution)/shard_map/pallas_call | solution.py:215
  5.1 2.6 %collective-permute-start.5 = (bf16[256,896]{1,0:T(8,128)(2,1)}, bf16[256,896]{1,0:T(8,128)(2,1)S(1)}, u32[]{:S(2)}, u32[]{:S(2)}) collective-permute-start(bf16[256,896]{1,0:T(8,128)(2,1)} %get-tuple-element.16), channel_id=1, source_target_pairs={{0,4},{2,6},{4,0},{6,2},{8,12},{10,14},{12,8},{14,10},{1,5},{3,7},... | collective-permute-start | bytes 1376264 | tf_op jit(solution)/shard_map/ppermute | solution.py:240
  7.7 0.0 copy-start.2
  7.7 1.0 %copy-done.2 = bf16[64,3584]{1,0:T(8,128)(2,1)S(1)} copy-done((bf16[64,3584]{1,0:T(8,128)(2,1)S(1)}, bf16[64,3584]{1,0:T(8,128)(2,1)}, u32[]{:S(2)}) %copy-start.2) | copy-done | bytes 458776
  8.7 0.0 copy-start.3
  8.7 0.7 copy-done.3
  9.4 0.0 copy-start.4
  9.4 0.7 copy-done.4
  10.1 1.0 %shard_map.56 = (bf16[64,2048]{1,0:T(8,128)(2,1)S(1)}, bf16[64,2048]{1,0:T(8,128)(2,1)S(1)}) custom-call(s32[16,28]{1,0:T(8,128)S(1)} %copy-done.3, s32[16]{0:T(128)S(1)} %copy-done.4, bf16[64,3584]{1,0:T(8,128)(2,1)S(1)} %copy-done.2), custom_call_target="tpu_custom_call" | custom-call | bytes 460608 | tf_op jit(solution)/shard_map/pallas_call | solution.py:215
  11.1 2.7 %collective-permute-start.3 = (bf16[64,2048]{1,0:T(8,128)(2,1)S(1)}, bf16[64,2048]{1,0:T(8,128)(2,1)S(1)}, u32[]{:S(2)}, u32[]{:S(2)}) collective-permute-start(bf16[64,2048]{1,0:T(8,128)(2,1)S(1)} %get-tuple-element.15), channel_id=1, source_target_pairs={{0,8},{2,10},{4,12},{6,14},{8,0},{10,2},{12,4},{14,6},{1,9},{3,11}... | collective-permute-start | bytes 786440 | tf_op jit(solution)/shard_map/ppermute | solution.py:240
  13.8 0.4 collective-permute-start
  14.2 1.5 %collective-permute-start.2 = (bf16[64,2048]{1,0:T(8,128)(2,1)S(1)}, bf16[64,2048]{1,0:T(8,128)(2,1)S(1)}, u32[]{:S(2)}, u32[]{:S(2)}) collective-permute-start(bf16[64,2048]{1,0:T(8,128)(2,1)S(1)} %get-tuple-element.14.a0), channel_id=1, source_target_pairs={{0,1},{1,0},{2,3},{3,2},{4,5},{5,4},{6,7},{7,6},{8,9},{9,8},{10,11... | collective-permute-start | bytes 786440 | tf_op jit(solution)/shard_map/ppermute | solution.py:241
  15.7 0.0 copy-done.5
  15.7 9.2 %collective-permute-done.5.z_ref = bf16[256,896]{1,0:T(8,128)(2,1)S(1)} collective-permute-done((bf16[256,896]{1,0:T(8,128)(2,1)}, bf16[256,896]{1,0:T(8,128)(2,1)S(1)}, u32[]{:S(2)}, u32[]{:S(2)}) %collective-permute-start.5) | collective-permute-done | bytes 458784 | tf_op jit(solution)/shard_map/ppermute | solution.py:240
  24.9 0.0 collective-permute-start.6
  24.9 0.0 collective-permute-done.3.a2
  24.9 1.9 %collective-permute-start.4 = (bf16[64,2048]{1,0:T(8,128)(2,1)S(1)}, bf16[64,2048]{1,0:T(8,128)(2,1)S(1)}, u32[]{:S(2)}, u32[]{:S(2)}) collective-permute-start(bf16[64,2048]{1,0:T(8,128)(2,1)S(1)} %collective-permute-done.3.a2), channel_id=1, source_target_pairs={{0,1},{1,0},{2,3},{3,2},{4,5},{5,4},{6,7},{7,6},{8,9},{9,8},{10,11... | collective-permute-start | bytes 786440 | tf_op jit(solution)/shard_map/ppermute | solution.py:241
  26.9 0.1 select_reduce_fusion
  27.0 5.1 %collective-permute-done.z_ref = bf16[192,896]{1,0:T(8,128)(2,1)S(1)} collective-permute-done((bf16[192,896]{1,0:T(8,128)(2,1)}, bf16[192,896]{1,0:T(8,128)(2,1)S(1)}, u32[]{:S(2)}, u32[]{:S(2)}) %collective-permute-start) | collective-permute-done | bytes 344096 | tf_op jit(solution)/shard_map/ppermute | solution.py:240
  32.0 0.0 collective-permute-start.1
  32.1 0.1 copy.10
  32.1 0.1 sub.7.place
  32.3 0.0 collective-permute-done.2.a1
  32.3 1.6 %collective-permute-done.4.a3 = bf16[64,2048]{1,0:T(8,128)(2,1)S(1)} collective-permute-done((bf16[64,2048]{1,0:T(8,128)(2,1)S(1)}, bf16[64,2048]{1,0:T(8,128)(2,1)S(1)}, u32[]{:S(2)}, u32[]{:S(2)}) %collective-permute-start.4) | collective-permute-done | bytes 262176 | tf_op jit(solution)/shard_map/ppermute | solution.py:241
  33.8 0.0 collective-permute-done.7.near_ref
  33.8 0.0 copy-done.1
  33.8 3.2 %shard_map.57.acc_ref = f32[256,1792]{1,0:T(8,128)S(1)} custom-call(s32[1568]{0:T(1024)S(1)} %sub.7.place, bf16[448,1792]{1,0:T(8,128)(2,1)S(1)} %copy-done.1, bf16[448,1792]{1,0:T(8,128)(2,1)} %collective-permute-done.7.near_ref, bf16[64,2048]{1,0:T(8,128)(2,1)S(1)} %get-tuple-element.14.a0, bf16[64,2048]{1,0:T(8,128)(2,1)S(1)} %collective-permute-done.2.a1, ...), custom_call_target="tpu_custom_call" | custom-call | flops 822083584 | bytes 4266112 | tf_op jit(solution)/shard_map/pallas_call | solution.py:215
  37.0 0.0 collective-permute-done.6.y_ref
  37.0 3.5 %shard_map.58.acc_ref = f32[256,1792]{1,0:T(8,128)S(1)} custom-call(s32[1568]{0:T(1024)S(1)} %sub.7.place, bf16[256,896]{1,0:T(8,128)(2,1)S(1)} %collective-permute-done.5.z_ref, bf16[256,896]{1,0:T(8,128)(2,1)} %collective-permute-done.6.y_ref, bf16[64,2048]{1,0:T(8,128)(2,1)S(1)} %get-tuple-element.14.a0, bf16[64,2048]{1,0:T(8,128)(2,1)S(1)} %collective-permute-done.2.a1, ...), custom_call_target="tpu_custom_call" | custom-call | flops 469762048 | bytes 3807360 | tf_op jit(solution)/shard_map/pallas_call | solution.py:215
  40.5 0.0 collective-permute-done.1.y_ref
  40.5 3.2 %shard_map.59 = (f32[64,1792]{1,0:T(8,128)S(1)}, f32[64,1792]{1,0:T(8,128)S(1)}, s16[64,1920]{1,0:T(8,128)(2,1)S(1)}, s16[64,1920]{1,0:T(8,128)(2,1)S(1)}) custom-call(s32[1568]{0:T(1024)S(1)} %sub.7.place, bf16[192,896]{1,0:T(8,128)(2,1)S(1)} %collective-permute-done.z_ref, bf16[192,896]{1,0:T(8,128)(2,1)} %collective-permute-done.1.y_ref, ...), custom_call_target="tpu_custom_call" | custom-call | flops 352321536 | bytes 3577984 | tf_op jit(solution)/shard_map/pallas_call | solution.py:215
  43.7 1.8 %collective-permute-start.8 = (f32[64,1792]{1,0:T(8,128)S(1)}, f32[64,1792]{1,0:T(8,128)S(1)}, u32[]{:S(2)}, u32[]{:S(2)}) collective-permute-start(f32[64,1792]{1,0:T(8,128)S(1)} %get-tuple-element.18), channel_id=1, source_target_pairs={{0,1},{1,0},{2,3},{3,2},{4,5},{5,4},{6,7},{7,6},{8,9},{9,8},{10,11... | collective-permute-start | bytes 1376264 | tf_op jit(solution)/shard_map/ppermute | solution.py:241
  45.5 1.6 %collective-permute-start.10 = (s16[64,1920]{1,0:T(8,128)(2,1)S(1)}, s16[64,1920]{1,0:T(8,128)(2,1)S(1)}, u32[]{:S(2)}, u32[]{:S(2)}) collective-permute-start(s16[64,1920]{1,0:T(8,128)(2,1)S(1)} %get-tuple-element.20), channel_id=1, source_target_pairs={{0,9},{1,8},{2,11},{3,10},{4,13},{5,12},{6,15},{7,14},{8,1},{9,0},... | collective-permute-start | bytes 737288 | tf_op jit(solution)/shard_map/ppermute | solution.py:238
  47.1 1.1 %collective-permute-start.9 = (s16[64,1920]{1,0:T(8,128)(2,1)S(1)}, s16[64,1920]{1,0:T(8,128)(2,1)S(1)}, u32[]{:S(2)}, u32[]{:S(2)}) collective-permute-start(s16[64,1920]{1,0:T(8,128)(2,1)S(1)} %get-tuple-element.19), channel_id=1, source_target_pairs={{0,8},{2,10},{4,12},{6,14},{8,0},{10,2},{12,4},{14,6},{1,9},{3,11}... | collective-permute-start | bytes 737288 | tf_op jit(solution)/shard_map/ppermute | solution.py:240
  48.2 17.3 %collective-permute-done.10.cross_ref = s16[64,1920]{1,0:T(8,128)(2,1)S(1)} collective-permute-done((s16[64,1920]{1,0:T(8,128)(2,1)S(1)}, s16[64,1920]{1,0:T(8,128)(2,1)S(1)}, u32[]{:S(2)}, u32[]{:S(2)}) %collective-permute-start.10) | collective-permute-done | bytes 245792 | tf_op jit(solution)/shard_map/ppermute | solution.py:238
  65.4 3.8 %collective-permute-done.9.same_ref = s16[64,1920]{1,0:T(8,128)(2,1)S(1)} collective-permute-done((s16[64,1920]{1,0:T(8,128)(2,1)S(1)}, s16[64,1920]{1,0:T(8,128)(2,1)S(1)}, u32[]{:S(2)}, u32[]{:S(2)}) %collective-permute-start.9) | collective-permute-done | bytes 245792 | tf_op jit(solution)/shard_map/ppermute | solution.py:240
  69.3 0.0 collective-permute-done.8.got_ref
  69.3 1.2 %shard_map.60 = f32[64,3584]{1,0:T(8,128)} custom-call(f32[64,1792]{1,0:T(8,128)S(1)} %get-tuple-element.17.keep_ref, f32[64,1792]{1,0:T(8,128)S(1)} %collective-permute-done.8.got_ref, s16[64,1920]{1,0:T(8,128)(2,1)S(1)} %collective-permute-done.9.same_ref, s16[64,1920]{1,0:T(8,128)(2,1)S(1)} %collective-permute-done.10.cross_ref), custom_call_target="tpu_custom_call" | custom-call | bytes 1409024 | tf_op jit(solution)/shard_map/pallas_call | solution.py:215
  (4 shorter events, 0.0 us)
Async XLA Ops:
  0.0 15.7 %copy-start.5 = (s32[56,2,14]{0,1,2:T(2,128)S(1)}, s32[56,2,14]{0,1,2:T(2,128)}, u32[]{:S(2)}) copy-start(s32[56,2,14]{0,1,2:T(2,128)} %param.9) | copy-start | bytes 18820
  0.0 33.8 %collective-permute-start.7 = (bf16[448,1792]{1,0:T(8,128)(2,1)}, bf16[448,1792]{1,0:T(8,128)(2,1)}, u32[]{:S(2)}, u32[]{:S(2)}) collective-permute-start(bf16[448,1792]{1,0:T(8,128)(2,1)} %own_ref.1), channel_id=1, source_target_pairs={{0,2},{2,0},{4,6},{6,4},{8,10},{10,8},{12,14},{14,12},{1,3},{3,1},... | collective-permute-start | bytes 4816904 | tf_op jit(solution)/shard_map/ppermute | solution.py:240
  1.4 1.4 %copy-start = (bf16[448,1792]{1,0:T(8,128)(2,1)S(1)}, bf16[448,1792]{1,0:T(8,128)(2,1)}, u32[]{:S(2)}) copy-start(bf16[448,1792]{1,0:T(8,128)(2,1)} %own_ref.1) | copy-start | bytes 4816900
  2.8 31.0 %copy-start.1 = (bf16[448,1792]{1,0:T(8,128)(2,1)S(1)}, bf16[448,1792]{1,0:T(8,128)(2,1)}, u32[]{:S(2)}) copy-start(bf16[448,1792]{1,0:T(8,128)(2,1)} %own_ref.1) | copy-start | bytes 4816900
  5.1 19.8 %collective-permute-start.5 = (bf16[256,896]{1,0:T(8,128)(2,1)}, bf16[256,896]{1,0:T(8,128)(2,1)S(1)}, u32[]{:S(2)}, u32[]{:S(2)}) collective-permute-start(bf16[256,896]{1,0:T(8,128)(2,1)} %get-tuple-element.16), channel_id=1, source_target_pairs={{0,4},{2,6},{4,0},{6,2},{8,12},{10,14},{12,8},{14,10},{1,5},{3,7},... | collective-permute-start | bytes 1376264 | tf_op jit(solution)/shard_map/ppermute | solution.py:240
  7.7 1.0 %copy-start.2 = (bf16[64,3584]{1,0:T(8,128)(2,1)S(1)}, bf16[64,3584]{1,0:T(8,128)(2,1)}, u32[]{:S(2)}) copy-start(bf16[64,3584]{1,0:T(8,128)(2,1)} %amp_ref.1) | copy-start | bytes 1376260
  8.7 0.7 copy-start.3
  9.4 0.7 copy-start.4
  11.1 13.8 %collective-permute-start.3 = (bf16[64,2048]{1,0:T(8,128)(2,1)S(1)}, bf16[64,2048]{1,0:T(8,128)(2,1)S(1)}, u32[]{:S(2)}, u32[]{:S(2)}) collective-permute-start(bf16[64,2048]{1,0:T(8,128)(2,1)S(1)} %get-tuple-element.15), channel_id=1, source_target_pairs={{0,8},{2,10},{4,12},{6,14},{8,0},{10,2},{12,4},{14,6},{1,9},{3,11}... | collective-permute-start | bytes 786440 | tf_op jit(solution)/shard_map/ppermute | solution.py:240
  13.8 18.3 %collective-permute-start = (bf16[192,896]{1,0:T(8,128)(2,1)}, bf16[192,896]{1,0:T(8,128)(2,1)S(1)}, u32[]{:S(2)}, u32[]{:S(2)}) collective-permute-start(bf16[192,896]{1,0:T(8,128)(2,1)} %get-tuple-element.13), channel_id=1, source_target_pairs={{0,4},{2,6},{4,0},{6,2},{8,12},{10,14},{12,8},{14,10},{1,5},{3,7},... | collective-permute-start | bytes 1032200 | tf_op jit(solution)/shard_map/ppermute | solution.py:240
  14.2 18.0 %collective-permute-start.2 = (bf16[64,2048]{1,0:T(8,128)(2,1)S(1)}, bf16[64,2048]{1,0:T(8,128)(2,1)S(1)}, u32[]{:S(2)}, u32[]{:S(2)}) collective-permute-start(bf16[64,2048]{1,0:T(8,128)(2,1)S(1)} %get-tuple-element.14.a0), channel_id=1, source_target_pairs={{0,1},{1,0},{2,3},{3,2},{4,5},{5,4},{6,7},{7,6},{8,9},{9,8},{10,11... | collective-permute-start | bytes 786440 | tf_op jit(solution)/shard_map/ppermute | solution.py:241
  24.9 12.1 %collective-permute-start.6 = (bf16[256,896]{1,0:T(8,128)(2,1)S(1)}, bf16[256,896]{1,0:T(8,128)(2,1)}, u32[]{:S(2)}, u32[]{:S(2)}) collective-permute-start(bf16[256,896]{1,0:T(8,128)(2,1)S(1)} %collective-permute-done.5.z_ref), channel_id=1, source_target_pairs={{0,2},{2,0},{4,6},{6,4},{8,10},{10,8},{12,14},{14,12},{1,3},{3,1},... | collective-permute-start | bytes 1376264 | tf_op jit(solution)/shard_map/ppermute | solution.py:240
  24.9 8.9 %collective-permute-start.4 = (bf16[64,2048]{1,0:T(8,128)(2,1)S(1)}, bf16[64,2048]{1,0:T(8,128)(2,1)S(1)}, u32[]{:S(2)}, u32[]{:S(2)}) collective-permute-start(bf16[64,2048]{1,0:T(8,128)(2,1)S(1)} %collective-permute-done.3.a2), channel_id=1, source_target_pairs={{0,1},{1,0},{2,3},{3,2},{4,5},{5,4},{6,7},{7,6},{8,9},{9,8},{10,11... | collective-permute-start | bytes 786440 | tf_op jit(solution)/shard_map/ppermute | solution.py:241
  32.0 8.5 %collective-permute-start.1 = (bf16[192,896]{1,0:T(8,128)(2,1)S(1)}, bf16[192,896]{1,0:T(8,128)(2,1)}, u32[]{:S(2)}, u32[]{:S(2)}) collective-permute-start(bf16[192,896]{1,0:T(8,128)(2,1)S(1)} %collective-permute-done.z_ref), channel_id=1, source_target_pairs={{0,2},{2,0},{4,6},{6,4},{8,10},{10,8},{12,14},{14,12},{1,3},{3,1},... | collective-permute-start | bytes 1032200 | tf_op jit(solution)/shard_map/ppermute | solution.py:240
  43.7 25.6 %collective-permute-start.8 = (f32[64,1792]{1,0:T(8,128)S(1)}, f32[64,1792]{1,0:T(8,128)S(1)}, u32[]{:S(2)}, u32[]{:S(2)}) collective-permute-start(f32[64,1792]{1,0:T(8,128)S(1)} %get-tuple-element.18), channel_id=1, source_target_pairs={{0,1},{1,0},{2,3},{3,2},{4,5},{5,4},{6,7},{7,6},{8,9},{9,8},{10,11... | collective-permute-start | bytes 1376264 | tf_op jit(solution)/shard_map/ppermute | solution.py:241
  45.5 19.9 %collective-permute-start.10 = (s16[64,1920]{1,0:T(8,128)(2,1)S(1)}, s16[64,1920]{1,0:T(8,128)(2,1)S(1)}, u32[]{:S(2)}, u32[]{:S(2)}) collective-permute-start(s16[64,1920]{1,0:T(8,128)(2,1)S(1)} %get-tuple-element.20), channel_id=1, source_target_pairs={{0,9},{1,8},{2,11},{3,10},{4,13},{5,12},{6,15},{7,14},{8,1},{9,0},... | collective-permute-start | bytes 737288 | tf_op jit(solution)/shard_map/ppermute | solution.py:238
  47.1 22.2 %collective-permute-start.9 = (s16[64,1920]{1,0:T(8,128)(2,1)S(1)}, s16[64,1920]{1,0:T(8,128)(2,1)S(1)}, u32[]{:S(2)}, u32[]{:S(2)}) collective-permute-start(s16[64,1920]{1,0:T(8,128)(2,1)S(1)} %get-tuple-element.19), channel_id=1, source_target_pairs={{0,8},{2,10},{4,12},{6,14},{8,0},{10,2},{12,4},{14,6},{1,9},{3,11}... | collective-permute-start | bytes 737288 | tf_op jit(solution)/shard_map/ppermute | solution.py:240

commit v2 on v0

--- a/solution.py
+++ b/solution.py
@@ -1,12 +1,24 @@
+import functools
+
 import jax
 import jax.numpy as jnp
 from jax import lax
+from jax.experimental import pallas as pl
+from jax.experimental.pallas import tpu as pltpu
 from jax.sharding import PartitionSpec as P
 
 BLK = 64
-
-
-def body(amplitudes, integrals, tile_list, slab_order, block_list):
+LANES = 128
+GROUP = 256
+LOW_EXP = -100.0
+ROOM = 60
+SPLIT = 3
+VMEM = pl.BlockSpec(memory_space=pltpu.VMEM)
+SMEM = pl.BlockSpec(memory_space=pltpu.SMEM)
+MIB = 1024 * 1024
+
+
+def gather_body(amplitudes, integrals, tile_list, slab_order, block_list):
     rows_dev, virt_cols = amplitudes.shape
     virt_tiles = virt_cols // BLK
     own_count = rows_dev // BLK
@@ -36,6 +48,313 @@
     return lax.all_to_all(ladder_slab, "pair", split_axis=0, concat_axis=1, tiled=True)
 
 
+def low_lanes(rows):
+    return lax.broadcasted_iota(jnp.int32, (rows, LANES), 1) < BLK
+
+
+def half(index):
+    return pl.ds(pl.multiple_of((index // 2) * LANES, LANES), LANES)
+
+
+def fetch(pairs, sems):
+    copies = [pltpu.make_async_copy(s, d, sems.at[n]) for n, (s, d) in enumerate(pairs)]
+    for copy in copies:
+        copy.start()
+    return copies
+
+
+def pack_kernel(lists_ref, block_ref, first_ref, second_ref, lists, block, sems):
+    wide, pair = lax.axis_index("wide"), lax.axis_index("pair")
+    tiles = block_ref.shape[0] // BLK
+    keep = first_ref.shape[1] // BLK
+    split = first_ref.shape[0] // BLK
+    rows = [pl.ds(i * BLK, BLK) for i in range(tiles)]
+    copies = fetch([(lists_ref, lists)] + [(block_ref.at[r], block.at[r]) for r in rows], sems)
+    copies[0].wait()
+    low = low_lanes(BLK)
+    for i in range(tiles):
+        copies[1 + i].wait()
+        out, row = (first_ref, i) if i < split else (second_ref, i - split)
+        u = wide * tiles + i
+        for j in range(keep // 2):
+            even, odd = lists[2 * j, pair, u], lists[2 * j + 1, pair, u]
+            left = pltpu.roll(block[rows[i], half(even)], (even % 2) * BLK, 1)
+            right = pltpu.roll(block[rows[i], half(odd)], BLK - (odd % 2) * BLK, 1)
+            out[row * BLK : (row + 1) * BLK, j * LANES : (j + 1) * LANES] = jnp.where(
+                low, left, right
+            )
+
+
+def mask_kernel(tile_ref, slab_ref, amp_ref, own_ref, far_ref, tile_list, slab, amp, present, sems):
+    wide, pair = lax.axis_index("wide"), lax.axis_index("pair")
+    copies = fetch([(tile_ref, tile_list), (slab_ref, slab), (amp_ref, amp)], sems)
+    count = amp_ref.shape[1] // BLK
+    for t in range(count):
+        present[t] = 0
+    copies[0].wait()
+    copies[1].wait()
+    tile = slab[wide * 2 + pair]
+    for k in range(tile_ref.shape[1]):
+        present[tile_list[tile, k]] = 1
+    copies[2].wait()
+    mine = wide // 4
+    low = low_lanes(BLK)
+    blocks = count // 4
+    for side, out in ((mine, own_ref), (1 - mine, far_ref)):
+        for s in range(blocks):
+            t = 2 * (side * blocks + s)
+            flag = jnp.where(low, present[t], present[t + 1])
+            out[:, s * LANES : (s + 1) * LANES] = jnp.where(flag > 0, amp[:, half(t)], 0)
+
+
+def raw_kernel(place, own_ref, near_ref, dense):
+    wide = lax.axis_index("wide")
+    depth, width = own_ref.shape
+    tiles, group = depth // BLK, width // BLK
+    low = low_lanes(BLK)
+    for block, source in ((own_ref, wide), (near_ref, wide ^ 1)):
+        for i in range(tiles):
+            base = (source * tiles + i) * group
+            here = pl.ds(pl.multiple_of((source % 2) * depth + i * BLK, BLK), BLK)
+            for s in range(group // 2):
+                cols = slice(s * LANES, (s + 1) * LANES)
+                flag = jnp.where(low, place[base + 2 * s], place[base + 2 * s + 1])
+                dense[here, cols] = jnp.where(flag >= 0, block[i * BLK : (i + 1) * BLK, cols], 0)
+
+
+def spread(place, packed, dense, source_row):
+    tiles = packed.shape[0] // BLK
+    group = dense.shape[1] // BLK
+    low = low_lanes(BLK)
+    for i in range(tiles):
+        here = slice(i * BLK, (i + 1) * BLK)
+        base = (source_row + i) * group
+        for s in range(group // 2):
+            even, odd = place[base + 2 * s], place[base + 2 * s + 1]
+            left_at, right_at = jnp.maximum(even, 0), jnp.maximum(odd, 0)
+            left = pltpu.roll(packed[here, half(left_at)], (left_at % 2) * BLK, 1)
+            right = pltpu.roll(packed[here, half(right_at)], BLK - (right_at % 2) * BLK, 1)
+            flag = jnp.where(low, even, odd)
+            dense[here, s * LANES : (s + 1) * LANES] = jnp.where(
+                flag >= 0, jnp.where(low, left, right), 0
+            )
+
+
+def pick(amps, rows, starts):
+    count = rows.shape[1] // BLK // len(starts)
+    low = low_lanes(BLK)
+    for b in range(rows.shape[1] // LANES):
+        even, odd = (starts[d // count] + d % count for d in (2 * b, 2 * b + 1))
+        for n, amp in enumerate(amps):
+            left = pltpu.roll(amp[:, half(even)], (even % 2) * BLK, 1)
+            right = pltpu.roll(amp[:, half(odd)], BLK - (odd % 2) * BLK, 1)
+            rows[n * BLK : (n + 1) * BLK, b * LANES : (b + 1) * LANES] = jnp.where(low, left, right)
+
+
+def dot(a, b):
+    return jnp.dot(a, b, preferred_element_type=jnp.float32)
+
+
+def spread_kernel(tiles, first, place, z_ref, y_ref, dense):
+    wide = lax.axis_index("wide")
+    for n, (block, source) in enumerate(((z_ref, wide ^ 2), (y_ref, wide ^ 3))):
+        rows = block.shape[0]
+        spread(place, block, dense.at[n * rows : (n + 1) * rows], source * tiles + first)
+
+
+def chip_rows(amps, rows):
+    at = (lax.axis_index("wide") // 2) % 2
+    depth = rows.shape[1]
+    for n, amp in enumerate(amps):
+        rows[n * BLK : (n + 1) * BLK] = amp[:, pl.ds(pl.multiple_of(at * depth, LANES), depth)]
+
+
+def meet(amps, tiles, first, rows, dense):
+    wide = lax.axis_index("wide")
+    pick(amps, rows, [(source % 4) * tiles + first for source in (wide ^ 2, wide ^ 3)])
+    return dot(rows[...], dense[...])
+
+
+def early_kernel(tiles, raw, dense, a0, a1, a2, a3, acc_ref, raw_rows, rows):
+    amps = (a0, a1, a2, a3)
+    chip_rows(amps, raw_rows)
+    acc_ref[...] = dot(raw_rows[...], raw[...]) + meet(amps, tiles, 0, rows, dense)
+
+
+def encode(values, out):
+    width = values.shape[1]
+    across = width // LANES
+    high = out.shape[1]
+    groups = width // GROUP
+    lane = lax.broadcasted_iota(jnp.int32, (high, LANES), 1)
+    exps = jnp.zeros((high, LANES), jnp.int32)
+    for i in range(BLK // high):
+        for g in range(groups):
+            part = values[i * high : (i + 1) * high, g * GROUP : (g + 1) * GROUP]
+            top = jnp.max(jnp.abs(part), axis=1, keepdims=True)
+            exp = jnp.maximum(jnp.ceil(jnp.log2(jnp.maximum(top, 2.0**LOW_EXP))), LOW_EXP)
+            scaled = jnp.clip(jnp.round(part * jnp.exp2(15.0 - exp)), -32767.0, 32767.0)
+            coded = scaled.astype(jnp.int32).astype(jnp.int16)
+            for k in range(GROUP // LANES):
+                at = i * across + g * (GROUP // LANES) + k
+                out[at] = coded[:, k * LANES : (k + 1) * LANES]
+            exps = jnp.where(lane == i * groups + g, exp.astype(jnp.int32), exps)
+    out[out.shape[0] - 1] = exps.astype(jnp.int16)
+
+
+def last_kernel(
+    tiles, first, place, z_ref, y_ref, a0, a1, a2, a3, acc_ref, keep_ref, upper_ref, lower_ref,
+    same_ref, cross_ref, dense, rows,
+):
+    spread_kernel(tiles, first, place, z_ref, y_ref, dense)
+    total = acc_ref[...] + meet((a0, a1, a2, a3), tiles, first, rows, dense)
+    encode(total[3 * BLK :], cross_ref)
+    encode(total[2 * BLK : 3 * BLK], same_ref)
+    keep_ref[...] = total[:BLK]
+    upper_ref[...] = total[BLK : BLK + BLK // 2]
+    lower_ref[...] = total[BLK + BLK // 2 : 2 * BLK]
+
+
+def join_kernel(keep_ref, upper_ref, lower_ref, same_ref, cross_ref, out_ref):
+    pair = lax.axis_index("pair")
+    width = keep_ref.shape[1]
+    across, groups, high = width // LANES, width // GROUP, same_ref.shape[1]
+    for side, bases, coded in (
+        (pair, (keep_ref,), same_ref),
+        (1 - pair, (upper_ref, lower_ref), cross_ref),
+    ):
+        exps = coded[coded.shape[0] - 1].astype(jnp.int32).astype(jnp.float32)
+        for i in range(BLK // high):
+            base = bases[i * high // bases[0].shape[0]]
+            at = i * high % bases[0].shape[0]
+            for g in range(groups):
+                n = i * groups + g
+                scale = jnp.exp2(exps[:, n : n + 1] - 15.0)
+                for k in range(GROUP // LANES):
+                    s = g * (GROUP // LANES) + k
+                    value = coded[i * across + s].astype(jnp.int32).astype(jnp.float32) * scale
+                    where = pl.ds(pl.multiple_of(side * width + s * LANES, LANES), LANES)
+                    out_ref[i * high : (i + 1) * high, where] = (
+                        base[at : at + high, s * LANES : (s + 1) * LANES] + value
+                    )
+
+
+def call(kernel, out, operands, places, scratch=(), room=32):
+    specs = {"s": SMEM, "v": VMEM, "a": pl.BlockSpec(memory_space=pltpu.HBM)}
+    return pl.pallas_call(
+        kernel,
+        out_shape=out,
+        in_specs=[specs[p] for p in places],
+        out_specs=jax.tree.map(lambda _: VMEM, out),
+        scratch_shapes=list(scratch),
+        compiler_params=pltpu.CompilerParams(vmem_limit_bytes=room * MIB),
+        cost_estimate=pl.CostEstimate(flops=1, bytes_accessed=1, transcendentals=0),
+    )(*operands)
+
+
+def swap_body(amplitudes, integrals, tile_list, slab_order, block_list):
+    wide_count, pair_count = lax.axis_size("wide"), lax.axis_size("pair")
+    depth, width = integrals.shape
+    tiles, group = depth // BLK, width // BLK
+    keep = block_list.shape[2]
+    bf16, f32, i16, i32 = jnp.bfloat16, jnp.float32, jnp.int16, jnp.int32
+    sds = jax.ShapeDtypeStruct
+    bind = functools.partial
+
+    def move(x, flip_wide, flip_pair=0):
+        if flip_wide and flip_pair:
+            n = wide_count * pair_count
+            flip = flip_wide * pair_count + flip_pair
+            return lax.ppermute(x, ("wide", "pair"), [(i, i ^ flip) for i in range(n)])
+        if flip_wide:
+            return lax.ppermute(x, "wide", [(i, i ^ flip_wide) for i in range(wide_count)])
+        return lax.ppermute(x, "pair", [(i, i ^ flip_pair) for i in range(pair_count)])
+
+    lists = block_list.transpose(2, 1, 0)
+
+    head = SPLIT
+    tail = tiles - head
+    first, second = call(
+        pack_kernel,
+        tuple(sds((count * BLK, keep * BLK), bf16) for count in (head, tail)),
+        (lists, integrals),
+        "aa",
+        [
+            pltpu.SMEM(lists.shape, i32),
+            pltpu.VMEM(integrals.shape, bf16),
+            pltpu.SemaphoreType.DMA((tiles + 1,)),
+        ],
+        ROOM,
+    )
+    own, far = call(
+        mask_kernel,
+        (sds((BLK, amplitudes.shape[1] // 2), bf16),) * 2,
+        (tile_list, slab_order, amplitudes),
+        "aaa",
+        [
+            pltpu.SMEM(tile_list.shape, i32),
+            pltpu.SMEM(slab_order.shape, i32),
+            pltpu.VMEM(amplitudes.shape, bf16),
+            pltpu.SMEM((amplitudes.shape[1] // BLK,), i32),
+            pltpu.SemaphoreType.DMA((3,)),
+        ],
+        ROOM,
+    )
+    z_first = move(first, 2)
+    z_second = move(second, 2)
+    far_same = move(far, 4)
+    near = move(integrals, 1)
+    own_cross = move(own, 0, 1)
+    far_cross = move(far_same, 0, 1)
+
+    my_lists = lax.dynamic_index_in_dim(block_list, lax.axis_index("pair"), 1, keepdims=False)
+    hit = my_lists[:, :, None] == jnp.arange(group, dtype=i32)[None, None, :]
+    order = jnp.arange(1, keep + 1, dtype=i32)[None, :, None]
+    place = (jnp.sum(jnp.where(hit, order, 0), axis=1) - 1).reshape(-1)
+
+    raw = call(raw_kernel, sds((2 * depth, width), bf16), (place, integrals, near), "svv")
+    y_first = move(z_first, 1)
+    amps = (own, own_cross, far_same, far_cross)
+    rows = len(amps) * BLK
+    raw_rows = pltpu.VMEM((rows, 2 * depth), bf16)
+
+    def scratch(count):
+        return pltpu.VMEM((rows, 2 * count * BLK), bf16)
+
+    dense_first = call(
+        bind(spread_kernel, tiles, 0),
+        sds((2 * head * BLK, width), bf16),
+        (place, z_first, y_first),
+        "svv",
+    )
+    acc = call(
+        bind(early_kernel, tiles),
+        sds((rows, width), f32),
+        (raw, dense_first, *amps),
+        "v" * 6,
+        [raw_rows, scratch(head)],
+    )
+    z_second, acc = lax.optimization_barrier((z_second, acc))
+    y_second = move(z_second, 1)
+    coded = sds((BLK * width // (16 * LANES) + 1, 16, LANES), i16)
+    part = sds((BLK // 2, width), f32)
+    keep_rows, upper, lower, same, cross = call(
+        bind(last_kernel, tiles, head),
+        (sds((BLK, width), f32), part, part, coded, coded),
+        (place, z_second, y_second, *amps, acc),
+        "s" + "v" * 7,
+        [pltpu.VMEM((2 * tail * BLK, width), bf16), scratch(tail)],
+    )
+    got_cross = move(cross, 4, 1)
+    got_same = move(same, 4)
+    return call(
+        join_kernel,
+        sds((BLK, pair_count * width), f32),
+        (keep_rows, move(upper, 0, 1), move(lower, 0, 1), got_same, got_cross),
+        "v" * 5,
+    )
+
+
 def solution(mesh):
     placed = (
         P(("grp", "wide", "pair"), None),
@@ -44,8 +363,9 @@
         P("grp"),
         P("grp", None, None),
     )
+    swapped = mesh.shape["wide"] == 8 and mesh.shape["pair"] == 2
     return jax.shard_map(
-        body,
+        swap_body if swapped else gather_body,
         mesh=mesh,
         in_specs=placed,
         out_specs=P(("grp", "wide", "pair"), None),

time: 184 us -> 63.5 us (0.35)
  local copies, waits for them, and re-layouts: 60.9 us -> 0.21 us
  waiting for transfers between devices: 64.5 us -> 30.6 us
  blocking collectives: 30.1 us -> 0 us
  Pallas kernels: 0 us -> 16.2 us
  starting transfers between devices: 0.01 us -> 16 us
  between operations: 15.4 us -> 0.16 us
  matrix products: 10.5 us -> 0 us
    all_gather x1 -> x0, waiting for transfers between devices: 63.8 us -> none  [body(): shard_block = lax.all_gather(integrals, 'wide', axis=0, tiled=True)]
    mul x4 -> x0, local copies, waits for them, and re-layouts: 40.7 us -> none  [the longest x2 40.5 us: body(): shard_block.reshape(qtiles, BLK, group_tiles, BLK) * live[:, None, :, None]]
    ppermute x0 -> x12, waiting for transfers between devices: none -> 30.6 us  [the longest x7 12.8 us: move(): lax.ppermute(x, 'wide', [(i, i ^ flip_wide) for i in range(wide_count)])]
    all_gather x1 -> x0, local copies, waits for them, and re-layouts: 18 us -> none  [body(): shard_block = lax.all_gather(integrals, 'wide', axis=0, tiled=True)]
    pallas_call x0 -> x7, Pallas kernels: none -> 16.2 us  [call(): pl.pallas_call(kernel, out_shape=out, in_specs=[specs[p] for p in places]...]
    ppermute x0 -> x12, starting transfers between devices: none -> 16 us  [the longest x7 7.69 us: move(): lax.ppermute(x, 'wide', [(i, i ^ flip_wide) for i in range(wide_count)])]
    all_to_all x1 -> x0, blocking collectives: 15.3 us -> none  [body(): lax.all_to_all(ladder_slab, 'pair', split_axis=0, concat_axis=1, tiled=True)]
    all_gather x1 -> x0, blocking collectives: 14.8 us -> none  [body(): slab_rows = lax.all_gather(masked, 'pair', axis=0, tiled=True)]
  transfers between devices with their start and end apart: 1 -> 12, of which waited for: 1 -> 7; matrix products, arithmetic and copies ran while one was open for 23% -> 0% of each run, Pallas kernels for 0% -> 18%
where the time goes in v2:
time: 63.5 us; the launch traced here: 63.3 us
  waiting for transfers between devices  30.6 us (48%)
  Pallas kernels  16.2 us (26%)
  starting transfers between devices  16 us (25%)
    pallas_call x7, Pallas kernels, call(): pl.pallas_call(kernel, out_shape=out, in_specs=[specs[p] for p in places]...  16.2 us
    ppermute x7, waiting for transfers between devices, move(): lax.ppermute(x, 'wide', [(i, i ^ flip_wide) for i in range(wide_count)])  12.8 us
    ppermute x4, waiting for transfers between devices, move(): lax.ppermute(x, 'pair', [(i, i ^ flip_pair) for i in range(pair_count)])  12.4 us
    ppermute x7, starting transfers between devices, move(): lax.ppermute(x, 'wide', [(i, i ^ flip_wide) for i in range(wide_count)])  7.69 us
    ppermute x4, starting transfers between devices, move(): lax.ppermute(x, 'pair', [(i, i ^ flip_pair) for i in range(pair_count)])  5.45 us
    ppermute x1, waiting for transfers between devices, move(): return lax.ppermute(x, ('wide', 'pair'), [(i, i ^ flip) for i in range(n)])  5.4 us
    ppermute x1, starting transfers between devices, move(): return lax.ppermute(x, ('wide', 'pair'), [(i, i ^ flip) for i in range(n)])  2.85 us
  transfers between devices with their start and end apart: 12, of which 7 were waited for; matrix products, arithmetic and copies ran while one was open for 0% of the time, Pallas kernels for 18%

profile of v2, /device:TPU:0, one launch (start us, length us, event | category | flops | bytes accessed | tf_op | source)
XLA Modules:
  0.0 63.3 jit_solution(9550515096573826159)
XLA Ops:
  0.0 0.0 copy-start.2
  0.0 0.5 collective-permute-start.1
  0.5 3.0 %shard_map.55 = (bf16[192,896]{1,0:T(8,128)(2,1)}, bf16[256,896]{1,0:T(8,128)(2,1)}) custom-call(s32[14,2,56]{2,1,0:T(2,128)} %bitcast.5, bf16[448,1792]{1,0:T(8,128)(2,1)} %own_ref.1), custom_call_target="tpu_custom_call" | custom-call | flops 1 | bytes 1 | tf_op jit(solution)/shard_map/pallas_call | solution.py:244
  3.5 0.0 copy-start
  3.5 2.7 %collective-permute-start.2 = (bf16[192,896]{1,0:T(8,128)(2,1)}, bf16[192,896]{1,0:T(8,128)(2,1)}, u32[]{:S(2)}, u32[]{:S(2)}) collective-permute-start(bf16[192,896]{1,0:T(8,128)(2,1)} %get-tuple-element.17), channel_id=1, source_target_pairs={{0,4},{2,6},{4,0},{6,2},{8,12},{10,14},{12,8},{14,10},{1,5},{3,7},... | collective-permute-start | bytes 1032200 | tf_op jit(solution)/shard_map/ppermute | solution.py:270
  6.2 2.1 %shard_map.58 = (bf16[64,1792]{1,0:T(8,128)(2,1)}, bf16[64,1792]{1,0:T(8,128)(2,1)}) custom-call(s32[16,28]{1,0:T(8,128)} %tile_ref.1, s32[16]{0:T(128)} %slab_ref.1, bf16[64,3584]{1,0:T(8,128)(2,1)} %amp_ref.1), custom_call_target="tpu_custom_call" | custom-call | flops 1 | bytes 1 | tf_op jit(solution)/shard_map/pallas_call | solution.py:244
  8.3 2.7 %collective-permute-start.5 = (bf16[64,1792]{1,0:T(8,128)(2,1)}, bf16[64,1792]{1,0:T(8,128)(2,1)S(1)}, u32[]{:S(2)}, u32[]{:S(2)}) collective-permute-start(bf16[64,1792]{1,0:T(8,128)(2,1)} %get-tuple-element.19), channel_id=1, source_target_pairs={{0,8},{2,10},{4,12},{6,14},{8,0},{10,2},{12,4},{14,6},{1,9},{3,11}... | collective-permute-start | bytes 688136 | tf_op jit(solution)/shard_map/ppermute | solution.py:270
  10.9 1.5 %collective-permute-start.4 = (bf16[64,1792]{1,0:T(8,128)(2,1)}, bf16[64,1792]{1,0:T(8,128)(2,1)}, u32[]{:S(2)}, u32[]{:S(2)}) collective-permute-start(bf16[64,1792]{1,0:T(8,128)(2,1)} %get-tuple-element.18.a0), channel_id=1, source_target_pairs={{0,1},{1,0},{2,3},{3,2},{4,5},{5,4},{6,7},{7,6},{8,9},{9,8},{10,11... | collective-permute-start | bytes 688136 | tf_op jit(solution)/shard_map/ppermute | solution.py:271
  12.4 0.4 collective-permute-start
  12.9 0.0 copy-done.2
  12.9 7.5 %collective-permute-done.2.z_ref = bf16[192,896]{1,0:T(8,128)(2,1)} collective-permute-done((bf16[192,896]{1,0:T(8,128)(2,1)}, bf16[192,896]{1,0:T(8,128)(2,1)}, u32[]{:S(2)}, u32[]{:S(2)}) %collective-permute-start.2) | collective-permute-done | bytes 344096 | tf_op jit(solution)/shard_map/ppermute | solution.py:270
  20.4 0.0 collective-permute-start.3
  20.4 0.0 collective-permute-done.5.a2
  20.4 1.9 %collective-permute-start.6 = (bf16[64,1792]{1,0:T(8,128)(2,1)S(1)}, bf16[64,1792]{1,0:T(8,128)(2,1)}, u32[]{:S(2)}, u32[]{:S(2)}) collective-permute-start(bf16[64,1792]{1,0:T(8,128)(2,1)S(1)} %collective-permute-done.5.a2), channel_id=1, source_target_pairs={{0,1},{1,0},{2,3},{3,2},{4,5},{5,4},{6,7},{7,6},{8,9},{9,8},{10,11... | collective-permute-start | bytes 688136 | tf_op jit(solution)/shard_map/ppermute | solution.py:271
  22.3 0.1 select_reduce_fusion
  22.4 0.1 copy.9
  22.5 0.1 sub.7.place
  22.6 0.0 collective-permute-done.3.y_ref
  22.6 2.1 %shard_map.57.dense = bf16[384,1792]{1,0:T(8,128)(2,1)S(1)} custom-call(s32[1568]{0:T(1024)S(1)} %sub.7.place, bf16[192,896]{1,0:T(8,128)(2,1)} %collective-permute-done.2.z_ref, bf16[192,896]{1,0:T(8,128)(2,1)} %collective-permute-done.3.y_ref), custom_call_target="tpu_custom_call" | custom-call | flops 1 | bytes 1 | tf_op jit(solution)/shard_map/pallas_call | solution.py:244
  24.8 0.0 copy-start.1
  24.8 0.0 collective-permute-done.1.near_ref
  24.8 0.0 copy-done
  24.8 1.4 %shard_map.56.raw = bf16[896,1792]{1,0:T(8,128)(2,1)S(1)} custom-call(s32[1568]{0:T(1024)S(1)} %sub.7.place, bf16[448,1792]{1,0:T(8,128)(2,1)S(1)} %copy-done, bf16[448,1792]{1,0:T(8,128)(2,1)S(1)} %collective-permute-done.1.near_ref), custom_call_target="tpu_custom_call" | custom-call | flops 1 | bytes 1 | tf_op jit(solution)/shard_map/pallas_call | solution.py:244
  26.2 0.0 collective-permute-done.4.a1
  26.3 2.4 %collective-permute-done.6.a3 = bf16[64,1792]{1,0:T(8,128)(2,1)} collective-permute-done((bf16[64,1792]{1,0:T(8,128)(2,1)S(1)}, bf16[64,1792]{1,0:T(8,128)(2,1)}, u32[]{:S(2)}, u32[]{:S(2)}) %collective-permute-start.6) | collective-permute-done | bytes 229408 | tf_op jit(solution)/shard_map/ppermute | solution.py:271
  28.7 0.0 copy-done.1
  28.7 2.8 %shard_map.59.acc_ref = f32[256,1792]{1,0:T(8,128)S(1)} custom-call(bf16[896,1792]{1,0:T(8,128)(2,1)S(1)} %shard_map.56.raw, bf16[384,1792]{1,0:T(8,128)(2,1)S(1)} %shard_map.57.dense, bf16[64,1792]{1,0:T(8,128)(2,1)S(1)} %copy-done.1, bf16[64,1792]{1,0:T(8,128)(2,1)} %collective-permute-done.4.a1, bf16[64,1792]{1,0:T(8,128)(2,1)S(1)} %collective-permute-done.5.a2, ...), custom_call_target="tpu_custom_call" | custom-call | flops 1 | bytes 1 | tf_op jit(solution)/shard_map/pallas_call | solution.py:244
  31.5 0.0 collective-permute-done.z_ref
  31.5 0.1 collective-permute-start.7
  31.6 2.0 %collective-permute-done.7.y_ref = bf16[256,896]{1,0:T(8,128)(2,1)S(1)} collective-permute-done((bf16[256,896]{1,0:T(8,128)(2,1)}, bf16[256,896]{1,0:T(8,128)(2,1)S(1)}, u32[]{:S(2)}, u32[]{:S(2)}) %collective-permute-start.7) | collective-permute-done | bytes 458784 | tf_op jit(solution)/shard_map/ppermute | solution.py:270
  33.6 3.6 %shard_map.60 = (f32[64,1792]{1,0:T(8,128)S(1)}, f32[32,1792]{1,0:T(8,128)S(1)}, f32[32,1792]{1,0:T(8,128)S(1)}, s16[57,16,128]{2,1,0:T(8,128)(2,1)S(1)}, s16[57,16,128]{2,1,0:T(8,128)(2,1)S(1)}) custom-call(s32[1568]{0:T(1024)S(1)} %sub.7.place, bf16[256,896]{1,0:T(8,128)(2,1)} %collective-permute-done.z_ref, ...), custom_call_target="tpu_custom_call" | custom-call | flops 1 | bytes 1 | tf_op jit(solution)/shard_map/pallas_call | solution.py:244
  37.2 1.3 %collective-permute-start.10 = (s16[57,16,128]{2,1,0:T(8,128)(2,1)S(1)}, s16[57,16,128]{2,1,0:T(8,128)(2,1)S(1)}, u32[]{:S(2)}, u32[]{:S(2)}) collective-permute-start(s16[57,16,128]{2,1,0:T(8,128)(2,1)S(1)} %get-tuple-element.25), channel_id=1, source_target_pairs={{0,8},{2,10},{4,12},{6,14},{8,0},{10,2},{12,4},{14,6},{1,9},{3,11}... | collective-permute-start | bytes 700424 | tf_op jit(solution)/shard_map/ppermute | solution.py:270
  38.5 2.9 %collective-permute-start.11 = (s16[57,16,128]{2,1,0:T(8,128)(2,1)S(1)}, s16[57,16,128]{2,1,0:T(8,128)(2,1)S(1)}, u32[]{:S(2)}, u32[]{:S(2)}) collective-permute-start(s16[57,16,128]{2,1,0:T(8,128)(2,1)S(1)} %get-tuple-element.26), channel_id=1, source_target_pairs={{0,9},{1,8},{2,11},{3,10},{4,13},{5,12},{6,15},{7,14},{8,1},{9,0},... | collective-permute-start | bytes 700424 | tf_op jit(solution)/shard_map/ppermute | solution.py:268
  41.4 0.3 collective-permute-start.8
  41.7 1.7 %collective-permute-start.9 = (f32[32,1792]{1,0:T(8,128)S(1)}, f32[32,1792]{1,0:T(8,128)S(1)}, u32[]{:S(2)}, u32[]{:S(2)}) collective-permute-start(f32[32,1792]{1,0:T(8,128)S(1)} %get-tuple-element.24), channel_id=1, source_target_pairs={{0,1},{1,0},{2,3},{3,2},{4,5},{5,4},{6,7},{7,6},{8,9},{9,8},{10,11... | collective-permute-start | bytes 688136 | tf_op jit(solution)/shard_map/ppermute | solution.py:271
  43.4 6.5 %collective-permute-done.8.upper_ref = f32[32,1792]{1,0:T(8,128)S(1)} collective-permute-done((f32[32,1792]{1,0:T(8,128)S(1)}, f32[32,1792]{1,0:T(8,128)S(1)}, u32[]{:S(2)}, u32[]{:S(2)}) %collective-permute-start.8) | collective-permute-done | bytes 229408 | tf_op jit(solution)/shard_map/ppermute | solution.py:271
  49.9 3.5 %collective-permute-done.9.lower_ref = f32[32,1792]{1,0:T(8,128)S(1)} collective-permute-done((f32[32,1792]{1,0:T(8,128)S(1)}, f32[32,1792]{1,0:T(8,128)S(1)}, u32[]{:S(2)}, u32[]{:S(2)}) %collective-permute-start.9) | collective-permute-done | bytes 229408 | tf_op jit(solution)/shard_map/ppermute | solution.py:271
  53.4 3.3 %collective-permute-done.10.same_ref = s16[57,16,128]{2,1,0:T(8,128)(2,1)S(1)} collective-permute-done((s16[57,16,128]{2,1,0:T(8,128)(2,1)S(1)}, s16[57,16,128]{2,1,0:T(8,128)(2,1)S(1)}, u32[]{:S(2)}, u32[]{:S(2)}) %collective-permute-start.10) | collective-permute-done | bytes 233504 | tf_op jit(solution)/shard_map/ppermute | solution.py:270
  56.7 5.4 %collective-permute-done.11.cross_ref = s16[57,16,128]{2,1,0:T(8,128)(2,1)S(1)} collective-permute-done((s16[57,16,128]{2,1,0:T(8,128)(2,1)S(1)}, s16[57,16,128]{2,1,0:T(8,128)(2,1)S(1)}, u32[]{:S(2)}, u32[]{:S(2)}) %collective-permute-start.11) | collective-permute-done | bytes 233504 | tf_op jit(solution)/shard_map/ppermute | solution.py:268
  62.1 1.2 %shard_map.61 = f32[64,3584]{1,0:T(8,128)} custom-call(f32[64,1792]{1,0:T(8,128)S(1)} %get-tuple-element.22.keep_ref, f32[32,1792]{1,0:T(8,128)S(1)} %collective-permute-done.8.upper_ref, f32[32,1792]{1,0:T(8,128)S(1)} %collective-permute-done.9.lower_ref, s16[57,16,128]{2,1,0:T(8,128)(2,1)S(1)} %collective-permute-done.10.same_ref, ...), custom_call_target="tpu_custom_call" | custom-call | flops 1 | bytes 1 | tf_op jit(solution)/shard_map/pallas_call | solution.py:244
  (4 shorter events, 0.0 us)
Async XLA Ops:
  0.0 12.9 %copy-start.2 = (s32[56,2,14]{0,1,2:T(2,128)S(1)}, s32[56,2,14]{0,1,2:T(2,128)}, u32[]{:S(2)}) copy-start(s32[56,2,14]{0,1,2:T(2,128)} %param.9) | copy-start | bytes 18820
  0.0 24.8 %collective-permute-start.1 = (bf16[448,1792]{1,0:T(8,128)(2,1)}, bf16[448,1792]{1,0:T(8,128)(2,1)S(1)}, u32[]{:S(2)}, u32[]{:S(2)}) collective-permute-start(bf16[448,1792]{1,0:T(8,128)(2,1)} %own_ref.1), channel_id=1, source_target_pairs={{0,2},{2,0},{4,6},{6,4},{8,10},{10,8},{12,14},{14,12},{1,3},{3,1},... | collective-permute-start | bytes 4816904 | tf_op jit(solution)/shard_map/ppermute | solution.py:270
  3.5 21.3 %copy-start = (bf16[448,1792]{1,0:T(8,128)(2,1)S(1)}, bf16[448,1792]{1,0:T(8,128)(2,1)}, u32[]{:S(2)}) copy-start(bf16[448,1792]{1,0:T(8,128)(2,1)} %own_ref.1) | copy-start | bytes 4816900
  3.5 16.9 %collective-permute-start.2 = (bf16[192,896]{1,0:T(8,128)(2,1)}, bf16[192,896]{1,0:T(8,128)(2,1)}, u32[]{:S(2)}, u32[]{:S(2)}) collective-permute-start(bf16[192,896]{1,0:T(8,128)(2,1)} %get-tuple-element.17), channel_id=1, source_target_pairs={{0,4},{2,6},{4,0},{6,2},{8,12},{10,14},{12,8},{14,10},{1,5},{3,7},... | collective-permute-start | bytes 1032200 | tf_op jit(solution)/shard_map/ppermute | solution.py:270
  8.3 12.1 %collective-permute-start.5 = (bf16[64,1792]{1,0:T(8,128)(2,1)}, bf16[64,1792]{1,0:T(8,128)(2,1)S(1)}, u32[]{:S(2)}, u32[]{:S(2)}) collective-permute-start(bf16[64,1792]{1,0:T(8,128)(2,1)} %get-tuple-element.19), channel_id=1, source_target_pairs={{0,8},{2,10},{4,12},{6,14},{8,0},{10,2},{12,4},{14,6},{1,9},{3,11}... | collective-permute-start | bytes 688136 | tf_op jit(solution)/shard_map/ppermute | solution.py:270
  10.9 15.3 %collective-permute-start.4 = (bf16[64,1792]{1,0:T(8,128)(2,1)}, bf16[64,1792]{1,0:T(8,128)(2,1)}, u32[]{:S(2)}, u32[]{:S(2)}) collective-permute-start(bf16[64,1792]{1,0:T(8,128)(2,1)} %get-tuple-element.18.a0), channel_id=1, source_target_pairs={{0,1},{1,0},{2,3},{3,2},{4,5},{5,4},{6,7},{7,6},{8,9},{9,8},{10,11... | collective-permute-start | bytes 688136 | tf_op jit(solution)/shard_map/ppermute | solution.py:271
  12.4 19.0 %collective-permute-start = (bf16[256,896]{1,0:T(8,128)(2,1)}, bf16[256,896]{1,0:T(8,128)(2,1)}, u32[]{:S(2)}, u32[]{:S(2)}) collective-permute-start(bf16[256,896]{1,0:T(8,128)(2,1)} %get-tuple-element.16), channel_id=1, source_target_pairs={{0,4},{2,6},{4,0},{6,2},{8,12},{10,14},{12,8},{14,10},{1,5},{3,7},... | collective-permute-start | bytes 1376264 | tf_op jit(solution)/shard_map/ppermute | solution.py:270
  20.4 2.3 %collective-permute-start.3 = (bf16[192,896]{1,0:T(8,128)(2,1)}, bf16[192,896]{1,0:T(8,128)(2,1)}, u32[]{:S(2)}, u32[]{:S(2)}) collective-permute-start(bf16[192,896]{1,0:T(8,128)(2,1)} %collective-permute-done.2.z_ref), channel_id=1, source_target_pairs={{0,2},{2,0},{4,6},{6,4},{8,10},{10,8},{12,14},{14,12},{1,3},{3,1},... | collective-permute-start | bytes 1032200 | tf_op jit(solution)/shard_map/ppermute | solution.py:270
  20.4 8.3 %collective-permute-start.6 = (bf16[64,1792]{1,0:T(8,128)(2,1)S(1)}, bf16[64,1792]{1,0:T(8,128)(2,1)}, u32[]{:S(2)}, u32[]{:S(2)}) collective-permute-start(bf16[64,1792]{1,0:T(8,128)(2,1)S(1)} %collective-permute-done.5.a2), channel_id=1, source_target_pairs={{0,1},{1,0},{2,3},{3,2},{4,5},{5,4},{6,7},{7,6},{8,9},{9,8},{10,11... | collective-permute-start | bytes 688136 | tf_op jit(solution)/shard_map/ppermute | solution.py:271
  24.8 3.9 %copy-start.1 = (bf16[64,1792]{1,0:T(8,128)(2,1)S(1)}, bf16[64,1792]{1,0:T(8,128)(2,1)}, u32[]{:S(2)}) copy-start(bf16[64,1792]{1,0:T(8,128)(2,1)} %get-tuple-element.18.a0) | copy-start | bytes 688132
  31.5 2.1 %collective-permute-start.7 = (bf16[256,896]{1,0:T(8,128)(2,1)}, bf16[256,896]{1,0:T(8,128)(2,1)S(1)}, u32[]{:S(2)}, u32[]{:S(2)}) collective-permute-start(bf16[256,896]{1,0:T(8,128)(2,1)} %collective-permute-done.z_ref), channel_id=1, source_target_pairs={{0,2},{2,0},{4,6},{6,4},{8,10},{10,8},{12,14},{14,12},{1,3},{3,1},... | collective-permute-start | bytes 1376264 | tf_op jit(solution)/shard_map/ppermute | solution.py:270
  37.2 19.5 %collective-permute-start.10 = (s16[57,16,128]{2,1,0:T(8,128)(2,1)S(1)}, s16[57,16,128]{2,1,0:T(8,128)(2,1)S(1)}, u32[]{:S(2)}, u32[]{:S(2)}) collective-permute-start(s16[57,16,128]{2,1,0:T(8,128)(2,1)S(1)} %get-tuple-element.25), channel_id=1, source_target_pairs={{0,8},{2,10},{4,12},{6,14},{8,0},{10,2},{12,4},{14,6},{1,9},{3,11}... | collective-permute-start | bytes 700424 | tf_op jit(solution)/shard_map/ppermute | solution.py:270
  38.5 23.6 %collective-permute-start.11 = (s16[57,16,128]{2,1,0:T(8,128)(2,1)S(1)}, s16[57,16,128]{2,1,0:T(8,128)(2,1)S(1)}, u32[]{:S(2)}, u32[]{:S(2)}) collective-permute-start(s16[57,16,128]{2,1,0:T(8,128)(2,1)S(1)} %get-tuple-element.26), channel_id=1, source_target_pairs={{0,9},{1,8},{2,11},{3,10},{4,13},{5,12},{6,15},{7,14},{8,1},{9,0},... | collective-permute-start | bytes 700424 | tf_op jit(solution)/shard_map/ppermute | solution.py:268
  41.4 8.5 %collective-permute-start.8 = (f32[32,1792]{1,0:T(8,128)S(1)}, f32[32,1792]{1,0:T(8,128)S(1)}, u32[]{:S(2)}, u32[]{:S(2)}) collective-permute-start(f32[32,1792]{1,0:T(8,128)S(1)} %get-tuple-element.23), channel_id=1, source_target_pairs={{0,1},{1,0},{2,3},{3,2},{4,5},{5,4},{6,7},{7,6},{8,9},{9,8},{10,11... | collective-permute-start | bytes 688136 | tf_op jit(solution)/shard_map/ppermute | solution.py:271
  41.7 11.7 %collective-permute-start.9 = (f32[32,1792]{1,0:T(8,128)S(1)}, f32[32,1792]{1,0:T(8,128)S(1)}, u32[]{:S(2)}, u32[]{:S(2)}) collective-permute-start(f32[32,1792]{1,0:T(8,128)S(1)} %get-tuple-element.24), channel_id=1, source_target_pairs={{0,1},{1,0},{2,3},{3,2},{4,5},{5,4},{6,7},{7,6},{8,9},{9,8},{10,11... | collective-permute-start | bytes 688136 | tf_op jit(solution)/shard_map/ppermute | solution.py:271

commit v3 on v2

--- a/solution.py
+++ b/solution.py
@@ -12,6 +12,7 @@
 GROUP = 256
 LOW_EXP = -100.0
 ROOM = 60
+PIECE = 192
 SPLIT = 3
 VMEM = pl.BlockSpec(memory_space=pltpu.VMEM)
 SMEM = pl.BlockSpec(memory_space=pltpu.SMEM)
@@ -85,28 +86,6 @@
             )
 
 
-def mask_kernel(tile_ref, slab_ref, amp_ref, own_ref, far_ref, tile_list, slab, amp, present, sems):
-    wide, pair = lax.axis_index("wide"), lax.axis_index("pair")
-    copies = fetch([(tile_ref, tile_list), (slab_ref, slab), (amp_ref, amp)], sems)
-    count = amp_ref.shape[1] // BLK
-    for t in range(count):
-        present[t] = 0
-    copies[0].wait()
-    copies[1].wait()
-    tile = slab[wide * 2 + pair]
-    for k in range(tile_ref.shape[1]):
-        present[tile_list[tile, k]] = 1
-    copies[2].wait()
-    mine = wide // 4
-    low = low_lanes(BLK)
-    blocks = count // 4
-    for side, out in ((mine, own_ref), (1 - mine, far_ref)):
-        for s in range(blocks):
-            t = 2 * (side * blocks + s)
-            flag = jnp.where(low, present[t], present[t + 1])
-            out[:, s * LANES : (s + 1) * LANES] = jnp.where(flag > 0, amp[:, half(t)], 0)
-
-
 def raw_kernel(place, own_ref, near_ref, dense):
     wide = lax.axis_index("wide")
     depth, width = own_ref.shape
@@ -140,45 +119,63 @@
             )
 
 
-def pick(amps, rows, starts):
-    count = rows.shape[1] // BLK // len(starts)
+def mask_kernel(
+    tiles, head, tile_ref, slab_ref, amp_ref, own, far, tile_list, slab, amp, present, sems
+):
+    wide, pair = lax.axis_index("wide"), lax.axis_index("pair")
+    copies = fetch([(tile_ref, tile_list), (slab_ref, slab), (amp_ref, amp)], sems)
+    count = amp_ref.shape[1] // BLK
+    for t in range(count):
+        present[t] = 0
+    copies[0].wait()
+    copies[1].wait()
+    tile = slab[wide * 2 + pair]
+    for k in range(tile_list.shape[1]):
+        present[tile_list[tile, k]] = 1
+    chip = ((wide // 2) % 2) * 2 * tiles
+    order = [chip + t for t in range(2 * tiles)]
+    for first, last in ((0, head), (head, tiles)):
+        for source in (wide ^ 2, wide ^ 3):
+            order += [(source % 4) * tiles + t for t in range(first, last)]
     low = low_lanes(BLK)
-    for b in range(rows.shape[1] // LANES):
-        even, odd = (starts[d // count] + d % count for d in (2 * b, 2 * b + 1))
-        for n, amp in enumerate(amps):
+    copies[2].wait()
+    for side, out in ((1 - wide // 4, far), (wide // 4, own)):
+        base = side * (count // 2)
+        for b in range(count // 4):
+            even, odd = base + order[2 * b], base + order[2 * b + 1]
             left = pltpu.roll(amp[:, half(even)], (even % 2) * BLK, 1)
             right = pltpu.roll(amp[:, half(odd)], BLK - (odd % 2) * BLK, 1)
-            rows[n * BLK : (n + 1) * BLK, b * LANES : (b + 1) * LANES] = jnp.where(low, left, right)
+            flag = jnp.where(low, present[even], present[odd])
+            out[:, b * LANES : (b + 1) * LANES] = jnp.where(
+                flag > 0, jnp.where(low, left, right), 0
+            )
 
 
 def dot(a, b):
     return jnp.dot(a, b, preferred_element_type=jnp.float32)
 
 
-def spread_kernel(tiles, first, place, z_ref, y_ref, dense):
+def first_kernel(tiles, place, z_ref, *rest):
     wide = lax.axis_index("wide")
-    for n, (block, source) in enumerate(((z_ref, wide ^ 2), (y_ref, wide ^ 3))):
-        rows = block.shape[0]
-        spread(place, block, dense.at[n * rows : (n + 1) * rows], source * tiles + first)
-
-
-def chip_rows(amps, rows):
-    at = (lax.axis_index("wide") // 2) % 2
-    depth = rows.shape[1]
-    for n, amp in enumerate(amps):
-        rows[n * BLK : (n + 1) * BLK] = amp[:, pl.ds(pl.multiple_of(at * depth, LANES), depth)]
-
-
-def meet(amps, tiles, first, rows, dense):
-    wide = lax.axis_index("wide")
-    pick(amps, rows, [(source % 4) * tiles + first for source in (wide ^ 2, wide ^ 3)])
-    return dot(rows[...], dense[...])
-
-
-def early_kernel(tiles, raw, dense, a0, a1, a2, a3, acc_ref, raw_rows, rows):
-    amps = (a0, a1, a2, a3)
-    chip_rows(amps, raw_rows)
-    acc_ref[...] = dot(raw_rows[...], raw[...]) + meet(amps, tiles, 0, rows, dense)
+    y_refs, dense = rest[:-1], rest[-1]
+    row = 0
+    for blocks, source in (((z_ref,), wide ^ 2), (y_refs, wide ^ 3)):
+        tile = source * tiles
+        for block in blocks:
+            size = block.shape[0]
+            spread(place, block, dense.at[row : row + size], tile)
+            row, tile = row + size, tile + size // BLK
+
+
+def second_kernel(tiles, first, place, z_ref, dense):
+    spread(place, z_ref, dense, (lax.axis_index("wide") ^ 2) * tiles + first)
+
+
+def early_kernel(raw, dense, rows, acc_ref):
+    depth = raw.shape[0]
+    acc_ref[...] = dot(rows[:, :depth], raw[...]) + dot(
+        rows[:, depth : depth + dense.shape[0]], dense[...]
+    )
 
 
 def encode(values, out):
@@ -203,13 +200,17 @@
 
 
 def last_kernel(
-    tiles, first, place, z_ref, y_ref, a0, a1, a2, a3, acc_ref, keep_ref, upper_ref, lower_ref,
-    same_ref, cross_ref, dense, rows,
+    tiles, first, place, y_ref, z_dense, rows, far_cross, acc, cross_acc, keep_ref, upper_ref,
+    lower_ref, same_ref, cross_ref, dense,
 ):
-    spread_kernel(tiles, first, place, z_ref, y_ref, dense)
-    total = acc_ref[...] + meet((a0, a1, a2, a3), tiles, first, rows, dense)
-    encode(total[3 * BLK :], cross_ref)
-    encode(total[2 * BLK : 3 * BLK], same_ref)
+    depth = z_dense.shape[0]
+    dense[:depth] = z_dense[...]
+    source = lax.axis_index("wide") ^ 3
+    spread(place, y_ref, dense.at[depth : 2 * depth], source * tiles + first)
+    at = rows.shape[1] - 2 * depth
+    encode(cross_acc[...] + dot(far_cross[:, at:], dense[...]), cross_ref)
+    total = acc[...] + dot(rows[:, at:], dense[...])
+    encode(total[2 * BLK :], same_ref)
     keep_ref[...] = total[:BLK]
     upper_ref[...] = total[BLK : BLK + BLK // 2]
     lower_ref[...] = total[BLK + BLK // 2 : 2 * BLK]
@@ -274,6 +275,7 @@
 
     head = SPLIT
     tail = tiles - head
+
     first, second = call(
         pack_kernel,
         tuple(sds((count * BLK, keep * BLK), bf16) for count in (head, tail)),
@@ -286,16 +288,17 @@
         ],
         ROOM,
     )
+    cols = amplitudes.shape[1] // 2
     own, far = call(
-        mask_kernel,
-        (sds((BLK, amplitudes.shape[1] // 2), bf16),) * 2,
+        bind(mask_kernel, tiles, head),
+        (sds((BLK, cols), bf16),) * 2,
         (tile_list, slab_order, amplitudes),
         "aaa",
         [
             pltpu.SMEM(tile_list.shape, i32),
             pltpu.SMEM(slab_order.shape, i32),
             pltpu.VMEM(amplitudes.shape, bf16),
-            pltpu.SMEM((amplitudes.shape[1] // BLK,), i32),
+            pltpu.SMEM((2 * cols // BLK,), i32),
             pltpu.SemaphoreType.DMA((3,)),
         ],
         ROOM,
@@ -313,37 +316,38 @@
     place = (jnp.sum(jnp.where(hit, order, 0), axis=1) - 1).reshape(-1)
 
     raw = call(raw_kernel, sds((2 * depth, width), bf16), (place, integrals, near), "svv")
-    y_first = move(z_first, 1)
-    amps = (own, own_cross, far_same, far_cross)
-    rows = len(amps) * BLK
-    raw_rows = pltpu.VMEM((rows, 2 * depth), bf16)
-
-    def scratch(count):
-        return pltpu.VMEM((rows, 2 * count * BLK), bf16)
-
+    y_first = [move(z_first[a : a + PIECE], 1) for a in range(0, head * BLK, PIECE)]
+    y_first[0], own_cross = lax.optimization_barrier((y_first[0], own_cross))
     dense_first = call(
-        bind(spread_kernel, tiles, 0),
+        bind(first_kernel, tiles),
         sds((2 * head * BLK, width), bf16),
-        (place, z_first, y_first),
-        "svv",
-    )
-    acc = call(
-        bind(early_kernel, tiles),
-        sds((rows, width), f32),
-        (raw, dense_first, *amps),
-        "v" * 6,
-        [raw_rows, scratch(head)],
-    )
-    z_second, acc = lax.optimization_barrier((z_second, acc))
+        (place, z_first, *y_first),
+        "sv" + "v" * len(y_first),
+    )
+
+    def begin(rows):
+        return call(early_kernel, sds((rows.shape[0], width), f32), (raw, dense_first, rows), "vvv")
+
+    rows = jnp.concatenate((own, own_cross, far_same), axis=0)
+    acc = begin(rows)
+    far_cross, acc = lax.optimization_barrier((far_cross, acc))
+    cross_acc = begin(far_cross)
+    z_second, cross_acc = lax.optimization_barrier((z_second, cross_acc))
     y_second = move(z_second, 1)
+    z_dense = call(
+        bind(second_kernel, tiles, head),
+        sds((tail * BLK, width), bf16),
+        (place, z_second),
+        "sv",
+    )
     coded = sds((BLK * width // (16 * LANES) + 1, 16, LANES), i16)
     part = sds((BLK // 2, width), f32)
     keep_rows, upper, lower, same, cross = call(
         bind(last_kernel, tiles, head),
         (sds((BLK, width), f32), part, part, coded, coded),
-        (place, z_second, y_second, *amps, acc),
-        "s" + "v" * 7,
-        [pltpu.VMEM((2 * tail * BLK, width), bf16), scratch(tail)],
+        (place, y_second, z_dense, rows, far_cross, acc, cross_acc),
+        "svvvvvv",
+        [pltpu.VMEM((2 * tail * BLK, width), bf16)],
     )
     got_cross = move(cross, 4, 1)
     got_same = move(same, 4)

time: 63.5 us -> 61.1 us (0.962)
  waiting for transfers between devices: 30.6 us -> 28 us
  local copies, waits for them, and re-layouts: 0.21 us -> 1.2 us
  Pallas kernels: 16.2 us -> 15.4 us
    ppermute x7, waiting for transfers between devices: 12.8 us -> 10.6 us  [move(): lax.ppermute(x, 'wide', [(i, i ^ flip_wide) for i in range(wide_count)])]
    unnamed x7, local copies, waits for them, and re-layouts: 0.02 us -> 0.98 us
    pallas_call x7 -> x9, Pallas kernels: 16.2 us -> 15.4 us  [call(): pl.pallas_call(kernel, out_shape=out, in_specs=[specs[p] for p in places]...]
    ppermute x1, starting transfers between devices: 2.85 us -> 2.12 us  [move(): return lax.ppermute(x, ('wide', 'pair'), [(i, i ^ flip) for i in range(n)])]
    ppermute x7, starting transfers between devices: 7.69 us -> 8.42 us  [move(): lax.ppermute(x, 'wide', [(i, i ^ flip_wide) for i in range(wide_count)])]
  transfers between devices with their start and end apart: 12 -> 12, of which waited for: 7 -> 7; matrix products, arithmetic and copies ran while one was open for 0% -> 2% of each run, Pallas kernels for 18% -> 19%
where the time goes in v3:
time: 61.1 us; the launch traced here: 60.9 us
  waiting for transfers between devices  28 us (46%)
  starting transfers between devices  16 us (26%)
  Pallas kernels  15.4 us (25%)
  local copies, waits for them, and re-layouts  1.2 us (2%)
    pallas_call x9, Pallas kernels, call(): pl.pallas_call(kernel, out_shape=out, in_specs=[specs[p] for p in places]...  15.4 us
    ppermute x4, waiting for transfers between devices, move(): lax.ppermute(x, 'pair', [(i, i ^ flip_pair) for i in range(pair_count)])  11.8 us
    ppermute x7, waiting for transfers between devices, move(): lax.ppermute(x, 'wide', [(i, i ^ flip_wide) for i in range(wide_count)])  10.6 us
    ppermute x7, starting transfers between devices, move(): lax.ppermute(x, 'wide', [(i, i ^ flip_wide) for i in range(wide_count)])  8.42 us
    ppermute x1, waiting for transfers between devices, move(): return lax.ppermute(x, ('wide', 'pair'), [(i, i ^ flip) for i in range(n)])  5.66 us
    ppermute x4, starting transfers between devices, move(): lax.ppermute(x, 'pair', [(i, i ^ flip_pair) for i in range(pair_count)])  5.45 us
    ppermute x1, starting transfers between devices, move(): return lax.ppermute(x, ('wide', 'pair'), [(i, i ^ flip) for i in range(n)])  2.12 us
  transfers between devices with their start and end apart: 12, of which 7 were waited for; matrix products, arithmetic and copies ran while one was open for 2% of the time, Pallas kernels for 19%

profile of v3, /device:TPU:0, one launch (start us, length us, event | category | flops | bytes accessed | tf_op | source)
XLA Modules:
  0.0 60.9 jit_solution(12018069989316323118)
XLA Ops:
  0.0 0.0 copy-start.1
  0.0 0.5 collective-permute-start.1
  0.5 3.0 %shard_map.55 = (bf16[192,896]{1,0:T(8,128)(2,1)}, bf16[256,896]{1,0:T(8,128)(2,1)}) custom-call(s32[14,2,56]{2,1,0:T(2,128)} %bitcast.5, bf16[448,1792]{1,0:T(8,128)(2,1)} %own_ref.1), custom_call_target="tpu_custom_call" | custom-call | flops 1 | bytes 1 | tf_op jit(solution)/shard_map/pallas_call | solution.py:245
  3.5 2.7 %collective-permute-start.2 = (bf16[192,896]{1,0:T(8,128)(2,1)}, bf16[192,896]{1,0:T(8,128)(2,1)S(1)}, u32[]{:S(2)}, u32[]{:S(2)}) collective-permute-start(bf16[192,896]{1,0:T(8,128)(2,1)} %get-tuple-element.21), channel_id=1, source_target_pairs={{0,4},{2,6},{4,0},{6,2},{8,12},{10,14},{12,8},{14,10},{1,5},{3,7},... | collective-permute-start | bytes 1032200 | tf_op jit(solution)/shard_map/ppermute | solution.py:271
  6.2 2.2 %shard_map.57 = (bf16[64,1792]{1,0:T(8,128)(2,1)}, bf16[64,1792]{1,0:T(8,128)(2,1)}) custom-call(s32[16,28]{1,0:T(8,128)} %tile_ref.1, s32[16]{0:T(128)} %slab_ref.1, bf16[64,3584]{1,0:T(8,128)(2,1)} %amp_ref.1), custom_call_target="tpu_custom_call" | custom-call | flops 1 | bytes 1 | tf_op jit(solution)/shard_map/pallas_call | solution.py:245
  8.4 2.7 %collective-permute-start.5 = (bf16[64,1792]{1,0:T(8,128)(2,1)}, bf16[64,1792]{1,0:T(8,128)(2,1)S(1)}, u32[]{:S(2)}, u32[]{:S(2)}) collective-permute-start(bf16[64,1792]{1,0:T(8,128)(2,1)} %get-tuple-element.24), channel_id=1, source_target_pairs={{0,8},{2,10},{4,12},{6,14},{8,0},{10,2},{12,4},{14,6},{1,9},{3,11}... | collective-permute-start | bytes 688136 | tf_op jit(solution)/shard_map/ppermute | solution.py:271
  11.1 1.5 %collective-permute-start.4 = (bf16[64,1792]{1,0:T(8,128)(2,1)}, bf16[64,1792]{1,0:T(8,128)(2,1)S(1)}, u32[]{:S(2)}, u32[]{:S(2)}) collective-permute-start(bf16[64,1792]{1,0:T(8,128)(2,1)} %get-tuple-element.22), channel_id=1, source_target_pairs={{0,1},{1,0},{2,3},{3,2},{4,5},{5,4},{6,7},{7,6},{8,9},{9,8},{10,11... | collective-permute-start | bytes 688136 | tf_op jit(solution)/shard_map/ppermute | solution.py:272
  12.6 0.4 collective-permute-start
  13.0 0.0 copy-done.1
  13.1 0.1 select_reduce_fusion
  13.2 7.1 %collective-permute-done.2.z_ref = bf16[192,896]{1,0:T(8,128)(2,1)S(1)} collective-permute-done((bf16[192,896]{1,0:T(8,128)(2,1)}, bf16[192,896]{1,0:T(8,128)(2,1)S(1)}, u32[]{:S(2)}, u32[]{:S(2)}) %collective-permute-start.2) | collective-permute-done | bytes 344096 | tf_op jit(solution)/shard_map/ppermute | solution.py:271
  20.2 0.0 collective-permute-start.3
  20.2 0.1 copy.9
  20.3 0.1 sub.7.place
  20.4 1.0 %constant_dynamic-update-slice_fusion.2 = bf16[192,1792]{1,0:T(8,128)(2,1)S(1)} fusion(bf16[64,1792]{1,0:T(8,128)(2,1)} %get-tuple-element.22), kind=kLoop, calls=%fused_computation.4 | loop fusion | bytes 458752
  21.4 0.0 copy-start
  21.4 0.0 collective-permute-done.5
  21.4 1.9 %collective-permute-start.6 = (bf16[64,1792]{1,0:T(8,128)(2,1)S(1)}, bf16[64,1792]{1,0:T(8,128)(2,1)S(1)}, u32[]{:S(2)}, u32[]{:S(2)}) collective-permute-start(bf16[64,1792]{1,0:T(8,128)(2,1)S(1)} %collective-permute-done.5), channel_id=1, source_target_pairs={{0,1},{1,0},{2,3},{3,2},{4,5},{5,4},{6,7},{7,6},{8,9},{9,8},{10,11... | collective-permute-start | bytes 688136 | tf_op jit(solution)/shard_map/ppermute | solution.py:272
  23.4 0.0 collective-permute-done.4
  23.4 0.0 collective-permute-done.3.rest_0_
  23.4 1.7 %shard_map.58.dense = bf16[384,1792]{1,0:T(8,128)(2,1)S(1)} custom-call(s32[1568]{0:T(1024)S(1)} %sub.7.place, bf16[192,896]{1,0:T(8,128)(2,1)S(1)} %collective-permute-done.2.z_ref, bf16[192,896]{1,0:T(8,128)(2,1)S(1)} %collective-permute-done.3.rest_0_), custom_call_target="tpu_custom_call" | custom-call | flops 1 | bytes 1 | tf_op jit(solution)/shard_map/pallas_call | solution.py:245
  25.1 0.0 collective-permute-done.1.near_ref
  25.1 0.0 copy-done
  25.1 1.4 %shard_map.56.raw = bf16[896,1792]{1,0:T(8,128)(2,1)S(1)} custom-call(s32[1568]{0:T(1024)S(1)} %sub.7.place, bf16[448,1792]{1,0:T(8,128)(2,1)S(1)} %copy-done, bf16[448,1792]{1,0:T(8,128)(2,1)S(1)} %collective-permute-done.1.near_ref), custom_call_target="tpu_custom_call" | custom-call | flops 1 | bytes 1 | tf_op jit(solution)/shard_map/pallas_call | solution.py:245
  26.6 1.2 %shard_map.59.acc = f32[192,1792]{1,0:T(8,128)S(1)} custom-call(bf16[896,1792]{1,0:T(8,128)(2,1)S(1)} %shard_map.56.raw, bf16[384,1792]{1,0:T(8,128)(2,1)S(1)} %shard_map.58.dense, bf16[192,1792]{1,0:T(8,128)(2,1)S(1)} %constant_dynamic-update-slice_fusion.rows), custom_call_target="tpu_custom_call" | custom-call | flops 1 | bytes 1 | tf_op jit(solution)/shard_map/pallas_call | solution.py:245
  27.8 1.8 %collective-permute-done.6.rows.far_cross = bf16[64,1792]{1,0:T(8,128)(2,1)S(1)} collective-permute-done((bf16[64,1792]{1,0:T(8,128)(2,1)S(1)}, bf16[64,1792]{1,0:T(8,128)(2,1)S(1)}, u32[]{:S(2)}, u32[]{:S(2)}) %collective-permute-start.6) | collective-permute-done | bytes 229408 | tf_op jit(solution)/shard_map/ppermute | solution.py:272
  29.6 0.9 %shard_map.60.cross_acc = f32[64,1792]{1,0:T(8,128)S(1)} custom-call(bf16[896,1792]{1,0:T(8,128)(2,1)S(1)} %shard_map.56.raw, bf16[384,1792]{1,0:T(8,128)(2,1)S(1)} %shard_map.58.dense, bf16[64,1792]{1,0:T(8,128)(2,1)S(1)} %collective-permute-done.6.rows.far_cross), custom_call_target="tpu_custom_call" | custom-call | flops 1 | bytes 1 | tf_op jit(solution)/shard_map/pallas_call | solution.py:245
  30.5 0.0 collective-permute-done.z_ref
  30.5 0.1 collective-permute-start.7
  30.6 1.4 %shard_map.61.z_dense = bf16[256,1792]{1,0:T(8,128)(2,1)S(1)} custom-call(s32[1568]{0:T(1024)S(1)} %sub.7.place, bf16[256,896]{1,0:T(8,128)(2,1)S(1)} %collective-permute-done.z_ref), custom_call_target="tpu_custom_call" | custom-call | flops 1 | bytes 1 | tf_op jit(solution)/shard_map/pallas_call | solution.py:245
  32.0 0.4 collective-permute-done.7.y_ref
  32.4 2.4 %shard_map.62 = (f32[64,1792]{1,0:T(8,128)S(1)}, f32[32,1792]{1,0:T(8,128)S(1)}, f32[32,1792]{1,0:T(8,128)S(1)}, s16[57,16,128]{2,1,0:T(8,128)(2,1)S(1)}, s16[57,16,128]{2,1,0:T(8,128)(2,1)S(1)}) custom-call(s32[1568]{0:T(1024)S(1)} %sub.7.place, bf16[256,896]{1,0:T(8,128)(2,1)S(1)} %collective-permute-done.7.y_ref, ...), custom_call_target="tpu_custom_call" | custom-call | flops 1 | bytes 1 | tf_op jit(solution)/shard_map/pallas_call | solution.py:245
  34.8 2.1 %collective-permute-start.10 = (s16[57,16,128]{2,1,0:T(8,128)(2,1)S(1)}, s16[57,16,128]{2,1,0:T(8,128)(2,1)S(1)}, u32[]{:S(2)}, u32[]{:S(2)}) collective-permute-start(s16[57,16,128]{2,1,0:T(8,128)(2,1)S(1)} %get-tuple-element.33), channel_id=1, source_target_pairs={{0,8},{2,10},{4,12},{6,14},{8,0},{10,2},{12,4},{14,6},{1,9},{3,11}... | collective-permute-start | bytes 700424 | tf_op jit(solution)/shard_map/ppermute | solution.py:271
  36.9 2.1 %collective-permute-start.11 = (s16[57,16,128]{2,1,0:T(8,128)(2,1)S(1)}, s16[57,16,128]{2,1,0:T(8,128)(2,1)S(1)}, u32[]{:S(2)}, u32[]{:S(2)}) collective-permute-start(s16[57,16,128]{2,1,0:T(8,128)(2,1)S(1)} %get-tuple-element.34), channel_id=1, source_target_pairs={{0,9},{1,8},{2,11},{3,10},{4,13},{5,12},{6,15},{7,14},{8,1},{9,0},... | collective-permute-start | bytes 700424 | tf_op jit(solution)/shard_map/ppermute | solution.py:269
  39.0 0.3 collective-permute-start.8
  39.3 1.7 %collective-permute-start.9 = (f32[32,1792]{1,0:T(8,128)S(1)}, f32[32,1792]{1,0:T(8,128)S(1)}, u32[]{:S(2)}, u32[]{:S(2)}) collective-permute-start(f32[32,1792]{1,0:T(8,128)S(1)} %get-tuple-element.32), channel_id=1, source_target_pairs={{0,1},{1,0},{2,3},{3,2},{4,5},{5,4},{6,7},{7,6},{8,9},{9,8},{10,11... | collective-permute-start | bytes 688136 | tf_op jit(solution)/shard_map/ppermute | solution.py:272
  41.0 6.5 %collective-permute-done.8.upper_ref = f32[32,1792]{1,0:T(8,128)S(1)} collective-permute-done((f32[32,1792]{1,0:T(8,128)S(1)}, f32[32,1792]{1,0:T(8,128)S(1)}, u32[]{:S(2)}, u32[]{:S(2)}) %collective-permute-start.8) | collective-permute-done | bytes 229408 | tf_op jit(solution)/shard_map/ppermute | solution.py:272
  47.5 3.5 %collective-permute-done.9.lower_ref = f32[32,1792]{1,0:T(8,128)S(1)} collective-permute-done((f32[32,1792]{1,0:T(8,128)S(1)}, f32[32,1792]{1,0:T(8,128)S(1)}, u32[]{:S(2)}, u32[]{:S(2)}) %collective-permute-start.9) | collective-permute-done | bytes 229408 | tf_op jit(solution)/shard_map/ppermute | solution.py:272
  51.0 3.1 %collective-permute-done.10.same_ref = s16[57,16,128]{2,1,0:T(8,128)(2,1)S(1)} collective-permute-done((s16[57,16,128]{2,1,0:T(8,128)(2,1)S(1)}, s16[57,16,128]{2,1,0:T(8,128)(2,1)S(1)}, u32[]{:S(2)}, u32[]{:S(2)}) %collective-permute-start.10) | collective-permute-done | bytes 233504 | tf_op jit(solution)/shard_map/ppermute | solution.py:271
  54.1 5.7 %collective-permute-done.11.cross_ref = s16[57,16,128]{2,1,0:T(8,128)(2,1)S(1)} collective-permute-done((s16[57,16,128]{2,1,0:T(8,128)(2,1)S(1)}, s16[57,16,128]{2,1,0:T(8,128)(2,1)S(1)}, u32[]{:S(2)}, u32[]{:S(2)}) %collective-permute-start.11) | collective-permute-done | bytes 233504 | tf_op jit(solution)/shard_map/ppermute | solution.py:269
  59.7 1.2 %shard_map.63 = f32[64,3584]{1,0:T(8,128)} custom-call(f32[64,1792]{1,0:T(8,128)S(1)} %get-tuple-element.30.keep_ref, f32[32,1792]{1,0:T(8,128)S(1)} %collective-permute-done.8.upper_ref, f32[32,1792]{1,0:T(8,128)S(1)} %collective-permute-done.9.lower_ref, s16[57,16,128]{2,1,0:T(8,128)(2,1)S(1)} %collective-permute-done.10.same_ref, ...), custom_call_target="tpu_custom_call" | custom-call | flops 1 | bytes 1 | tf_op jit(solution)/shard_map/pallas_call | solution.py:245
  (6 shorter events, 0.1 us)
Async XLA Ops:
  0.0 13.0 %copy-start.1 = (s32[56,2,14]{0,1,2:T(2,128)S(1)}, s32[56,2,14]{0,1,2:T(2,128)}, u32[]{:S(2)}) copy-start(s32[56,2,14]{0,1,2:T(2,128)} %param.9) | copy-start | bytes 18820
  0.0 25.1 %collective-permute-start.1 = (bf16[448,1792]{1,0:T(8,128)(2,1)}, bf16[448,1792]{1,0:T(8,128)(2,1)S(1)}, u32[]{:S(2)}, u32[]{:S(2)}) collective-permute-start(bf16[448,1792]{1,0:T(8,128)(2,1)} %own_ref.1), channel_id=1, source_target_pairs={{0,2},{2,0},{4,6},{6,4},{8,10},{10,8},{12,14},{14,12},{1,3},{3,1},... | collective-permute-start | bytes 4816904 | tf_op jit(solution)/shard_map/ppermute | solution.py:271
  3.5 16.8 %collective-permute-start.2 = (bf16[192,896]{1,0:T(8,128)(2,1)}, bf16[192,896]{1,0:T(8,128)(2,1)S(1)}, u32[]{:S(2)}, u32[]{:S(2)}) collective-permute-start(bf16[192,896]{1,0:T(8,128)(2,1)} %get-tuple-element.21), channel_id=1, source_target_pairs={{0,4},{2,6},{4,0},{6,2},{8,12},{10,14},{12,8},{14,10},{1,5},{3,7},... | collective-permute-start | bytes 1032200 | tf_op jit(solution)/shard_map/ppermute | solution.py:271
  8.4 13.0 %collective-permute-start.5 = (bf16[64,1792]{1,0:T(8,128)(2,1)}, bf16[64,1792]{1,0:T(8,128)(2,1)S(1)}, u32[]{:S(2)}, u32[]{:S(2)}) collective-permute-start(bf16[64,1792]{1,0:T(8,128)(2,1)} %get-tuple-element.24), channel_id=1, source_target_pairs={{0,8},{2,10},{4,12},{6,14},{8,0},{10,2},{12,4},{14,6},{1,9},{3,11}... | collective-permute-start | bytes 688136 | tf_op jit(solution)/shard_map/ppermute | solution.py:271
  11.1 12.3 %collective-permute-start.4 = (bf16[64,1792]{1,0:T(8,128)(2,1)}, bf16[64,1792]{1,0:T(8,128)(2,1)S(1)}, u32[]{:S(2)}, u32[]{:S(2)}) collective-permute-start(bf16[64,1792]{1,0:T(8,128)(2,1)} %get-tuple-element.22), channel_id=1, source_target_pairs={{0,1},{1,0},{2,3},{3,2},{4,5},{5,4},{6,7},{7,6},{8,9},{9,8},{10,11... | collective-permute-start | bytes 688136 | tf_op jit(solution)/shard_map/ppermute | solution.py:272
  12.6 17.9 %collective-permute-start = (bf16[256,896]{1,0:T(8,128)(2,1)}, bf16[256,896]{1,0:T(8,128)(2,1)S(1)}, u32[]{:S(2)}, u32[]{:S(2)}) collective-permute-start(bf16[256,896]{1,0:T(8,128)(2,1)} %get-tuple-element.20), channel_id=1, source_target_pairs={{0,4},{2,6},{4,0},{6,2},{8,12},{10,14},{12,8},{14,10},{1,5},{3,7},... | collective-permute-start | bytes 1376264 | tf_op jit(solution)/shard_map/ppermute | solution.py:271
  20.2 3.1 %collective-permute-start.3 = (bf16[192,896]{1,0:T(8,128)(2,1)S(1)}, bf16[192,896]{1,0:T(8,128)(2,1)S(1)}, u32[]{:S(2)}, u32[]{:S(2)}) collective-permute-start(bf16[192,896]{1,0:T(8,128)(2,1)S(1)} %collective-permute-done.2.z_ref), channel_id=1, source_target_pairs={{0,2},{2,0},{4,6},{6,4},{8,10},{10,8},{12,14},{14,12},{1,3},{3,1},... | collective-permute-start | bytes 1032200 | tf_op jit(solution)/shard_map/ppermute | solution.py:271
  21.4 3.7 %copy-start = (bf16[448,1792]{1,0:T(8,128)(2,1)S(1)}, bf16[448,1792]{1,0:T(8,128)(2,1)}, u32[]{:S(2)}) copy-start(bf16[448,1792]{1,0:T(8,128)(2,1)} %own_ref.1) | copy-start | bytes 4816900
  21.4 8.2 %collective-permute-start.6 = (bf16[64,1792]{1,0:T(8,128)(2,1)S(1)}, bf16[64,1792]{1,0:T(8,128)(2,1)S(1)}, u32[]{:S(2)}, u32[]{:S(2)}) collective-permute-start(bf16[64,1792]{1,0:T(8,128)(2,1)S(1)} %collective-permute-done.5), channel_id=1, source_target_pairs={{0,1},{1,0},{2,3},{3,2},{4,5},{5,4},{6,7},{7,6},{8,9},{9,8},{10,11... | collective-permute-start | bytes 688136 | tf_op jit(solution)/shard_map/ppermute | solution.py:272
  30.5 1.9 %collective-permute-start.7 = (bf16[256,896]{1,0:T(8,128)(2,1)S(1)}, bf16[256,896]{1,0:T(8,128)(2,1)S(1)}, u32[]{:S(2)}, u32[]{:S(2)}) collective-permute-start(bf16[256,896]{1,0:T(8,128)(2,1)S(1)} %collective-permute-done.z_ref), channel_id=1, source_target_pairs={{0,2},{2,0},{4,6},{6,4},{8,10},{10,8},{12,14},{14,12},{1,3},{3,1},... | collective-permute-start | bytes 1376264 | tf_op jit(solution)/shard_map/ppermute | solution.py:271
  34.8 19.2 %collective-permute-start.10 = (s16[57,16,128]{2,1,0:T(8,128)(2,1)S(1)}, s16[57,16,128]{2,1,0:T(8,128)(2,1)S(1)}, u32[]{:S(2)}, u32[]{:S(2)}) collective-permute-start(s16[57,16,128]{2,1,0:T(8,128)(2,1)S(1)} %get-tuple-element.33), channel_id=1, source_target_pairs={{0,8},{2,10},{4,12},{6,14},{8,0},{10,2},{12,4},{14,6},{1,9},{3,11}... | collective-permute-start | bytes 700424 | tf_op jit(solution)/shard_map/ppermute | solution.py:271
  36.9 22.8 %collective-permute-start.11 = (s16[57,16,128]{2,1,0:T(8,128)(2,1)S(1)}, s16[57,16,128]{2,1,0:T(8,128)(2,1)S(1)}, u32[]{:S(2)}, u32[]{:S(2)}) collective-permute-start(s16[57,16,128]{2,1,0:T(8,128)(2,1)S(1)} %get-tuple-element.34), channel_id=1, source_target_pairs={{0,9},{1,8},{2,11},{3,10},{4,13},{5,12},{6,15},{7,14},{8,1},{9,0},... | collective-permute-start | bytes 700424 | tf_op jit(solution)/shard_map/ppermute | solution.py:269
  39.0 8.5 %collective-permute-start.8 = (f32[32,1792]{1,0:T(8,128)S(1)}, f32[32,1792]{1,0:T(8,128)S(1)}, u32[]{:S(2)}, u32[]{:S(2)}) collective-permute-start(f32[32,1792]{1,0:T(8,128)S(1)} %get-tuple-element.31), channel_id=1, source_target_pairs={{0,1},{1,0},{2,3},{3,2},{4,5},{5,4},{6,7},{7,6},{8,9},{9,8},{10,11... | collective-permute-start | bytes 688136 | tf_op jit(solution)/shard_map/ppermute | solution.py:272
  39.3 11.7 %collective-permute-start.9 = (f32[32,1792]{1,0:T(8,128)S(1)}, f32[32,1792]{1,0:T(8,128)S(1)}, u32[]{:S(2)}, u32[]{:S(2)}) collective-permute-start(f32[32,1792]{1,0:T(8,128)S(1)} %get-tuple-element.32), channel_id=1, source_target_pairs={{0,1},{1,0},{2,3},{3,2},{4,5},{5,4},{6,7},{7,6},{8,9},{9,8},{10,11... | collective-permute-start | bytes 688136 | tf_op jit(solution)/shard_map/ppermute | solution.py:272

commit v4 on v3

--- a/solution.py
+++ b/solution.py
@@ -64,26 +64,26 @@
     return copies
 
 
-def pack_kernel(lists_ref, block_ref, first_ref, second_ref, lists, block, sems):
+def pack_kernel(start, lists_ref, block_ref, out, lists, block, sems):
     wide, pair = lax.axis_index("wide"), lax.axis_index("pair")
     tiles = block_ref.shape[0] // BLK
-    keep = first_ref.shape[1] // BLK
-    split = first_ref.shape[0] // BLK
-    rows = [pl.ds(i * BLK, BLK) for i in range(tiles)]
-    copies = fetch([(lists_ref, lists)] + [(block_ref.at[r], block.at[r]) for r in rows], sems)
+    keep = out.shape[1] // BLK
+    count = out.shape[0] // BLK
+    rows = [pl.ds(i * BLK, BLK) for i in range(count)]
+    sources = [block_ref.at[pl.ds((start + i) * BLK, BLK)] for i in range(count)]
+    copies = fetch(
+        [(lists_ref, lists)] + [(s, block.at[r]) for s, r in zip(sources, rows)], sems
+    )
     copies[0].wait()
     low = low_lanes(BLK)
-    for i in range(tiles):
+    for i in range(count):
         copies[1 + i].wait()
-        out, row = (first_ref, i) if i < split else (second_ref, i - split)
-        u = wide * tiles + i
+        u = wide * tiles + start + i
         for j in range(keep // 2):
             even, odd = lists[2 * j, pair, u], lists[2 * j + 1, pair, u]
             left = pltpu.roll(block[rows[i], half(even)], (even % 2) * BLK, 1)
             right = pltpu.roll(block[rows[i], half(odd)], BLK - (odd % 2) * BLK, 1)
-            out[row * BLK : (row + 1) * BLK, j * LANES : (j + 1) * LANES] = jnp.where(
-                low, left, right
-            )
+            out[rows[i], j * LANES : (j + 1) * LANES] = jnp.where(low, left, right)
 
 
 def raw_kernel(place, own_ref, near_ref, dense):
@@ -196,60 +196,71 @@
                 at = i * across + g * (GROUP // LANES) + k
                 out[at] = coded[:, k * LANES : (k + 1) * LANES]
             exps = jnp.where(lane == i * groups + g, exp.astype(jnp.int32), exps)
-    out[out.shape[0] - 1] = exps.astype(jnp.int16)
-
-
-def last_kernel(
-    tiles, first, place, y_ref, z_dense, rows, far_cross, acc, cross_acc, keep_ref, upper_ref,
-    lower_ref, same_ref, cross_ref, dense,
-):
+    for n in range(BLK // high * across, out.shape[0]):
+        out[n] = exps.astype(jnp.int16)
+
+
+def cross_kernel(tiles, first, place, y_ref, z_dense, rows, acc, coded, y_dense):
+    spread(place, y_ref, y_dense, (lax.axis_index("wide") ^ 3) * tiles + first)
+    encode(acc[...] + finish(rows[...], z_dense, y_dense), coded)
+
+
+def finish(rows, z_dense, y_dense):
     depth = z_dense.shape[0]
-    dense[:depth] = z_dense[...]
-    source = lax.axis_index("wide") ^ 3
-    spread(place, y_ref, dense.at[depth : 2 * depth], source * tiles + first)
     at = rows.shape[1] - 2 * depth
-    encode(cross_acc[...] + dot(far_cross[:, at:], dense[...]), cross_ref)
-    total = acc[...] + dot(rows[:, at:], dense[...])
-    encode(total[2 * BLK :], same_ref)
+    return dot(rows[:, at : at + depth], z_dense[...]) + dot(rows[:, at + depth :], y_dense[...])
+
+
+def same_kernel(z_dense, y_dense, rows, acc, coded):
+    here = slice(2 * BLK, 3 * BLK)
+    encode(acc[here] + finish(rows[here], z_dense, y_dense), coded)
+
+
+def own_kernel(z_dense, y_dense, rows, acc, _, keep_ref, upper_ref, lower_ref):
+    here = slice(0, 2 * BLK)
+    total = acc[here] + finish(rows[here], z_dense, y_dense)
     keep_ref[...] = total[:BLK]
     upper_ref[...] = total[BLK : BLK + BLK // 2]
-    lower_ref[...] = total[BLK + BLK // 2 : 2 * BLK]
-
-
-def join_kernel(keep_ref, upper_ref, lower_ref, same_ref, cross_ref, out_ref):
-    pair = lax.axis_index("pair")
-    width = keep_ref.shape[1]
-    across, groups, high = width // LANES, width // GROUP, same_ref.shape[1]
-    for side, bases, coded in (
-        (pair, (keep_ref,), same_ref),
-        (1 - pair, (upper_ref, lower_ref), cross_ref),
-    ):
-        exps = coded[coded.shape[0] - 1].astype(jnp.int32).astype(jnp.float32)
-        for i in range(BLK // high):
-            base = bases[i * high // bases[0].shape[0]]
-            at = i * high % bases[0].shape[0]
-            for g in range(groups):
-                n = i * groups + g
-                scale = jnp.exp2(exps[:, n : n + 1] - 15.0)
-                for k in range(GROUP // LANES):
-                    s = g * (GROUP // LANES) + k
-                    value = coded[i * across + s].astype(jnp.int32).astype(jnp.float32) * scale
-                    where = pl.ds(pl.multiple_of(side * width + s * LANES, LANES), LANES)
-                    out_ref[i * high : (i + 1) * high, where] = (
-                        base[at : at + high, s * LANES : (s + 1) * LANES] + value
-                    )
-
-
-def call(kernel, out, operands, places, scratch=(), room=32):
+    lower_ref[...] = total[BLK + BLK // 2 :]
+
+
+def join_kernel(flip, coded, *rest):
+    bases, (out_ref, whole, sems) = rest[:-3], rest[-3:]
+    bases = bases[-2:] if flip else bases[-1:]
+    pair = lax.axis_index("pair") ^ flip
+    width = whole.shape[1]
+    across, groups, high = width // LANES, width // GROUP, coded.shape[1]
+    cols = pl.ds(pl.multiple_of(pair * width, LANES), width)
+    exps = coded[BLK // high * across].astype(jnp.int32).astype(jnp.float32)
+    copies = []
+    for i in range(BLK // high):
+        base = bases[i * high // bases[0].shape[0]]
+        at = i * high % bases[0].shape[0]
+        for g in range(groups):
+            n = i * groups + g
+            scale = jnp.exp2(exps[:, n : n + 1] - 15.0)
+            for k in range(GROUP // LANES):
+                s = g * (GROUP // LANES) + k
+                here = slice(s * LANES, (s + 1) * LANES)
+                value = coded[i * across + s].astype(jnp.int32).astype(jnp.float32) * scale
+                whole[i * high : (i + 1) * high, here] = base[at : at + high, here] + value
+        here = pl.ds(i * high, high)
+        copies.append(pltpu.make_async_copy(whole.at[here], out_ref.at[here, cols], sems.at[i]))
+        copies[-1].start()
+    for copy in copies:
+        copy.wait()
+
+
+def call(kernel, out, operands, places, scratch=(), room=32, **options):
     specs = {"s": SMEM, "v": VMEM, "a": pl.BlockSpec(memory_space=pltpu.HBM)}
     return pl.pallas_call(
         kernel,
         out_shape=out,
         in_specs=[specs[p] for p in places],
-        out_specs=jax.tree.map(lambda _: VMEM, out),
         scratch_shapes=list(scratch),
         compiler_params=pltpu.CompilerParams(vmem_limit_bytes=room * MIB),
         cost_estimate=pl.CostEstimate(flops=1, bytes_accessed=1, transcendentals=0),
+        **{"out_specs": jax.tree.map(lambda _: VMEM, out), **options},
     )(*operands)
 
 
@@ -276,18 +287,20 @@
     head = SPLIT
     tail = tiles - head
 
-    first, second = call(
-        pack_kernel,
-        tuple(sds((count * BLK, keep * BLK), bf16) for count in (head, tail)),
-        (lists, integrals),
-        "aa",
-        [
-            pltpu.SMEM(lists.shape, i32),
-            pltpu.VMEM(integrals.shape, bf16),
-            pltpu.SemaphoreType.DMA((tiles + 1,)),
-        ],
-        ROOM,
-    )
+    def pack(start, count):
+        return call(
+            bind(pack_kernel, start),
+            sds((count * BLK, keep * BLK), bf16),
+            (lists, integrals),
+            "aa",
+            [
+                pltpu.SMEM(lists.shape, i32),
+                pltpu.VMEM((count * BLK, width), bf16),
+                pltpu.SemaphoreType.DMA((count + 1,)),
+            ],
+            ROOM,
+        )
+
     cols = amplitudes.shape[1] // 2
     own, far = call(
         bind(mask_kernel, tiles, head),
@@ -303,8 +316,8 @@
         ],
         ROOM,
     )
-    z_first = move(first, 2)
-    z_second = move(second, 2)
+    z_first = move(pack(0, head), 2)
+    z_second = move(pack(head, tail), 2)
     far_same = move(far, 4)
     near = move(integrals, 1)
     own_cross = move(own, 0, 1)
@@ -340,23 +353,39 @@
         (place, z_second),
         "sv",
     )
-    coded = sds((BLK * width // (16 * LANES) + 1, 16, LANES), i16)
+    coded = BLK * width // (16 * LANES) + 1
     part = sds((BLK // 2, width), f32)
-    keep_rows, upper, lower, same, cross = call(
-        bind(last_kernel, tiles, head),
-        (sds((BLK, width), f32), part, part, coded, coded),
-        (place, y_second, z_dense, rows, far_cross, acc, cross_acc),
-        "svvvvvv",
-        [pltpu.VMEM((2 * tail * BLK, width), bf16)],
+    cross, y_dense = call(
+        bind(cross_kernel, tiles, head),
+        (sds((coded + 1, 16, LANES), i16), sds((tail * BLK, width), bf16)),
+        (place, y_second, z_dense, far_cross, cross_acc),
+        "svvvv",
     )
     got_cross = move(cross, 4, 1)
+    same = call(
+        same_kernel, sds((coded, 16, LANES), i16), (z_dense, y_dense, rows, acc), "vvvv"
+    )
     got_same = move(same, 4)
-    return call(
-        join_kernel,
-        sds((BLK, pair_count * width), f32),
-        (keep_rows, move(upper, 0, 1), move(lower, 0, 1), got_same, got_cross),
-        "v" * 5,
-    )
+    keep_rows, upper, lower = call(
+        own_kernel,
+        (sds((BLK, width), f32), part, part),
+        (z_dense, y_dense, rows, acc, same),
+        "vvvva",
+    )
+
+    def join(flip, coded, *bases):
+        return call(
+            bind(join_kernel, flip),
+            sds((BLK, pair_count * width), f32),
+            (coded, *bases),
+            "v" + ("vv" if flip else "av"),
+            [pltpu.VMEM((BLK, width), f32), pltpu.SemaphoreType.DMA((BLK // 16,))],
+            out_specs=pl.BlockSpec(memory_space=pltpu.HBM),
+            input_output_aliases={} if flip else {1: 0},
+        )
+
+    half_done = join(1, got_cross, move(upper, 0, 1), move(lower, 0, 1))
+    return join(0, got_same, half_done, keep_rows)
 
 
 def solution(mesh):

time: 61.1 us -> 59 us (0.966)
  Pallas kernels: 15.4 us -> 18.3 us
  starting transfers between devices: 16 us -> 13.3 us
  waiting for transfers between devices: 28 us -> 26.6 us
  local copies, waits for them, and re-layouts: 1.2 us -> 0.27 us
    ppermute x1, waiting for transfers between devices: 5.66 us -> 0.01 us  [move(): return lax.ppermute(x, ('wide', 'pair'), [(i, i ^ flip) for i in range(n)])]
    ppermute x4, waiting for transfers between devices: 11.8 us -> 16.5 us  [move(): lax.ppermute(x, 'pair', [(i, i ^ flip_pair) for i in range(pair_count)])]
    pallas_call x9 -> x13, Pallas kernels: 15.4 us -> 18.3 us  [call(): pl.pallas_call(kernel, out_shape=out, in_specs=[specs[p] for p in places]...]
    ppermute x7, starting transfers between devices: 8.42 us -> 6.62 us  [move(): lax.ppermute(x, 'wide', [(i, i ^ flip_wide) for i in range(wide_count)])]
    ppermute x4, starting transfers between devices: 5.45 us -> 3.97 us  [move(): lax.ppermute(x, 'pair', [(i, i ^ flip_pair) for i in range(pair_count)])]
    unnamed x7 -> x9, local copies, waits for them, and re-layouts: 0.98 us -> 0.05 us
  transfers between devices with their start and end apart: 12 -> 12, of which waited for: 7 -> 7; matrix products, arithmetic and copies ran while one was open for 2% -> 1% of each run, Pallas kernels for 19% -> 26%
where the time goes in v4:
time: 59 us; the launch traced here: 58.8 us
  waiting for transfers between devices  26.6 us (45%)
  Pallas kernels  18.3 us (31%)
  starting transfers between devices  13.3 us (23%)
    pallas_call x13, Pallas kernels, call(): pl.pallas_call(kernel, out_shape=out, in_specs=[specs[p] for p in places]...  18.3 us
    ppermute x4, waiting for transfers between devices, move(): lax.ppermute(x, 'pair', [(i, i ^ flip_pair) for i in range(pair_count)])  16.5 us
    ppermute x7, waiting for transfers between devices, move(): lax.ppermute(x, 'wide', [(i, i ^ flip_wide) for i in range(wide_count)])  10.1 us
    ppermute x7, starting transfers between devices, move(): lax.ppermute(x, 'wide', [(i, i ^ flip_wide) for i in range(wide_count)])  6.62 us
    ppermute x4, starting transfers between devices, move(): lax.ppermute(x, 'pair', [(i, i ^ flip_pair) for i in range(pair_count)])  3.97 us
    ppermute x1, starting transfers between devices, move(): return lax.ppermute(x, ('wide', 'pair'), [(i, i ^ flip) for i in range(n)])  2.68 us
  transfers between devices with their start and end apart: 12, of which 7 were waited for; matrix products, arithmetic and copies ran while one was open for 1% of the time, Pallas kernels for 26%

profile of v4, /device:TPU:0, one launch (start us, length us, event | category | flops | bytes accessed | tf_op | source)
XLA Modules:
  0.0 58.8 jit_solution(7356580538811053401)
XLA Ops:
  0.0 0.5 collective-permute-start.1
  0.5 2.2 %shard_map.57 = bf16[192,896]{1,0:T(8,128)(2,1)} custom-call(s32[14,2,56]{2,1,0:T(2,128)} %bitcast.4, bf16[448,1792]{1,0:T(8,128)(2,1)} %block_ref.3), custom_call_target="tpu_custom_call" | custom-call | flops 1 | bytes 1 | tf_op jit(solution)/shard_map/pallas_call | solution.py:256
  2.7 0.0 copy-start.2
  2.7 2.6 %collective-permute-start.2 = (bf16[192,896]{1,0:T(8,128)(2,1)}, bf16[192,896]{1,0:T(8,128)(2,1)S(1)}, u32[]{:S(2)}, u32[]{:S(2)}) collective-permute-start(bf16[192,896]{1,0:T(8,128)(2,1)} %shard_map.57), channel_id=1, source_target_pairs={{0,4},{2,6},{4,0},{6,2},{8,12},{10,14},{12,8},{14,10},{1,5},{3,7},... | collective-permute-start | bytes 1032200 | tf_op jit(solution)/shard_map/ppermute | solution.py:282
  5.3 2.2 %shard_map.58 = (bf16[64,1792]{1,0:T(8,128)(2,1)}, bf16[64,1792]{1,0:T(8,128)(2,1)}) custom-call(s32[16,28]{1,0:T(8,128)} %tile_ref.1, s32[16]{0:T(128)} %slab_ref.1, bf16[64,3584]{1,0:T(8,128)(2,1)} %amp_ref.1), custom_call_target="tpu_custom_call" | custom-call | flops 1 | bytes 1 | tf_op jit(solution)/shard_map/pallas_call | solution.py:256
  7.6 0.0 copy-start.1
  7.6 1.6 %collective-permute-start.4 = (bf16[64,1792]{1,0:T(8,128)(2,1)}, bf16[64,1792]{1,0:T(8,128)(2,1)S(1)}, u32[]{:S(2)}, u32[]{:S(2)}) collective-permute-start(bf16[64,1792]{1,0:T(8,128)(2,1)} %get-tuple-element.18), channel_id=1, source_target_pairs={{0,1},{1,0},{2,3},{3,2},{4,5},{5,4},{6,7},{7,6},{8,9},{9,8},{10,11... | collective-permute-start | bytes 688136 | tf_op jit(solution)/shard_map/ppermute | solution.py:283
  9.1 2.6 %collective-permute-start.5 = (bf16[64,1792]{1,0:T(8,128)(2,1)}, bf16[64,1792]{1,0:T(8,128)(2,1)S(1)}, u32[]{:S(2)}, u32[]{:S(2)}) collective-permute-start(bf16[64,1792]{1,0:T(8,128)(2,1)} %get-tuple-element.20), channel_id=1, source_target_pairs={{0,8},{2,10},{4,12},{6,14},{8,0},{10,2},{12,4},{14,6},{1,9},{3,11}... | collective-permute-start | bytes 688136 | tf_op jit(solution)/shard_map/ppermute | solution.py:282
  11.7 2.4 %shard_map.55 = bf16[256,896]{1,0:T(8,128)(2,1)} custom-call(s32[14,2,56]{2,1,0:T(2,128)} %bitcast.5, bf16[448,1792]{1,0:T(8,128)(2,1)} %block_ref.3), custom_call_target="tpu_custom_call" | custom-call | flops 1 | bytes 1 | tf_op jit(solution)/shard_map/pallas_call | solution.py:256
  14.1 0.5 collective-permute-start
  14.7 0.0 copy-done.2
  14.7 0.1 select_reduce_fusion
  14.8 3.4 %collective-permute-done.2.z_ref = bf16[192,896]{1,0:T(8,128)(2,1)S(1)} collective-permute-done((bf16[192,896]{1,0:T(8,128)(2,1)}, bf16[192,896]{1,0:T(8,128)(2,1)S(1)}, u32[]{:S(2)}, u32[]{:S(2)}) %collective-permute-start.2) | collective-permute-done | bytes 344096 | tf_op jit(solution)/shard_map/ppermute | solution.py:282
  18.2 0.0 collective-permute-start.3
  18.2 0.1 copy.10
  18.3 0.1 sub.7.place
  18.4 0.0 copy-done.1
  18.4 0.0 copy-start
  18.4 4.3 %collective-permute-done.5 = bf16[64,1792]{1,0:T(8,128)(2,1)S(1)} collective-permute-done((bf16[64,1792]{1,0:T(8,128)(2,1)}, bf16[64,1792]{1,0:T(8,128)(2,1)S(1)}, u32[]{:S(2)}, u32[]{:S(2)}) %collective-permute-start.5) | collective-permute-done | bytes 229408 | tf_op jit(solution)/shard_map/ppermute | solution.py:282
  22.8 0.3 collective-permute-start.6
  23.1 0.0 collective-permute-done.4
  23.1 0.0 collective-permute-done.3.rest_0_
  23.1 1.7 %shard_map.59.dense = bf16[384,1792]{1,0:T(8,128)(2,1)S(1)} custom-call(s32[1568]{0:T(1024)S(1)} %sub.7.place, bf16[192,896]{1,0:T(8,128)(2,1)S(1)} %collective-permute-done.2.z_ref, bf16[192,896]{1,0:T(8,128)(2,1)S(1)} %collective-permute-done.3.rest_0_), custom_call_target="tpu_custom_call" | custom-call | flops 1 | bytes 1 | tf_op jit(solution)/shard_map/pallas_call | solution.py:256
  24.8 0.0 collective-permute-done.1.near_ref
  24.8 0.0 copy-done
  24.8 1.4 %shard_map.56.raw = bf16[896,1792]{1,0:T(8,128)(2,1)S(1)} custom-call(s32[1568]{0:T(1024)S(1)} %sub.7.place, bf16[448,1792]{1,0:T(8,128)(2,1)S(1)} %copy-done, bf16[448,1792]{1,0:T(8,128)(2,1)S(1)} %collective-permute-done.1.near_ref), custom_call_target="tpu_custom_call" | custom-call | flops 1 | bytes 1 | tf_op jit(solution)/shard_map/pallas_call | solution.py:256
  26.3 1.2 %shard_map.60.acc = f32[192,1792]{1,0:T(8,128)S(1)} custom-call(bf16[896,1792]{1,0:T(8,128)(2,1)S(1)} %shard_map.56.raw, bf16[384,1792]{1,0:T(8,128)(2,1)S(1)} %shard_map.59.dense, bf16[192,1792]{1,0:T(8,128)(2,1)S(1)} %constant_dynamic-update-slice_fusion.rows), custom_call_target="tpu_custom_call" | custom-call | flops 1 | bytes 1 | tf_op jit(solution)/shard_map/pallas_call | solution.py:256
  27.5 1.6 %collective-permute-done.6.rows = bf16[64,1792]{1,0:T(8,128)(2,1)S(1)} collective-permute-done((bf16[64,1792]{1,0:T(8,128)(2,1)S(1)}, bf16[64,1792]{1,0:T(8,128)(2,1)S(1)}, u32[]{:S(2)}, u32[]{:S(2)}) %collective-permute-start.6) | collective-permute-done | bytes 229408 | tf_op jit(solution)/shard_map/ppermute | solution.py:283
  29.2 0.9 %shard_map.61.acc = f32[64,1792]{1,0:T(8,128)S(1)} custom-call(bf16[896,1792]{1,0:T(8,128)(2,1)S(1)} %shard_map.56.raw, bf16[384,1792]{1,0:T(8,128)(2,1)S(1)} %shard_map.59.dense, bf16[64,1792]{1,0:T(8,128)(2,1)S(1)} %collective-permute-done.6.rows), custom_call_target="tpu_custom_call" | custom-call | flops 1 | bytes 1 | tf_op jit(solution)/shard_map/pallas_call | solution.py:256
  30.0 0.0 collective-permute-done.z_ref
  30.1 0.1 collective-permute-start.7
  30.1 1.4 %shard_map.62.z_dense = bf16[256,1792]{1,0:T(8,128)(2,1)S(1)} custom-call(s32[1568]{0:T(1024)S(1)} %sub.7.place, bf16[256,896]{1,0:T(8,128)(2,1)S(1)} %collective-permute-done.z_ref), custom_call_target="tpu_custom_call" | custom-call | flops 1 | bytes 1 | tf_op jit(solution)/shard_map/pallas_call | solution.py:256
  31.5 0.4 collective-permute-done.7.y_ref
  31.9 2.0 %shard_map.63 = (s16[58,16,128]{2,1,0:T(8,128)(2,1)S(1)}, bf16[256,1792]{1,0:T(8,128)(2,1)S(1)}) custom-call(s32[1568]{0:T(1024)S(1)} %sub.7.place, bf16[256,896]{1,0:T(8,128)(2,1)S(1)} %collective-permute-done.7.y_ref, bf16[256,1792]{1,0:T(8,128)(2,1)S(1)} %shard_map.62.z_dense, bf16[64,1792]{1,0:T(8,128)(2,1)S(1)} %collective-permute-done.6.rows, ...), custom_call_target="tpu_custom_call" | custom-call | flops 1 | bytes 1 | tf_op jit(solution)/shard_map/pallas_call | solution.py:256
  34.0 2.7 %collective-permute-start.9 = (s16[58,16,128]{2,1,0:T(8,128)(2,1)S(1)}, s16[58,16,128]{2,1,0:T(8,128)(2,1)S(1)}, u32[]{:S(2)}, u32[]{:S(2)}) collective-permute-start(s16[58,16,128]{2,1,0:T(8,128)(2,1)S(1)} %get-tuple-element.27), channel_id=1, source_target_pairs={{0,9},{1,8},{2,11},{3,10},{4,13},{5,12},{6,15},{7,14},{8,1},{9,0},... | collective-permute-start | bytes 712712 | tf_op jit(solution)/shard_map/ppermute | solution.py:280
  36.7 0.6 %shard_map.64._ = s16[57,16,128]{2,1,0:T(8,128)(2,1)S(1)} custom-call(bf16[256,1792]{1,0:T(8,128)(2,1)S(1)} %shard_map.62.z_dense, bf16[256,1792]{1,0:T(8,128)(2,1)S(1)} %get-tuple-element.25.y_dense, bf16[192,1792]{1,0:T(8,128)(2,1)S(1)} %constant_dynamic-update-slice_fusion.rows, f32[192,1792]{1,0:T(8,128)S(1)} %shard_map.60.acc), custom_call_target="tpu_custom_call" | custom-call | flops 1 | bytes 1 | tf_op jit(solution)/shard_map/pallas_call | solution.py:256
  37.3 0.4 collective-permute-start.8
  37.6 0.4 shard_map.65
  38.1 1.5 %collective-permute-start.10 = (f32[32,1792]{1,0:T(8,128)S(1)}, f32[32,1792]{1,0:T(8,128)S(1)}, u32[]{:S(2)}, u32[]{:S(2)}) collective-permute-start(f32[32,1792]{1,0:T(8,128)S(1)} %get-tuple-element.28), channel_id=1, source_target_pairs={{0,1},{1,0},{2,3},{3,2},{4,5},{5,4},{6,7},{7,6},{8,9},{9,8},{10,11... | collective-permute-start | bytes 688136 | tf_op jit(solution)/shard_map/ppermute | solution.py:283
  39.6 0.5 collective-permute-start.11
  40.2 6.5 %collective-permute-done.10.rest_0_ = f32[32,1792]{1,0:T(8,128)S(1)} collective-permute-done((f32[32,1792]{1,0:T(8,128)S(1)}, f32[32,1792]{1,0:T(8,128)S(1)}, u32[]{:S(2)}, u32[]{:S(2)}) %collective-permute-start.10) | collective-permute-done | bytes 229408 | tf_op jit(solution)/shard_map/ppermute | solution.py:283
  46.7 8.3 %collective-permute-done.11.rest_1_ = f32[32,1792]{1,0:T(8,128)S(1)} collective-permute-done((f32[32,1792]{1,0:T(8,128)S(1)}, f32[32,1792]{1,0:T(8,128)S(1)}, u32[]{:S(2)}, u32[]{:S(2)}) %collective-permute-start.11) | collective-permute-done | bytes 229408 | tf_op jit(solution)/shard_map/ppermute | solution.py:283
  55.0 0.0 collective-permute-done.9.coded
  55.0 0.9 %shard_map.66.rest_0_ = f32[64,3584]{1,0:T(8,128)} custom-call(s16[58,16,128]{2,1,0:T(8,128)(2,1)S(1)} %collective-permute-done.9.coded, f32[32,1792]{1,0:T(8,128)S(1)} %collective-permute-done.10.rest_0_, f32[32,1792]{1,0:T(8,128)S(1)} %collective-permute-done.11.rest_1_), custom_call_target="tpu_custom_call" | custom-call | flops 1 | bytes 1 | tf_op jit(solution)/shard_map/pallas_call | solution.py:256
  55.9 2.0 %collective-permute-done.8.coded = s16[57,16,128]{2,1,0:T(8,128)(2,1)S(1)} collective-permute-done((s16[57,16,128]{2,1,0:T(8,128)(2,1)S(1)}, s16[57,16,128]{2,1,0:T(8,128)(2,1)S(1)}, u32[]{:S(2)}, u32[]{:S(2)}) %collective-permute-start.8) | collective-permute-done | bytes 233504 | tf_op jit(solution)/shard_map/ppermute | solution.py:282
  57.9 0.9 %shard_map.67 = f32[64,3584]{1,0:T(8,128)} custom-call(s16[57,16,128]{2,1,0:T(8,128)(2,1)S(1)} %collective-permute-done.8.coded, f32[64,3584]{1,0:T(8,128)} %shard_map.66.rest_0_, f32[64,1792]{1,0:T(8,128)S(1)} %get-tuple-element.30.rest_1_), custom_call_target="tpu_custom_call", output_to_operand_aliasing={{}: (1, {})} | custom-call | flops 1 | bytes 1 | tf_op jit(solution)/shard_map/pallas_call | solution.py:256
  (7 shorter events, 0.1 us)
Async XLA Ops:
  0.0 24.8 %collective-permute-start.1 = (bf16[448,1792]{1,0:T(8,128)(2,1)}, bf16[448,1792]{1,0:T(8,128)(2,1)S(1)}, u32[]{:S(2)}, u32[]{:S(2)}) collective-permute-start(bf16[448,1792]{1,0:T(8,128)(2,1)} %block_ref.3), channel_id=1, source_target_pairs={{0,2},{2,0},{4,6},{6,4},{8,10},{10,8},{12,14},{14,12},{1,3},{3,1},... | collective-permute-start | bytes 4816904 | tf_op jit(solution)/shard_map/ppermute | solution.py:282
  2.7 12.0 %copy-start.2 = (s32[56,2,14]{0,1,2:T(2,128)S(1)}, s32[56,2,14]{0,1,2:T(2,128)}, u32[]{:S(2)}) copy-start(s32[56,2,14]{0,1,2:T(2,128)} %param.9) | copy-start | bytes 18820
  2.7 15.5 %collective-permute-start.2 = (bf16[192,896]{1,0:T(8,128)(2,1)}, bf16[192,896]{1,0:T(8,128)(2,1)S(1)}, u32[]{:S(2)}, u32[]{:S(2)}) collective-permute-start(bf16[192,896]{1,0:T(8,128)(2,1)} %shard_map.57), channel_id=1, source_target_pairs={{0,4},{2,6},{4,0},{6,2},{8,12},{10,14},{12,8},{14,10},{1,5},{3,7},... | collective-permute-start | bytes 1032200 | tf_op jit(solution)/shard_map/ppermute | solution.py:282
  7.6 10.8 %copy-start.1 = (bf16[64,1792]{1,0:T(8,128)(2,1)S(1)}, bf16[64,1792]{1,0:T(8,128)(2,1)}, u32[]{:S(2)}) copy-start(bf16[64,1792]{1,0:T(8,128)(2,1)} %get-tuple-element.18) | copy-start | bytes 688132
  7.6 15.5 %collective-permute-start.4 = (bf16[64,1792]{1,0:T(8,128)(2,1)}, bf16[64,1792]{1,0:T(8,128)(2,1)S(1)}, u32[]{:S(2)}, u32[]{:S(2)}) collective-permute-start(bf16[64,1792]{1,0:T(8,128)(2,1)} %get-tuple-element.18), channel_id=1, source_target_pairs={{0,1},{1,0},{2,3},{3,2},{4,5},{5,4},{6,7},{7,6},{8,9},{9,8},{10,11... | collective-permute-start | bytes 688136 | tf_op jit(solution)/shard_map/ppermute | solution.py:283
  9.1 13.6 %collective-permute-start.5 = (bf16[64,1792]{1,0:T(8,128)(2,1)}, bf16[64,1792]{1,0:T(8,128)(2,1)S(1)}, u32[]{:S(2)}, u32[]{:S(2)}) collective-permute-start(bf16[64,1792]{1,0:T(8,128)(2,1)} %get-tuple-element.20), channel_id=1, source_target_pairs={{0,8},{2,10},{4,12},{6,14},{8,0},{10,2},{12,4},{14,6},{1,9},{3,11}... | collective-permute-start | bytes 688136 | tf_op jit(solution)/shard_map/ppermute | solution.py:282
  14.1 15.9 %collective-permute-start = (bf16[256,896]{1,0:T(8,128)(2,1)}, bf16[256,896]{1,0:T(8,128)(2,1)S(1)}, u32[]{:S(2)}, u32[]{:S(2)}) collective-permute-start(bf16[256,896]{1,0:T(8,128)(2,1)} %shard_map.55), channel_id=1, source_target_pairs={{0,4},{2,6},{4,0},{6,2},{8,12},{10,14},{12,8},{14,10},{1,5},{3,7},... | collective-permute-start | bytes 1376264 | tf_op jit(solution)/shard_map/ppermute | solution.py:282
  18.2 4.9 %collective-permute-start.3 = (bf16[192,896]{1,0:T(8,128)(2,1)S(1)}, bf16[192,896]{1,0:T(8,128)(2,1)S(1)}, u32[]{:S(2)}, u32[]{:S(2)}) collective-permute-start(bf16[192,896]{1,0:T(8,128)(2,1)S(1)} %collective-permute-done.2.z_ref), channel_id=1, source_target_pairs={{0,2},{2,0},{4,6},{6,4},{8,10},{10,8},{12,14},{14,12},{1,3},{3,1},... | collective-permute-start | bytes 1032200 | tf_op jit(solution)/shard_map/ppermute | solution.py:282
  18.4 6.4 %copy-start = (bf16[448,1792]{1,0:T(8,128)(2,1)S(1)}, bf16[448,1792]{1,0:T(8,128)(2,1)}, u32[]{:S(2)}) copy-start(bf16[448,1792]{1,0:T(8,128)(2,1)} %block_ref.3) | copy-start | bytes 4816900
  22.8 6.4 %collective-permute-start.6 = (bf16[64,1792]{1,0:T(8,128)(2,1)S(1)}, bf16[64,1792]{1,0:T(8,128)(2,1)S(1)}, u32[]{:S(2)}, u32[]{:S(2)}) collective-permute-start(bf16[64,1792]{1,0:T(8,128)(2,1)S(1)} %collective-permute-done.5), channel_id=1, source_target_pairs={{0,1},{1,0},{2,3},{3,2},{4,5},{5,4},{6,7},{7,6},{8,9},{9,8},{10,11... | collective-permute-start | bytes 688136 | tf_op jit(solution)/shard_map/ppermute | solution.py:283
  30.1 1.9 %collective-permute-start.7 = (bf16[256,896]{1,0:T(8,128)(2,1)S(1)}, bf16[256,896]{1,0:T(8,128)(2,1)S(1)}, u32[]{:S(2)}, u32[]{:S(2)}) collective-permute-start(bf16[256,896]{1,0:T(8,128)(2,1)S(1)} %collective-permute-done.z_ref), channel_id=1, source_target_pairs={{0,2},{2,0},{4,6},{6,4},{8,10},{10,8},{12,14},{14,12},{1,3},{3,1},... | collective-permute-start | bytes 1376264 | tf_op jit(solution)/shard_map/ppermute | solution.py:282
  34.0 21.0 %collective-permute-start.9 = (s16[58,16,128]{2,1,0:T(8,128)(2,1)S(1)}, s16[58,16,128]{2,1,0:T(8,128)(2,1)S(1)}, u32[]{:S(2)}, u32[]{:S(2)}) collective-permute-start(s16[58,16,128]{2,1,0:T(8,128)(2,1)S(1)} %get-tuple-element.27), channel_id=1, source_target_pairs={{0,9},{1,8},{2,11},{3,10},{4,13},{5,12},{6,15},{7,14},{8,1},{9,0},... | collective-permute-start | bytes 712712 | tf_op jit(solution)/shard_map/ppermute | solution.py:280
  37.3 20.6 %collective-permute-start.8 = (s16[57,16,128]{2,1,0:T(8,128)(2,1)S(1)}, s16[57,16,128]{2,1,0:T(8,128)(2,1)S(1)}, u32[]{:S(2)}, u32[]{:S(2)}) collective-permute-start(s16[57,16,128]{2,1,0:T(8,128)(2,1)S(1)} %shard_map.64._), channel_id=1, source_target_pairs={{0,8},{2,10},{4,12},{6,14},{8,0},{10,2},{12,4},{14,6},{1,9},{3,11}... | collective-permute-start | bytes 700424 | tf_op jit(solution)/shard_map/ppermute | solution.py:282
  38.1 8.6 %collective-permute-start.10 = (f32[32,1792]{1,0:T(8,128)S(1)}, f32[32,1792]{1,0:T(8,128)S(1)}, u32[]{:S(2)}, u32[]{:S(2)}) collective-permute-start(f32[32,1792]{1,0:T(8,128)S(1)} %get-tuple-element.28), channel_id=1, source_target_pairs={{0,1},{1,0},{2,3},{3,2},{4,5},{5,4},{6,7},{7,6},{8,9},{9,8},{10,11... | collective-permute-start | bytes 688136 | tf_op jit(solution)/shard_map/ppermute | solution.py:283
  39.6 15.4 %collective-permute-start.11 = (f32[32,1792]{1,0:T(8,128)S(1)}, f32[32,1792]{1,0:T(8,128)S(1)}, u32[]{:S(2)}, u32[]{:S(2)}) collective-permute-start(f32[32,1792]{1,0:T(8,128)S(1)} %get-tuple-element.29), channel_id=1, source_target_pairs={{0,1},{1,0},{2,3},{3,2},{4,5},{5,4},{6,7},{7,6},{8,9},{9,8},{10,11... | collective-permute-start | bytes 688136 | tf_op jit(solution)/shard_map/ppermute | solution.py:283

commit v5 on v4

--- a/solution.py
+++ b/solution.py
@@ -200,9 +200,17 @@
         out[n] = exps.astype(jnp.int16)
 
 
-def cross_kernel(tiles, first, place, y_ref, z_dense, rows, acc, coded, y_dense):
-    spread(place, y_ref, y_dense, (lax.axis_index("wide") ^ 3) * tiles + first)
-    encode(acc[...] + finish(rows[...], z_dense, y_dense), coded)
+def cross_kernel(
+    tiles, first, place_ref, y_ref, z_dense, rows, acc, coded, y_dense, place, y, sems
+):
+    copies = fetch([(place_ref, place), (y_ref, y)], sems)
+    depth = z_dense.shape[0]
+    at = rows.shape[1] - 2 * depth
+    total = acc[...] + dot(rows[:, at : at + depth], z_dense[...])
+    for copy in copies:
+        copy.wait()
+    spread(place, y, y_dense, (lax.axis_index("wide") ^ 3) * tiles + first)
+    encode(total + dot(rows[:, at + depth :], y_dense[...]), coded)
 
 
 def finish(rows, z_dense, y_dense):
@@ -252,7 +260,7 @@
 
 
 def call(kernel, out, operands, places, scratch=(), room=32, **options):
-    specs = {"s": SMEM, "v": VMEM, "a": pl.BlockSpec(memory_space=pltpu.HBM)}
+    specs = {"s": SMEM, "v": VMEM, "a": pl.BlockSpec(memory_space=pl.ANY)}
     return pl.pallas_call(
         kernel,
         out_shape=out,
@@ -359,7 +367,12 @@
         bind(cross_kernel, tiles, head),
         (sds((coded + 1, 16, LANES), i16), sds((tail * BLK, width), bf16)),
         (place, y_second, z_dense, far_cross, cross_acc),
-        "svvvv",
+        "aavvv",
+        [
+            pltpu.SMEM(place.shape, i32),
+            pltpu.VMEM(y_second.shape, bf16),
+            pltpu.SemaphoreType.DMA((2,)),
+        ],
     )
     got_cross = move(cross, 4, 1)
     same = call(

time: 59 us -> 58.9 us (level)
  no operation moved by 1% of the time
where the time goes in v5:
time: 58.9 us; the launch traced here: 58.7 us
  waiting for transfers between devices  26.6 us (45%)
  Pallas kernels  18.2 us (31%)
  starting transfers between devices  13.3 us (23%)
    pallas_call x13, Pallas kernels, call(): pl.pallas_call(kernel, out_shape=out, in_specs=[specs[p] for p in places]...  18.2 us
    ppermute x4, waiting for transfers between devices, move(): lax.ppermute(x, 'pair', [(i, i ^ flip_pair) for i in range(pair_count)])  16.5 us
    ppermute x7, waiting for transfers between devices, move(): lax.ppermute(x, 'wide', [(i, i ^ flip_wide) for i in range(wide_count)])  10.1 us
    ppermute x7, starting transfers between devices, move(): lax.ppermute(x, 'wide', [(i, i ^ flip_wide) for i in range(wide_count)])  6.63 us
    ppermute x4, starting transfers between devices, move(): lax.ppermute(x, 'pair', [(i, i ^ flip_pair) for i in range(pair_count)])  3.97 us
    ppermute x1, starting transfers between devices, move(): return lax.ppermute(x, ('wide', 'pair'), [(i, i ^ flip) for i in range(n)])  2.68 us
  transfers between devices with their start and end apart: 12, of which 7 were waited for; matrix products, arithmetic and copies ran while one was open for 1% of the time, Pallas kernels for 26%

profile of v5, /device:TPU:0, one launch (start us, length us, event | category | flops | bytes accessed | tf_op | source)
XLA Modules:
  0.0 58.7 jit_solution(11303221098677979042)
XLA Ops:
  0.0 0.5 collective-permute-start.1
  0.5 2.2 %shard_map.57 = bf16[192,896]{1,0:T(8,128)(2,1)} custom-call(s32[14,2,56]{2,1,0:T(2,128)} %bitcast.4, bf16[448,1792]{1,0:T(8,128)(2,1)} %block_ref.3), custom_call_target="tpu_custom_call" | custom-call | flops 1 | bytes 1 | tf_op jit(solution)/shard_map/pallas_call | solution.py:264
  2.7 0.0 copy-start.2
  2.7 2.6 %collective-permute-start.2 = (bf16[192,896]{1,0:T(8,128)(2,1)}, bf16[192,896]{1,0:T(8,128)(2,1)S(1)}, u32[]{:S(2)}, u32[]{:S(2)}) collective-permute-start(bf16[192,896]{1,0:T(8,128)(2,1)} %shard_map.57), channel_id=1, source_target_pairs={{0,4},{2,6},{4,0},{6,2},{8,12},{10,14},{12,8},{14,10},{1,5},{3,7},... | collective-permute-start | bytes 1032200 | tf_op jit(solution)/shard_map/ppermute | solution.py:290
  5.3 2.2 %shard_map.58 = (bf16[64,1792]{1,0:T(8,128)(2,1)}, bf16[64,1792]{1,0:T(8,128)(2,1)}) custom-call(s32[16,28]{1,0:T(8,128)} %tile_ref.1, s32[16]{0:T(128)} %slab_ref.1, bf16[64,3584]{1,0:T(8,128)(2,1)} %amp_ref.1), custom_call_target="tpu_custom_call" | custom-call | flops 1 | bytes 1 | tf_op jit(solution)/shard_map/pallas_call | solution.py:264
  7.6 0.0 copy-start.1
  7.6 1.6 %collective-permute-start.4 = (bf16[64,1792]{1,0:T(8,128)(2,1)}, bf16[64,1792]{1,0:T(8,128)(2,1)S(1)}, u32[]{:S(2)}, u32[]{:S(2)}) collective-permute-start(bf16[64,1792]{1,0:T(8,128)(2,1)} %get-tuple-element.18), channel_id=1, source_target_pairs={{0,1},{1,0},{2,3},{3,2},{4,5},{5,4},{6,7},{7,6},{8,9},{9,8},{10,11... | collective-permute-start | bytes 688136 | tf_op jit(solution)/shard_map/ppermute | solution.py:291
  9.1 2.6 %collective-permute-start.5 = (bf16[64,1792]{1,0:T(8,128)(2,1)}, bf16[64,1792]{1,0:T(8,128)(2,1)S(1)}, u32[]{:S(2)}, u32[]{:S(2)}) collective-permute-start(bf16[64,1792]{1,0:T(8,128)(2,1)} %get-tuple-element.20), channel_id=1, source_target_pairs={{0,8},{2,10},{4,12},{6,14},{8,0},{10,2},{12,4},{14,6},{1,9},{3,11}... | collective-permute-start | bytes 688136 | tf_op jit(solution)/shard_map/ppermute | solution.py:290
  11.7 2.4 %shard_map.55 = bf16[256,896]{1,0:T(8,128)(2,1)} custom-call(s32[14,2,56]{2,1,0:T(2,128)} %bitcast.5, bf16[448,1792]{1,0:T(8,128)(2,1)} %block_ref.3), custom_call_target="tpu_custom_call" | custom-call | flops 1 | bytes 1 | tf_op jit(solution)/shard_map/pallas_call | solution.py:264
  14.1 0.5 collective-permute-start
  14.7 0.0 copy-done.2
  14.7 0.1 select_reduce_fusion
  14.8 3.4 %collective-permute-done.2.z_ref = bf16[192,896]{1,0:T(8,128)(2,1)S(1)} collective-permute-done((bf16[192,896]{1,0:T(8,128)(2,1)}, bf16[192,896]{1,0:T(8,128)(2,1)S(1)}, u32[]{:S(2)}, u32[]{:S(2)}) %collective-permute-start.2) | collective-permute-done | bytes 344096 | tf_op jit(solution)/shard_map/ppermute | solution.py:290
  18.2 0.0 collective-permute-start.3
  18.2 0.1 copy.10
  18.3 0.1 sub.7.place.place_ref
  18.4 0.0 copy-done.1
  18.4 0.0 copy-start
  18.4 4.3 %collective-permute-done.5 = bf16[64,1792]{1,0:T(8,128)(2,1)S(1)} collective-permute-done((bf16[64,1792]{1,0:T(8,128)(2,1)}, bf16[64,1792]{1,0:T(8,128)(2,1)S(1)}, u32[]{:S(2)}, u32[]{:S(2)}) %collective-permute-start.5) | collective-permute-done | bytes 229408 | tf_op jit(solution)/shard_map/ppermute | solution.py:290
  22.8 0.3 collective-permute-start.6
  23.1 0.0 collective-permute-done.4
  23.1 0.0 collective-permute-done.3.rest_0_
  23.1 1.7 %shard_map.59.dense = bf16[384,1792]{1,0:T(8,128)(2,1)S(1)} custom-call(s32[1568]{0:T(1024)S(1)} %sub.7.place.place_ref, bf16[192,896]{1,0:T(8,128)(2,1)S(1)} %collective-permute-done.2.z_ref, bf16[192,896]{1,0:T(8,128)(2,1)S(1)} %collective-permute-done.3.rest_0_), custom_call_target="tpu_custom_call" | custom-call | flops 1 | bytes 1 | tf_op jit(solution)/shard_map/pallas_call | solution.py:264
  24.8 0.0 collective-permute-done.1.near_ref
  24.8 0.0 copy-done
  24.8 1.4 %shard_map.56.raw = bf16[896,1792]{1,0:T(8,128)(2,1)S(1)} custom-call(s32[1568]{0:T(1024)S(1)} %sub.7.place.place_ref, bf16[448,1792]{1,0:T(8,128)(2,1)S(1)} %copy-done, bf16[448,1792]{1,0:T(8,128)(2,1)S(1)} %collective-permute-done.1.near_ref), custom_call_target="tpu_custom_call" | custom-call | flops 1 | bytes 1 | tf_op jit(solution)/shard_map/pallas_call | solution.py:264
  26.3 1.2 %shard_map.60.acc = f32[192,1792]{1,0:T(8,128)S(1)} custom-call(bf16[896,1792]{1,0:T(8,128)(2,1)S(1)} %shard_map.56.raw, bf16[384,1792]{1,0:T(8,128)(2,1)S(1)} %shard_map.59.dense, bf16[192,1792]{1,0:T(8,128)(2,1)S(1)} %constant_dynamic-update-slice_fusion.rows), custom_call_target="tpu_custom_call" | custom-call | flops 1 | bytes 1 | tf_op jit(solution)/shard_map/pallas_call | solution.py:264
  27.5 1.6 %collective-permute-done.6.rows = bf16[64,1792]{1,0:T(8,128)(2,1)S(1)} collective-permute-done((bf16[64,1792]{1,0:T(8,128)(2,1)S(1)}, bf16[64,1792]{1,0:T(8,128)(2,1)S(1)}, u32[]{:S(2)}, u32[]{:S(2)}) %collective-permute-start.6) | collective-permute-done | bytes 229408 | tf_op jit(solution)/shard_map/ppermute | solution.py:291
  29.2 0.9 %shard_map.61.acc = f32[64,1792]{1,0:T(8,128)S(1)} custom-call(bf16[896,1792]{1,0:T(8,128)(2,1)S(1)} %shard_map.56.raw, bf16[384,1792]{1,0:T(8,128)(2,1)S(1)} %shard_map.59.dense, bf16[64,1792]{1,0:T(8,128)(2,1)S(1)} %collective-permute-done.6.rows), custom_call_target="tpu_custom_call" | custom-call | flops 1 | bytes 1 | tf_op jit(solution)/shard_map/pallas_call | solution.py:264
  30.0 0.0 collective-permute-done.z_ref
  30.1 0.1 collective-permute-start.7
  30.1 1.4 %shard_map.62.z_dense = bf16[256,1792]{1,0:T(8,128)(2,1)S(1)} custom-call(s32[1568]{0:T(1024)S(1)} %sub.7.place.place_ref, bf16[256,896]{1,0:T(8,128)(2,1)S(1)} %collective-permute-done.z_ref), custom_call_target="tpu_custom_call" | custom-call | flops 1 | bytes 1 | tf_op jit(solution)/shard_map/pallas_call | solution.py:264
  31.5 0.4 collective-permute-done.7.y_ref
  31.9 1.9 %shard_map.63 = (s16[58,16,128]{2,1,0:T(8,128)(2,1)S(1)}, bf16[256,1792]{1,0:T(8,128)(2,1)S(1)}) custom-call(s32[1568]{0:T(1024)S(1)} %sub.7.place.place_ref, bf16[256,896]{1,0:T(8,128)(2,1)S(1)} %collective-permute-done.7.y_ref, bf16[256,1792]{1,0:T(8,128)(2,1)S(1)} %shard_map.62.z_dense, bf16[64,1792]{1,0:T(8,128)(2,1)S(1)} %collective-permute-done.6.rows, ...), custom_call_target="tpu_custom_call" | custom-call | flops 1 | bytes 1 | tf_op jit(solution)/shard_map/pallas_call | solution.py:264
  33.9 2.7 %collective-permute-start.9 = (s16[58,16,128]{2,1,0:T(8,128)(2,1)S(1)}, s16[58,16,128]{2,1,0:T(8,128)(2,1)S(1)}, u32[]{:S(2)}, u32[]{:S(2)}) collective-permute-start(s16[58,16,128]{2,1,0:T(8,128)(2,1)S(1)} %get-tuple-element.27), channel_id=1, source_target_pairs={{0,9},{1,8},{2,11},{3,10},{4,13},{5,12},{6,15},{7,14},{8,1},{9,0},... | collective-permute-start | bytes 712712 | tf_op jit(solution)/shard_map/ppermute | solution.py:288
  36.6 0.6 %shard_map.64._ = s16[57,16,128]{2,1,0:T(8,128)(2,1)S(1)} custom-call(bf16[256,1792]{1,0:T(8,128)(2,1)S(1)} %shard_map.62.z_dense, bf16[256,1792]{1,0:T(8,128)(2,1)S(1)} %get-tuple-element.25.y_dense, bf16[192,1792]{1,0:T(8,128)(2,1)S(1)} %constant_dynamic-update-slice_fusion.rows, f32[192,1792]{1,0:T(8,128)S(1)} %shard_map.60.acc), custom_call_target="tpu_custom_call" | custom-call | flops 1 | bytes 1 | tf_op jit(solution)/shard_map/pallas_call | solution.py:264
  37.2 0.4 collective-permute-start.8
  37.5 0.4 shard_map.65
  38.0 1.5 %collective-permute-start.10 = (f32[32,1792]{1,0:T(8,128)S(1)}, f32[32,1792]{1,0:T(8,128)S(1)}, u32[]{:S(2)}, u32[]{:S(2)}) collective-permute-start(f32[32,1792]{1,0:T(8,128)S(1)} %get-tuple-element.28), channel_id=1, source_target_pairs={{0,1},{1,0},{2,3},{3,2},{4,5},{5,4},{6,7},{7,6},{8,9},{9,8},{10,11... | collective-permute-start | bytes 688136 | tf_op jit(solution)/shard_map/ppermute | solution.py:291
  39.5 0.5 collective-permute-start.11
  40.1 6.5 %collective-permute-done.10.rest_0_ = f32[32,1792]{1,0:T(8,128)S(1)} collective-permute-done((f32[32,1792]{1,0:T(8,128)S(1)}, f32[32,1792]{1,0:T(8,128)S(1)}, u32[]{:S(2)}, u32[]{:S(2)}) %collective-permute-start.10) | collective-permute-done | bytes 229408 | tf_op jit(solution)/shard_map/ppermute | solution.py:291
  46.6 8.3 %collective-permute-done.11.rest_1_ = f32[32,1792]{1,0:T(8,128)S(1)} collective-permute-done((f32[32,1792]{1,0:T(8,128)S(1)}, f32[32,1792]{1,0:T(8,128)S(1)}, u32[]{:S(2)}, u32[]{:S(2)}) %collective-permute-start.11) | collective-permute-done | bytes 229408 | tf_op jit(solution)/shard_map/ppermute | solution.py:291
  54.9 0.0 collective-permute-done.9.coded
  54.9 0.9 %shard_map.66.rest_0_ = f32[64,3584]{1,0:T(8,128)} custom-call(s16[58,16,128]{2,1,0:T(8,128)(2,1)S(1)} %collective-permute-done.9.coded, f32[32,1792]{1,0:T(8,128)S(1)} %collective-permute-done.10.rest_0_, f32[32,1792]{1,0:T(8,128)S(1)} %collective-permute-done.11.rest_1_), custom_call_target="tpu_custom_call" | custom-call | flops 1 | bytes 1 | tf_op jit(solution)/shard_map/pallas_call | solution.py:264
  55.8 1.9 %collective-permute-done.8.coded = s16[57,16,128]{2,1,0:T(8,128)(2,1)S(1)} collective-permute-done((s16[57,16,128]{2,1,0:T(8,128)(2,1)S(1)}, s16[57,16,128]{2,1,0:T(8,128)(2,1)S(1)}, u32[]{:S(2)}, u32[]{:S(2)}) %collective-permute-start.8) | collective-permute-done | bytes 233504 | tf_op jit(solution)/shard_map/ppermute | solution.py:290
  57.8 0.9 %shard_map.67 = f32[64,3584]{1,0:T(8,128)} custom-call(s16[57,16,128]{2,1,0:T(8,128)(2,1)S(1)} %collective-permute-done.8.coded, f32[64,3584]{1,0:T(8,128)} %shard_map.66.rest_0_, f32[64,1792]{1,0:T(8,128)S(1)} %get-tuple-element.30.rest_1_), custom_call_target="tpu_custom_call", output_to_operand_aliasing={{}: (1, {})} | custom-call | flops 1 | bytes 1 | tf_op jit(solution)/shard_map/pallas_call | solution.py:264
  (7 shorter events, 0.1 us)
Async XLA Ops:
  0.0 24.8 %collective-permute-start.1 = (bf16[448,1792]{1,0:T(8,128)(2,1)}, bf16[448,1792]{1,0:T(8,128)(2,1)S(1)}, u32[]{:S(2)}, u32[]{:S(2)}) collective-permute-start(bf16[448,1792]{1,0:T(8,128)(2,1)} %block_ref.3), channel_id=1, source_target_pairs={{0,2},{2,0},{4,6},{6,4},{8,10},{10,8},{12,14},{14,12},{1,3},{3,1},... | collective-permute-start | bytes 4816904 | tf_op jit(solution)/shard_map/ppermute | solution.py:290
  2.7 12.0 %copy-start.2 = (s32[56,2,14]{0,1,2:T(2,128)S(1)}, s32[56,2,14]{0,1,2:T(2,128)}, u32[]{:S(2)}) copy-start(s32[56,2,14]{0,1,2:T(2,128)} %param.9) | copy-start | bytes 18820
  2.7 15.5 %collective-permute-start.2 = (bf16[192,896]{1,0:T(8,128)(2,1)}, bf16[192,896]{1,0:T(8,128)(2,1)S(1)}, u32[]{:S(2)}, u32[]{:S(2)}) collective-permute-start(bf16[192,896]{1,0:T(8,128)(2,1)} %shard_map.57), channel_id=1, source_target_pairs={{0,4},{2,6},{4,0},{6,2},{8,12},{10,14},{12,8},{14,10},{1,5},{3,7},... | collective-permute-start | bytes 1032200 | tf_op jit(solution)/shard_map/ppermute | solution.py:290
  7.6 10.8 %copy-start.1 = (bf16[64,1792]{1,0:T(8,128)(2,1)S(1)}, bf16[64,1792]{1,0:T(8,128)(2,1)}, u32[]{:S(2)}) copy-start(bf16[64,1792]{1,0:T(8,128)(2,1)} %get-tuple-element.18) | copy-start | bytes 688132
  7.6 15.5 %collective-permute-start.4 = (bf16[64,1792]{1,0:T(8,128)(2,1)}, bf16[64,1792]{1,0:T(8,128)(2,1)S(1)}, u32[]{:S(2)}, u32[]{:S(2)}) collective-permute-start(bf16[64,1792]{1,0:T(8,128)(2,1)} %get-tuple-element.18), channel_id=1, source_target_pairs={{0,1},{1,0},{2,3},{3,2},{4,5},{5,4},{6,7},{7,6},{8,9},{9,8},{10,11... | collective-permute-start | bytes 688136 | tf_op jit(solution)/shard_map/ppermute | solution.py:291
  9.1 13.6 %collective-permute-start.5 = (bf16[64,1792]{1,0:T(8,128)(2,1)}, bf16[64,1792]{1,0:T(8,128)(2,1)S(1)}, u32[]{:S(2)}, u32[]{:S(2)}) collective-permute-start(bf16[64,1792]{1,0:T(8,128)(2,1)} %get-tuple-element.20), channel_id=1, source_target_pairs={{0,8},{2,10},{4,12},{6,14},{8,0},{10,2},{12,4},{14,6},{1,9},{3,11}... | collective-permute-start | bytes 688136 | tf_op jit(solution)/shard_map/ppermute | solution.py:290
  14.1 15.9 %collective-permute-start = (bf16[256,896]{1,0:T(8,128)(2,1)}, bf16[256,896]{1,0:T(8,128)(2,1)S(1)}, u32[]{:S(2)}, u32[]{:S(2)}) collective-permute-start(bf16[256,896]{1,0:T(8,128)(2,1)} %shard_map.55), channel_id=1, source_target_pairs={{0,4},{2,6},{4,0},{6,2},{8,12},{10,14},{12,8},{14,10},{1,5},{3,7},... | collective-permute-start | bytes 1376264 | tf_op jit(solution)/shard_map/ppermute | solution.py:290
  18.2 4.9 %collective-permute-start.3 = (bf16[192,896]{1,0:T(8,128)(2,1)S(1)}, bf16[192,896]{1,0:T(8,128)(2,1)S(1)}, u32[]{:S(2)}, u32[]{:S(2)}) collective-permute-start(bf16[192,896]{1,0:T(8,128)(2,1)S(1)} %collective-permute-done.2.z_ref), channel_id=1, source_target_pairs={{0,2},{2,0},{4,6},{6,4},{8,10},{10,8},{12,14},{14,12},{1,3},{3,1},... | collective-permute-start | bytes 1032200 | tf_op jit(solution)/shard_map/ppermute | solution.py:290
  18.4 6.4 %copy-start = (bf16[448,1792]{1,0:T(8,128)(2,1)S(1)}, bf16[448,1792]{1,0:T(8,128)(2,1)}, u32[]{:S(2)}) copy-start(bf16[448,1792]{1,0:T(8,128)(2,1)} %block_ref.3) | copy-start | bytes 4816900
  22.8 6.4 %collective-permute-start.6 = (bf16[64,1792]{1,0:T(8,128)(2,1)S(1)}, bf16[64,1792]{1,0:T(8,128)(2,1)S(1)}, u32[]{:S(2)}, u32[]{:S(2)}) collective-permute-start(bf16[64,1792]{1,0:T(8,128)(2,1)S(1)} %collective-permute-done.5), channel_id=1, source_target_pairs={{0,1},{1,0},{2,3},{3,2},{4,5},{5,4},{6,7},{7,6},{8,9},{9,8},{10,11... | collective-permute-start | bytes 688136 | tf_op jit(solution)/shard_map/ppermute | solution.py:291
  30.1 1.9 %collective-permute-start.7 = (bf16[256,896]{1,0:T(8,128)(2,1)S(1)}, bf16[256,896]{1,0:T(8,128)(2,1)S(1)}, u32[]{:S(2)}, u32[]{:S(2)}) collective-permute-start(bf16[256,896]{1,0:T(8,128)(2,1)S(1)} %collective-permute-done.z_ref), channel_id=1, source_target_pairs={{0,2},{2,0},{4,6},{6,4},{8,10},{10,8},{12,14},{14,12},{1,3},{3,1},... | collective-permute-start | bytes 1376264 | tf_op jit(solution)/shard_map/ppermute | solution.py:290
  33.9 21.1 %collective-permute-start.9 = (s16[58,16,128]{2,1,0:T(8,128)(2,1)S(1)}, s16[58,16,128]{2,1,0:T(8,128)(2,1)S(1)}, u32[]{:S(2)}, u32[]{:S(2)}) collective-permute-start(s16[58,16,128]{2,1,0:T(8,128)(2,1)S(1)} %get-tuple-element.27), channel_id=1, source_target_pairs={{0,9},{1,8},{2,11},{3,10},{4,13},{5,12},{6,15},{7,14},{8,1},{9,0},... | collective-permute-start | bytes 712712 | tf_op jit(solution)/shard_map/ppermute | solution.py:288
  37.2 20.6 %collective-permute-start.8 = (s16[57,16,128]{2,1,0:T(8,128)(2,1)S(1)}, s16[57,16,128]{2,1,0:T(8,128)(2,1)S(1)}, u32[]{:S(2)}, u32[]{:S(2)}) collective-permute-start(s16[57,16,128]{2,1,0:T(8,128)(2,1)S(1)} %shard_map.64._), channel_id=1, source_target_pairs={{0,8},{2,10},{4,12},{6,14},{8,0},{10,2},{12,4},{14,6},{1,9},{3,11}... | collective-permute-start | bytes 700424 | tf_op jit(solution)/shard_map/ppermute | solution.py:290
  38.0 8.6 %collective-permute-start.10 = (f32[32,1792]{1,0:T(8,128)S(1)}, f32[32,1792]{1,0:T(8,128)S(1)}, u32[]{:S(2)}, u32[]{:S(2)}) collective-permute-start(f32[32,1792]{1,0:T(8,128)S(1)} %get-tuple-element.28), channel_id=1, source_target_pairs={{0,1},{1,0},{2,3},{3,2},{4,5},{5,4},{6,7},{7,6},{8,9},{9,8},{10,11... | collective-permute-start | bytes 688136 | tf_op jit(solution)/shard_map/ppermute | solution.py:291
  39.5 15.4 %collective-permute-start.11 = (f32[32,1792]{1,0:T(8,128)S(1)}, f32[32,1792]{1,0:T(8,128)S(1)}, u32[]{:S(2)}, u32[]{:S(2)}) collective-permute-start(f32[32,1792]{1,0:T(8,128)S(1)} %get-tuple-element.29), channel_id=1, source_target_pairs={{0,1},{1,0},{2,3},{3,2},{4,5},{5,4},{6,7},{7,6},{8,9},{9,8},{10,11... | collective-permute-start | bytes 688136 | tf_op jit(solution)/shard_map/ppermute | solution.py:291

commit v6 on v4

--- a/solution.py
+++ b/solution.py
@@ -200,9 +200,15 @@
         out[n] = exps.astype(jnp.int16)
 
 
-def cross_kernel(tiles, first, place, y_ref, z_dense, rows, acc, coded, y_dense):
+def cross_kernel(tiles, first, place_ref, y_ref, z_dense, rows, acc, coded, y_dense, place, sems):
+    copies = fetch([(place_ref, place)], sems)
+    depth = z_dense.shape[0]
+    at = rows.shape[1] - 2 * depth
+    here = slice(rows.shape[0] - BLK, rows.shape[0])
+    total = acc[here] + dot(rows[here, at : at + depth], z_dense[...])
+    copies[0].wait()
     spread(place, y_ref, y_dense, (lax.axis_index("wide") ^ 3) * tiles + first)
-    encode(acc[...] + finish(rows[...], z_dense, y_dense), coded)
+    encode(total + dot(rows[here, at + depth :], y_dense[...]), coded)
 
 
 def finish(rows, z_dense, y_dense):
@@ -212,7 +218,7 @@
 
 
 def same_kernel(z_dense, y_dense, rows, acc, coded):
-    here = slice(2 * BLK, 3 * BLK)
+    here = slice(rows.shape[0] - BLK, rows.shape[0])
     encode(acc[here] + finish(rows[here], z_dense, y_dense), coded)
 
 
@@ -252,7 +258,7 @@
 
 
 def call(kernel, out, operands, places, scratch=(), room=32, **options):
-    specs = {"s": SMEM, "v": VMEM, "a": pl.BlockSpec(memory_space=pltpu.HBM)}
+    specs = {"s": SMEM, "v": VMEM, "a": pl.BlockSpec(memory_space=pl.ANY)}
     return pl.pallas_call(
         kernel,
         out_shape=out,
@@ -344,9 +350,9 @@
     rows = jnp.concatenate((own, own_cross, far_same), axis=0)
     acc = begin(rows)
     far_cross, acc = lax.optimization_barrier((far_cross, acc))
+    z_second, far_cross = lax.optimization_barrier((z_second, far_cross))
+    y_second = move(z_second, 1)
     cross_acc = begin(far_cross)
-    z_second, cross_acc = lax.optimization_barrier((z_second, cross_acc))
-    y_second = move(z_second, 1)
     z_dense = call(
         bind(second_kernel, tiles, head),
         sds((tail * BLK, width), bf16),
@@ -355,21 +361,22 @@
     )
     coded = BLK * width // (16 * LANES) + 1
     part = sds((BLK // 2, width), f32)
-    cross, y_dense = call(
+    same, y_dense = call(
         bind(cross_kernel, tiles, head),
         (sds((coded + 1, 16, LANES), i16), sds((tail * BLK, width), bf16)),
-        (place, y_second, z_dense, far_cross, cross_acc),
-        "svvvv",
+        (place, y_second, z_dense, rows, acc),
+        "avvvv",
+        [pltpu.SMEM(place.shape, i32), pltpu.SemaphoreType.DMA((1,))],
+    )
+    got_same = move(same, 4)
+    cross = call(
+        same_kernel, sds((coded, 16, LANES), i16), (z_dense, y_dense, far_cross, cross_acc), "vvvv"
     )
     got_cross = move(cross, 4, 1)
-    same = call(
-        same_kernel, sds((coded, 16, LANES), i16), (z_dense, y_dense, rows, acc), "vvvv"
-    )
-    got_same = move(same, 4)
     keep_rows, upper, lower = call(
         own_kernel,
         (sds((BLK, width), f32), part, part),
-        (z_dense, y_dense, rows, acc, same),
+        (z_dense, y_dense, rows, acc, cross),
         "vvvva",
     )
 
@@ -378,14 +385,14 @@
             bind(join_kernel, flip),
             sds((BLK, pair_count * width), f32),
             (coded, *bases),
-            "v" + ("vv" if flip else "av"),
+            "v" + ("avv" if flip else "v"),
             [pltpu.VMEM((BLK, width), f32), pltpu.SemaphoreType.DMA((BLK // 16,))],
             out_specs=pl.BlockSpec(memory_space=pltpu.HBM),
-            input_output_aliases={} if flip else {1: 0},
+            input_output_aliases={1: 0} if flip else {},
         )
 
-    half_done = join(1, got_cross, move(upper, 0, 1), move(lower, 0, 1))
-    return join(0, got_same, half_done, keep_rows)
+    half_done = join(0, got_same, keep_rows)
+    return join(1, got_cross, half_done, move(upper, 0, 1), move(lower, 0, 1))
 
 
 def solution(mesh):

time: 59 us -> 58.9 us (level)
  waiting for transfers between devices: 26.6 us -> 23.9 us
  starting transfers between devices: 13.3 us -> 15.9 us
    ppermute x4, waiting for transfers between devices: 16.5 us -> 1.85 us  [move(): lax.ppermute(x, 'pair', [(i, i ^ flip_pair) for i in range(pair_count)])]
    ppermute x7, waiting for transfers between devices: 10.1 us -> 17.7 us  [move(): lax.ppermute(x, 'wide', [(i, i ^ flip_wide) for i in range(wide_count)])]
    ppermute x1, waiting for transfers between devices: 0.01 us -> 4.39 us  [move(): return lax.ppermute(x, ('wide', 'pair'), [(i, i ^ flip) for i in range(n)])]
    ppermute x7, starting transfers between devices: 6.62 us -> 9.11 us  [move(): lax.ppermute(x, 'wide', [(i, i ^ flip_wide) for i in range(wide_count)])]
    ppermute x4, starting transfers between devices: 3.97 us -> 5.51 us  [move(): lax.ppermute(x, 'pair', [(i, i ^ flip_pair) for i in range(pair_count)])]
    ppermute x1, starting transfers between devices: 2.68 us -> 1.3 us  [move(): return lax.ppermute(x, ('wide', 'pair'), [(i, i ^ flip) for i in range(n)])]
  transfers between devices with their start and end apart: 12 -> 12, of which waited for: 7 -> 6; matrix products, arithmetic and copies ran while one was open for 1% -> 1% of each run, Pallas kernels for 26% -> 26%
where the time goes in v6:
time: 58.9 us; the launch traced here: 58.6 us
  waiting for transfers between devices  23.9 us (41%)
  Pallas kernels  18.2 us (31%)
  starting transfers between devices  15.9 us (27%)
    pallas_call x13, Pallas kernels, call(): pl.pallas_call(kernel, out_shape=out, in_specs=[specs[p] for p in places]...  18.2 us
    ppermute x7, waiting for transfers between devices, move(): lax.ppermute(x, 'wide', [(i, i ^ flip_wide) for i in range(wide_count)])  17.7 us
    ppermute x7, starting transfers between devices, move(): lax.ppermute(x, 'wide', [(i, i ^ flip_wide) for i in range(wide_count)])  9.11 us
    ppermute x4, starting transfers between devices, move(): lax.ppermute(x, 'pair', [(i, i ^ flip_pair) for i in range(pair_count)])  5.51 us
    ppermute x1, waiting for transfers between devices, move(): return lax.ppermute(x, ('wide', 'pair'), [(i, i ^ flip) for i in range(n)])  4.39 us
    ppermute x4, waiting for transfers between devices, move(): lax.ppermute(x, 'pair', [(i, i ^ flip_pair) for i in range(pair_count)])  1.85 us
    ppermute x1, starting transfers between devices, move(): return lax.ppermute(x, ('wide', 'pair'), [(i, i ^ flip) for i in range(n)])  1.3 us
  transfers between devices with their start and end apart: 12, of which 6 were waited for; matrix products, arithmetic and copies ran while one was open for 1% of the time, Pallas kernels for 26%

profile of v6, /device:TPU:0, one launch (start us, length us, event | category | flops | bytes accessed | tf_op | source)
XLA Modules:
  0.0 58.6 jit_solution(14245188197277379697)
XLA Ops:
  0.0 0.5 collective-permute-start.3
  0.5 2.2 %shard_map.58 = bf16[192,896]{1,0:T(8,128)(2,1)} custom-call(s32[14,2,56]{2,1,0:T(2,128)} %bitcast.4, bf16[448,1792]{1,0:T(8,128)(2,1)} %block_ref.3), custom_call_target="tpu_custom_call" | custom-call | flops 1 | bytes 1 | tf_op jit(solution)/shard_map/pallas_call | solution.py:262
  2.7 0.0 copy-start.2
  2.7 2.6 %collective-permute-start.4 = (bf16[192,896]{1,0:T(8,128)(2,1)}, bf16[192,896]{1,0:T(8,128)(2,1)S(1)}, u32[]{:S(2)}, u32[]{:S(2)}) collective-permute-start(bf16[192,896]{1,0:T(8,128)(2,1)} %shard_map.58), channel_id=1, source_target_pairs={{0,4},{2,6},{4,0},{6,2},{8,12},{10,14},{12,8},{14,10},{1,5},{3,7},... | collective-permute-start | bytes 1032200 | tf_op jit(solution)/shard_map/ppermute | solution.py:288
  5.3 2.2 %shard_map.56 = (bf16[64,1792]{1,0:T(8,128)(2,1)}, bf16[64,1792]{1,0:T(8,128)(2,1)}) custom-call(s32[16,28]{1,0:T(8,128)} %tile_ref.1, s32[16]{0:T(128)} %slab_ref.1, bf16[64,3584]{1,0:T(8,128)(2,1)} %amp_ref.1), custom_call_target="tpu_custom_call" | custom-call | flops 1 | bytes 1 | tf_op jit(solution)/shard_map/pallas_call | solution.py:262
  7.6 0.0 copy-start.1
  7.6 2.7 %collective-permute-start.1 = (bf16[64,1792]{1,0:T(8,128)(2,1)}, bf16[64,1792]{1,0:T(8,128)(2,1)S(1)}, u32[]{:S(2)}, u32[]{:S(2)}) collective-permute-start(bf16[64,1792]{1,0:T(8,128)(2,1)} %get-tuple-element.18), channel_id=1, source_target_pairs={{0,8},{2,10},{4,12},{6,14},{8,0},{10,2},{12,4},{14,6},{1,9},{3,11}... | collective-permute-start | bytes 688136 | tf_op jit(solution)/shard_map/ppermute | solution.py:288
  10.2 1.5 %collective-permute-start.6 = (bf16[64,1792]{1,0:T(8,128)(2,1)}, bf16[64,1792]{1,0:T(8,128)(2,1)S(1)}, u32[]{:S(2)}, u32[]{:S(2)}) collective-permute-start(bf16[64,1792]{1,0:T(8,128)(2,1)} %get-tuple-element.19), channel_id=1, source_target_pairs={{0,1},{1,0},{2,3},{3,2},{4,5},{5,4},{6,7},{7,6},{8,9},{9,8},{10,11... | collective-permute-start | bytes 688136 | tf_op jit(solution)/shard_map/ppermute | solution.py:289
  11.7 2.4 %shard_map.55 = bf16[256,896]{1,0:T(8,128)(2,1)} custom-call(s32[14,2,56]{2,1,0:T(2,128)} %bitcast.5, bf16[448,1792]{1,0:T(8,128)(2,1)} %block_ref.3), custom_call_target="tpu_custom_call" | custom-call | flops 1 | bytes 1 | tf_op jit(solution)/shard_map/pallas_call | solution.py:262
  14.1 0.5 collective-permute-start
  14.7 0.0 copy-done.2
  14.7 0.1 select_reduce_fusion
  14.8 4.6 %collective-permute-done.4.z_ref = bf16[192,896]{1,0:T(8,128)(2,1)S(1)} collective-permute-done((bf16[192,896]{1,0:T(8,128)(2,1)}, bf16[192,896]{1,0:T(8,128)(2,1)S(1)}, u32[]{:S(2)}, u32[]{:S(2)}) %collective-permute-start.4) | collective-permute-done | bytes 344096 | tf_op jit(solution)/shard_map/ppermute | solution.py:288
  19.4 0.0 collective-permute-start.5
  19.4 0.1 copy.10
  19.5 0.1 sub.7.place.place_ref
  19.6 0.0 copy-done.1
  19.6 0.0 copy-start
  19.6 0.0 collective-permute-done.1
  19.6 1.9 %collective-permute-start.2 = (bf16[64,1792]{1,0:T(8,128)(2,1)S(1)}, bf16[64,1792]{1,0:T(8,128)(2,1)S(1)}, u32[]{:S(2)}, u32[]{:S(2)}) collective-permute-start(bf16[64,1792]{1,0:T(8,128)(2,1)S(1)} %collective-permute-done.1), channel_id=1, source_target_pairs={{0,1},{1,0},{2,3},{3,2},{4,5},{5,4},{6,7},{7,6},{8,9},{9,8},{10,11... | collective-permute-start | bytes 688136 | tf_op jit(solution)/shard_map/ppermute | solution.py:289
  21.5 0.0 collective-permute-done.6
  21.5 0.0 collective-permute-done.5.rest_0_
  21.6 1.7 %shard_map.59.dense = bf16[384,1792]{1,0:T(8,128)(2,1)S(1)} custom-call(s32[1568]{0:T(1024)S(1)} %sub.7.place.place_ref, bf16[192,896]{1,0:T(8,128)(2,1)S(1)} %collective-permute-done.4.z_ref, bf16[192,896]{1,0:T(8,128)(2,1)S(1)} %collective-permute-done.5.rest_0_), custom_call_target="tpu_custom_call" | custom-call | flops 1 | bytes 1 | tf_op jit(solution)/shard_map/pallas_call | solution.py:262
  23.3 0.0 collective-permute-done.3.near_ref
  23.3 0.0 copy-done
  23.3 1.4 %shard_map.57.raw = bf16[896,1792]{1,0:T(8,128)(2,1)S(1)} custom-call(s32[1568]{0:T(1024)S(1)} %sub.7.place.place_ref, bf16[448,1792]{1,0:T(8,128)(2,1)S(1)} %copy-done, bf16[448,1792]{1,0:T(8,128)(2,1)S(1)} %collective-permute-done.3.near_ref), custom_call_target="tpu_custom_call" | custom-call | flops 1 | bytes 1 | tf_op jit(solution)/shard_map/pallas_call | solution.py:262
  24.7 1.2 %shard_map.60.acc = f32[192,1792]{1,0:T(8,128)S(1)} custom-call(bf16[896,1792]{1,0:T(8,128)(2,1)S(1)} %shard_map.57.raw, bf16[384,1792]{1,0:T(8,128)(2,1)S(1)} %shard_map.59.dense, bf16[192,1792]{1,0:T(8,128)(2,1)S(1)} %constant_dynamic-update-slice_fusion.rows), custom_call_target="tpu_custom_call" | custom-call | flops 1 | bytes 1 | tf_op jit(solution)/shard_map/pallas_call | solution.py:262
  26.0 1.8 %collective-permute-done.2.rows = bf16[64,1792]{1,0:T(8,128)(2,1)S(1)} collective-permute-done((bf16[64,1792]{1,0:T(8,128)(2,1)S(1)}, bf16[64,1792]{1,0:T(8,128)(2,1)S(1)}, u32[]{:S(2)}, u32[]{:S(2)}) %collective-permute-start.2) | collective-permute-done | bytes 229408 | tf_op jit(solution)/shard_map/ppermute | solution.py:289
  27.8 1.2 %collective-permute-done.z_ref = bf16[256,896]{1,0:T(8,128)(2,1)S(1)} collective-permute-done((bf16[256,896]{1,0:T(8,128)(2,1)}, bf16[256,896]{1,0:T(8,128)(2,1)S(1)}, u32[]{:S(2)}, u32[]{:S(2)}) %collective-permute-start) | collective-permute-done | bytes 458784 | tf_op jit(solution)/shard_map/ppermute | solution.py:288
  29.0 0.0 collective-permute-start.7
  29.0 1.4 %shard_map.61.z_dense = bf16[256,1792]{1,0:T(8,128)(2,1)S(1)} custom-call(s32[1568]{0:T(1024)S(1)} %sub.7.place.place_ref, bf16[256,896]{1,0:T(8,128)(2,1)S(1)} %collective-permute-done.z_ref), custom_call_target="tpu_custom_call" | custom-call | flops 1 | bytes 1 | tf_op jit(solution)/shard_map/pallas_call | solution.py:262
  30.4 0.4 collective-permute-done.7.y_ref
  30.8 1.9 %shard_map.62 = (s16[58,16,128]{2,1,0:T(8,128)(2,1)S(1)}, bf16[256,1792]{1,0:T(8,128)(2,1)S(1)}) custom-call(s32[1568]{0:T(1024)S(1)} %sub.7.place.place_ref, bf16[256,896]{1,0:T(8,128)(2,1)S(1)} %collective-permute-done.7.y_ref, bf16[256,1792]{1,0:T(8,128)(2,1)S(1)} %shard_map.61.z_dense, bf16[192,1792]{1,0:T(8,128)(2,1)S(1)} %constant_dynamic-update-slice_fusion.rows, ...), custom_call_target="tpu_custom_call" | custom-call | flops 1 | bytes 1 | tf_op jit(solution)/shard_map/pallas_call | solution.py:262
  32.8 2.8 %collective-permute-start.9 = (s16[58,16,128]{2,1,0:T(8,128)(2,1)S(1)}, s16[58,16,128]{2,1,0:T(8,128)(2,1)S(1)}, u32[]{:S(2)}, u32[]{:S(2)}) collective-permute-start(s16[58,16,128]{2,1,0:T(8,128)(2,1)S(1)} %get-tuple-element.27), channel_id=1, source_target_pairs={{0,8},{2,10},{4,12},{6,14},{8,0},{10,2},{12,4},{14,6},{1,9},{3,11}... | collective-permute-start | bytes 712712 | tf_op jit(solution)/shard_map/ppermute | solution.py:288
  35.6 0.9 %shard_map.63.acc = f32[64,1792]{1,0:T(8,128)S(1)} custom-call(bf16[896,1792]{1,0:T(8,128)(2,1)S(1)} %shard_map.57.raw, bf16[384,1792]{1,0:T(8,128)(2,1)S(1)} %shard_map.59.dense, bf16[64,1792]{1,0:T(8,128)(2,1)S(1)} %collective-permute-done.2.rows), custom_call_target="tpu_custom_call" | custom-call | flops 1 | bytes 1 | tf_op jit(solution)/shard_map/pallas_call | solution.py:262
  36.5 0.6 %shard_map.64._ = s16[57,16,128]{2,1,0:T(8,128)(2,1)S(1)} custom-call(bf16[256,1792]{1,0:T(8,128)(2,1)S(1)} %shard_map.61.z_dense, bf16[256,1792]{1,0:T(8,128)(2,1)S(1)} %get-tuple-element.25.y_dense, bf16[64,1792]{1,0:T(8,128)(2,1)S(1)} %collective-permute-done.2.rows, f32[64,1792]{1,0:T(8,128)S(1)} %shard_map.63.acc), custom_call_target="tpu_custom_call" | custom-call | flops 1 | bytes 1 | tf_op jit(solution)/shard_map/pallas_call | solution.py:262
  37.1 1.3 %collective-permute-start.8 = (s16[57,16,128]{2,1,0:T(8,128)(2,1)S(1)}, s16[57,16,128]{2,1,0:T(8,128)(2,1)S(1)}, u32[]{:S(2)}, u32[]{:S(2)}) collective-permute-start(s16[57,16,128]{2,1,0:T(8,128)(2,1)S(1)} %shard_map.64._), channel_id=1, source_target_pairs={{0,9},{1,8},{2,11},{3,10},{4,13},{5,12},{6,15},{7,14},{8,1},{9,0},... | collective-permute-start | bytes 700424 | tf_op jit(solution)/shard_map/ppermute | solution.py:286
  38.4 0.4 shard_map.65
  38.8 0.5 collective-permute-start.10
  39.3 1.6 %collective-permute-start.11 = (f32[32,1792]{1,0:T(8,128)S(1)}, f32[32,1792]{1,0:T(8,128)S(1)}, u32[]{:S(2)}, u32[]{:S(2)}) collective-permute-start(f32[32,1792]{1,0:T(8,128)S(1)} %get-tuple-element.30), channel_id=1, source_target_pairs={{0,1},{1,0},{2,3},{3,2},{4,5},{5,4},{6,7},{7,6},{8,9},{9,8},{10,11... | collective-permute-start | bytes 688136 | tf_op jit(solution)/shard_map/ppermute | solution.py:289
  40.9 11.5 %collective-permute-done.9.coded = s16[58,16,128]{2,1,0:T(8,128)(2,1)S(1)} collective-permute-done((s16[58,16,128]{2,1,0:T(8,128)(2,1)S(1)}, s16[58,16,128]{2,1,0:T(8,128)(2,1)S(1)}, u32[]{:S(2)}, u32[]{:S(2)}) %collective-permute-start.9) | collective-permute-done | bytes 237600 | tf_op jit(solution)/shard_map/ppermute | solution.py:288
  52.4 0.9 %shard_map.66.rest_0_ = f32[64,3584]{1,0:T(8,128)} custom-call(s16[58,16,128]{2,1,0:T(8,128)(2,1)S(1)} %collective-permute-done.9.coded, f32[64,1792]{1,0:T(8,128)S(1)} %get-tuple-element.28.rest_0_), custom_call_target="tpu_custom_call" | custom-call | flops 1 | bytes 1 | tf_op jit(solution)/shard_map/pallas_call | solution.py:262
  53.3 0.0 collective-permute-done.10.rest_1_
  53.3 0.0 collective-permute-done.11.rest_2_
  53.4 4.4 %collective-permute-done.8.coded = s16[57,16,128]{2,1,0:T(8,128)(2,1)S(1)} collective-permute-done((s16[57,16,128]{2,1,0:T(8,128)(2,1)S(1)}, s16[57,16,128]{2,1,0:T(8,128)(2,1)S(1)}, u32[]{:S(2)}, u32[]{:S(2)}) %collective-permute-start.8) | collective-permute-done | bytes 233504 | tf_op jit(solution)/shard_map/ppermute | solution.py:286
  57.7 0.9 %shard_map.67 = f32[64,3584]{1,0:T(8,128)} custom-call(s16[57,16,128]{2,1,0:T(8,128)(2,1)S(1)} %collective-permute-done.8.coded, f32[64,3584]{1,0:T(8,128)} %shard_map.66.rest_0_, f32[32,1792]{1,0:T(8,128)S(1)} %collective-permute-done.10.rest_1_, f32[32,1792]{1,0:T(8,128)S(1)} %collective-permute-done.11.rest_2_), custom_call_target="tpu_custom_call", output_to_operand_aliasing={{}: (1, {})} | custom-call | flops 1 | bytes 1 | tf_op jit(solution)/shard_map/pallas_call | solution.py:262
  (7 shorter events, 0.1 us)
Async XLA Ops:
  0.0 23.3 %collective-permute-start.3 = (bf16[448,1792]{1,0:T(8,128)(2,1)}, bf16[448,1792]{1,0:T(8,128)(2,1)S(1)}, u32[]{:S(2)}, u32[]{:S(2)}) collective-permute-start(bf16[448,1792]{1,0:T(8,128)(2,1)} %block_ref.3), channel_id=1, source_target_pairs={{0,2},{2,0},{4,6},{6,4},{8,10},{10,8},{12,14},{14,12},{1,3},{3,1},... | collective-permute-start | bytes 4816904 | tf_op jit(solution)/shard_map/ppermute | solution.py:288
  2.7 12.0 %copy-start.2 = (s32[56,2,14]{0,1,2:T(2,128)S(1)}, s32[56,2,14]{0,1,2:T(2,128)}, u32[]{:S(2)}) copy-start(s32[56,2,14]{0,1,2:T(2,128)} %param.9) | copy-start | bytes 18820
  2.7 16.7 %collective-permute-start.4 = (bf16[192,896]{1,0:T(8,128)(2,1)}, bf16[192,896]{1,0:T(8,128)(2,1)S(1)}, u32[]{:S(2)}, u32[]{:S(2)}) collective-permute-start(bf16[192,896]{1,0:T(8,128)(2,1)} %shard_map.58), channel_id=1, source_target_pairs={{0,4},{2,6},{4,0},{6,2},{8,12},{10,14},{12,8},{14,10},{1,5},{3,7},... | collective-permute-start | bytes 1032200 | tf_op jit(solution)/shard_map/ppermute | solution.py:288
  7.6 12.0 %copy-start.1 = (bf16[64,1792]{1,0:T(8,128)(2,1)S(1)}, bf16[64,1792]{1,0:T(8,128)(2,1)}, u32[]{:S(2)}) copy-start(bf16[64,1792]{1,0:T(8,128)(2,1)} %get-tuple-element.19) | copy-start | bytes 688132
  7.6 12.0 %collective-permute-start.1 = (bf16[64,1792]{1,0:T(8,128)(2,1)}, bf16[64,1792]{1,0:T(8,128)(2,1)S(1)}, u32[]{:S(2)}, u32[]{:S(2)}) collective-permute-start(bf16[64,1792]{1,0:T(8,128)(2,1)} %get-tuple-element.18), channel_id=1, source_target_pairs={{0,8},{2,10},{4,12},{6,14},{8,0},{10,2},{12,4},{14,6},{1,9},{3,11}... | collective-permute-start | bytes 688136 | tf_op jit(solution)/shard_map/ppermute | solution.py:288
  10.2 11.3 %collective-permute-start.6 = (bf16[64,1792]{1,0:T(8,128)(2,1)}, bf16[64,1792]{1,0:T(8,128)(2,1)S(1)}, u32[]{:S(2)}, u32[]{:S(2)}) collective-permute-start(bf16[64,1792]{1,0:T(8,128)(2,1)} %get-tuple-element.19), channel_id=1, source_target_pairs={{0,1},{1,0},{2,3},{3,2},{4,5},{5,4},{6,7},{7,6},{8,9},{9,8},{10,11... | collective-permute-start | bytes 688136 | tf_op jit(solution)/shard_map/ppermute | solution.py:289
  14.1 14.9 %collective-permute-start = (bf16[256,896]{1,0:T(8,128)(2,1)}, bf16[256,896]{1,0:T(8,128)(2,1)S(1)}, u32[]{:S(2)}, u32[]{:S(2)}) collective-permute-start(bf16[256,896]{1,0:T(8,128)(2,1)} %shard_map.55), channel_id=1, source_target_pairs={{0,4},{2,6},{4,0},{6,2},{8,12},{10,14},{12,8},{14,10},{1,5},{3,7},... | collective-permute-start | bytes 1376264 | tf_op jit(solution)/shard_map/ppermute | solution.py:288
  19.4 2.2 %collective-permute-start.5 = (bf16[192,896]{1,0:T(8,128)(2,1)S(1)}, bf16[192,896]{1,0:T(8,128)(2,1)S(1)}, u32[]{:S(2)}, u32[]{:S(2)}) collective-permute-start(bf16[192,896]{1,0:T(8,128)(2,1)S(1)} %collective-permute-done.4.z_ref), channel_id=1, source_target_pairs={{0,2},{2,0},{4,6},{6,4},{8,10},{10,8},{12,14},{14,12},{1,3},{3,1},... | collective-permute-start | bytes 1032200 | tf_op jit(solution)/shard_map/ppermute | solution.py:288
  19.6 3.7 %copy-start = (bf16[448,1792]{1,0:T(8,128)(2,1)S(1)}, bf16[448,1792]{1,0:T(8,128)(2,1)}, u32[]{:S(2)}) copy-start(bf16[448,1792]{1,0:T(8,128)(2,1)} %block_ref.3) | copy-start | bytes 4816900
  19.6 8.2 %collective-permute-start.2 = (bf16[64,1792]{1,0:T(8,128)(2,1)S(1)}, bf16[64,1792]{1,0:T(8,128)(2,1)S(1)}, u32[]{:S(2)}, u32[]{:S(2)}) collective-permute-start(bf16[64,1792]{1,0:T(8,128)(2,1)S(1)} %collective-permute-done.1), channel_id=1, source_target_pairs={{0,1},{1,0},{2,3},{3,2},{4,5},{5,4},{6,7},{7,6},{8,9},{9,8},{10,11... | collective-permute-start | bytes 688136 | tf_op jit(solution)/shard_map/ppermute | solution.py:289
  29.0 1.8 %collective-permute-start.7 = (bf16[256,896]{1,0:T(8,128)(2,1)S(1)}, bf16[256,896]{1,0:T(8,128)(2,1)S(1)}, u32[]{:S(2)}, u32[]{:S(2)}) collective-permute-start(bf16[256,896]{1,0:T(8,128)(2,1)S(1)} %collective-permute-done.z_ref), channel_id=1, source_target_pairs={{0,2},{2,0},{4,6},{6,4},{8,10},{10,8},{12,14},{14,12},{1,3},{3,1},... | collective-permute-start | bytes 1376264 | tf_op jit(solution)/shard_map/ppermute | solution.py:288
  32.8 19.7 %collective-permute-start.9 = (s16[58,16,128]{2,1,0:T(8,128)(2,1)S(1)}, s16[58,16,128]{2,1,0:T(8,128)(2,1)S(1)}, u32[]{:S(2)}, u32[]{:S(2)}) collective-permute-start(s16[58,16,128]{2,1,0:T(8,128)(2,1)S(1)} %get-tuple-element.27), channel_id=1, source_target_pairs={{0,8},{2,10},{4,12},{6,14},{8,0},{10,2},{12,4},{14,6},{1,9},{3,11}... | collective-permute-start | bytes 712712 | tf_op jit(solution)/shard_map/ppermute | solution.py:288
  37.1 20.6 %collective-permute-start.8 = (s16[57,16,128]{2,1,0:T(8,128)(2,1)S(1)}, s16[57,16,128]{2,1,0:T(8,128)(2,1)S(1)}, u32[]{:S(2)}, u32[]{:S(2)}) collective-permute-start(s16[57,16,128]{2,1,0:T(8,128)(2,1)S(1)} %shard_map.64._), channel_id=1, source_target_pairs={{0,9},{1,8},{2,11},{3,10},{4,13},{5,12},{6,15},{7,14},{8,1},{9,0},... | collective-permute-start | bytes 700424 | tf_op jit(solution)/shard_map/ppermute | solution.py:286
  38.8 14.5 %collective-permute-start.10 = (f32[32,1792]{1,0:T(8,128)S(1)}, f32[32,1792]{1,0:T(8,128)S(1)}, u32[]{:S(2)}, u32[]{:S(2)}) collective-permute-start(f32[32,1792]{1,0:T(8,128)S(1)} %get-tuple-element.29), channel_id=1, source_target_pairs={{0,1},{1,0},{2,3},{3,2},{4,5},{5,4},{6,7},{7,6},{8,9},{9,8},{10,11... | collective-permute-start | bytes 688136 | tf_op jit(solution)/shard_map/ppermute | solution.py:289
  39.3 14.1 %collective-permute-start.11 = (f32[32,1792]{1,0:T(8,128)S(1)}, f32[32,1792]{1,0:T(8,128)S(1)}, u32[]{:S(2)}, u32[]{:S(2)}) collective-permute-start(f32[32,1792]{1,0:T(8,128)S(1)} %get-tuple-element.30), channel_id=1, source_target_pairs={{0,1},{1,0},{2,3},{3,2},{4,5},{5,4},{6,7},{7,6},{8,9},{9,8},{10,11... | collective-permute-start | bytes 688136 | tf_op jit(solution)/shard_map/ppermute | solution.py:289

commit v7 on v6

--- a/solution.py
+++ b/solution.py
@@ -363,7 +363,7 @@
     part = sds((BLK // 2, width), f32)
     same, y_dense = call(
         bind(cross_kernel, tiles, head),
-        (sds((coded + 1, 16, LANES), i16), sds((tail * BLK, width), bf16)),
+        (sds((coded, 16, LANES), i16), sds((tail * BLK, width), bf16)),
         (place, y_second, z_dense, rows, acc),
         "avvvv",
         [pltpu.SMEM(place.shape, i32), pltpu.SemaphoreType.DMA((1,))],

time: 58.9 us -> 58.7 us (level)
  no operation moved by 1% of the time
where the time goes in v7:
time: 58.7 us; the launch traced here: 58.5 us
  waiting for transfers between devices  23.7 us (40%)
  Pallas kernels  18.2 us (31%)
  starting transfers between devices  15.9 us (27%)
    pallas_call x13, Pallas kernels, call(): pl.pallas_call(kernel, out_shape=out, in_specs=[specs[p] for p in places]...  18.2 us
    ppermute x7, waiting for transfers between devices, move(): lax.ppermute(x, 'wide', [(i, i ^ flip_wide) for i in range(wide_count)])  17.5 us
    ppermute x7, starting transfers between devices, move(): lax.ppermute(x, 'wide', [(i, i ^ flip_wide) for i in range(wide_count)])  9.11 us
    ppermute x4, starting transfers between devices, move(): lax.ppermute(x, 'pair', [(i, i ^ flip_pair) for i in range(pair_count)])  5.51 us
    ppermute x1, waiting for transfers between devices, move(): return lax.ppermute(x, ('wide', 'pair'), [(i, i ^ flip) for i in range(n)])  4.39 us
    ppermute x4, waiting for transfers between devices, move(): lax.ppermute(x, 'pair', [(i, i ^ flip_pair) for i in range(pair_count)])  1.83 us
    ppermute x1, starting transfers between devices, move(): return lax.ppermute(x, ('wide', 'pair'), [(i, i ^ flip) for i in range(n)])  1.31 us
  transfers between devices with their start and end apart: 12, of which 6 were waited for; matrix products, arithmetic and copies ran while one was open for 1% of the time, Pallas kernels for 26%

profile of v7, /device:TPU:0, one launch (start us, length us, event | category | flops | bytes accessed | tf_op | source)
XLA Modules:
  0.0 58.5 jit_solution(14171469720639534936)
XLA Ops:
  0.0 0.5 collective-permute-start.3
  0.5 2.2 %shard_map.58 = bf16[192,896]{1,0:T(8,128)(2,1)} custom-call(s32[14,2,56]{2,1,0:T(2,128)} %bitcast.4, bf16[448,1792]{1,0:T(8,128)(2,1)} %block_ref.3), custom_call_target="tpu_custom_call" | custom-call | flops 1 | bytes 1 | tf_op jit(solution)/shard_map/pallas_call | solution.py:262
  2.7 0.0 copy-start.2
  2.7 2.6 %collective-permute-start.4 = (bf16[192,896]{1,0:T(8,128)(2,1)}, bf16[192,896]{1,0:T(8,128)(2,1)S(1)}, u32[]{:S(2)}, u32[]{:S(2)}) collective-permute-start(bf16[192,896]{1,0:T(8,128)(2,1)} %shard_map.58), channel_id=1, source_target_pairs={{0,4},{2,6},{4,0},{6,2},{8,12},{10,14},{12,8},{14,10},{1,5},{3,7},... | collective-permute-start | bytes 1032200 | tf_op jit(solution)/shard_map/ppermute | solution.py:288
  5.3 2.2 %shard_map.56 = (bf16[64,1792]{1,0:T(8,128)(2,1)}, bf16[64,1792]{1,0:T(8,128)(2,1)}) custom-call(s32[16,28]{1,0:T(8,128)} %tile_ref.1, s32[16]{0:T(128)} %slab_ref.1, bf16[64,3584]{1,0:T(8,128)(2,1)} %amp_ref.1), custom_call_target="tpu_custom_call" | custom-call | flops 1 | bytes 1 | tf_op jit(solution)/shard_map/pallas_call | solution.py:262
  7.6 0.0 copy-start.1
  7.6 2.7 %collective-permute-start.1 = (bf16[64,1792]{1,0:T(8,128)(2,1)}, bf16[64,1792]{1,0:T(8,128)(2,1)S(1)}, u32[]{:S(2)}, u32[]{:S(2)}) collective-permute-start(bf16[64,1792]{1,0:T(8,128)(2,1)} %get-tuple-element.18), channel_id=1, source_target_pairs={{0,8},{2,10},{4,12},{6,14},{8,0},{10,2},{12,4},{14,6},{1,9},{3,11}... | collective-permute-start | bytes 688136 | tf_op jit(solution)/shard_map/ppermute | solution.py:288
  10.2 1.5 %collective-permute-start.6 = (bf16[64,1792]{1,0:T(8,128)(2,1)}, bf16[64,1792]{1,0:T(8,128)(2,1)S(1)}, u32[]{:S(2)}, u32[]{:S(2)}) collective-permute-start(bf16[64,1792]{1,0:T(8,128)(2,1)} %get-tuple-element.19), channel_id=1, source_target_pairs={{0,1},{1,0},{2,3},{3,2},{4,5},{5,4},{6,7},{7,6},{8,9},{9,8},{10,11... | collective-permute-start | bytes 688136 | tf_op jit(solution)/shard_map/ppermute | solution.py:289
  11.7 2.4 %shard_map.55 = bf16[256,896]{1,0:T(8,128)(2,1)} custom-call(s32[14,2,56]{2,1,0:T(2,128)} %bitcast.5, bf16[448,1792]{1,0:T(8,128)(2,1)} %block_ref.3), custom_call_target="tpu_custom_call" | custom-call | flops 1 | bytes 1 | tf_op jit(solution)/shard_map/pallas_call | solution.py:262
  14.1 0.5 collective-permute-start
  14.7 0.0 copy-done.2
  14.7 0.1 select_reduce_fusion
  14.8 4.6 %collective-permute-done.4.z_ref = bf16[192,896]{1,0:T(8,128)(2,1)S(1)} collective-permute-done((bf16[192,896]{1,0:T(8,128)(2,1)}, bf16[192,896]{1,0:T(8,128)(2,1)S(1)}, u32[]{:S(2)}, u32[]{:S(2)}) %collective-permute-start.4) | collective-permute-done | bytes 344096 | tf_op jit(solution)/shard_map/ppermute | solution.py:288
  19.4 0.0 collective-permute-start.5
  19.4 0.1 copy.10
  19.5 0.1 sub.7.place.place_ref
  19.6 0.0 copy-done.1
  19.6 0.0 copy-start
  19.6 0.0 collective-permute-done.1
  19.6 1.9 %collective-permute-start.2 = (bf16[64,1792]{1,0:T(8,128)(2,1)S(1)}, bf16[64,1792]{1,0:T(8,128)(2,1)S(1)}, u32[]{:S(2)}, u32[]{:S(2)}) collective-permute-start(bf16[64,1792]{1,0:T(8,128)(2,1)S(1)} %collective-permute-done.1), channel_id=1, source_target_pairs={{0,1},{1,0},{2,3},{3,2},{4,5},{5,4},{6,7},{7,6},{8,9},{9,8},{10,11... | collective-permute-start | bytes 688136 | tf_op jit(solution)/shard_map/ppermute | solution.py:289
  21.5 0.0 collective-permute-done.6
  21.5 0.0 collective-permute-done.5.rest_0_
  21.6 1.7 %shard_map.59.dense = bf16[384,1792]{1,0:T(8,128)(2,1)S(1)} custom-call(s32[1568]{0:T(1024)S(1)} %sub.7.place.place_ref, bf16[192,896]{1,0:T(8,128)(2,1)S(1)} %collective-permute-done.4.z_ref, bf16[192,896]{1,0:T(8,128)(2,1)S(1)} %collective-permute-done.5.rest_0_), custom_call_target="tpu_custom_call" | custom-call | flops 1 | bytes 1 | tf_op jit(solution)/shard_map/pallas_call | solution.py:262
  23.3 0.0 collective-permute-done.3.near_ref
  23.3 0.0 copy-done
  23.3 1.4 %shard_map.57.raw = bf16[896,1792]{1,0:T(8,128)(2,1)S(1)} custom-call(s32[1568]{0:T(1024)S(1)} %sub.7.place.place_ref, bf16[448,1792]{1,0:T(8,128)(2,1)S(1)} %copy-done, bf16[448,1792]{1,0:T(8,128)(2,1)S(1)} %collective-permute-done.3.near_ref), custom_call_target="tpu_custom_call" | custom-call | flops 1 | bytes 1 | tf_op jit(solution)/shard_map/pallas_call | solution.py:262
  24.7 1.2 %shard_map.60.acc = f32[192,1792]{1,0:T(8,128)S(1)} custom-call(bf16[896,1792]{1,0:T(8,128)(2,1)S(1)} %shard_map.57.raw, bf16[384,1792]{1,0:T(8,128)(2,1)S(1)} %shard_map.59.dense, bf16[192,1792]{1,0:T(8,128)(2,1)S(1)} %constant_dynamic-update-slice_fusion.rows), custom_call_target="tpu_custom_call" | custom-call | flops 1 | bytes 1 | tf_op jit(solution)/shard_map/pallas_call | solution.py:262
  26.0 1.8 %collective-permute-done.2.rows = bf16[64,1792]{1,0:T(8,128)(2,1)S(1)} collective-permute-done((bf16[64,1792]{1,0:T(8,128)(2,1)S(1)}, bf16[64,1792]{1,0:T(8,128)(2,1)S(1)}, u32[]{:S(2)}, u32[]{:S(2)}) %collective-permute-start.2) | collective-permute-done | bytes 229408 | tf_op jit(solution)/shard_map/ppermute | solution.py:289
  27.8 1.2 %collective-permute-done.z_ref = bf16[256,896]{1,0:T(8,128)(2,1)S(1)} collective-permute-done((bf16[256,896]{1,0:T(8,128)(2,1)}, bf16[256,896]{1,0:T(8,128)(2,1)S(1)}, u32[]{:S(2)}, u32[]{:S(2)}) %collective-permute-start) | collective-permute-done | bytes 458784 | tf_op jit(solution)/shard_map/ppermute | solution.py:288
  29.0 0.0 collective-permute-start.7
  29.0 1.4 %shard_map.61.z_dense = bf16[256,1792]{1,0:T(8,128)(2,1)S(1)} custom-call(s32[1568]{0:T(1024)S(1)} %sub.7.place.place_ref, bf16[256,896]{1,0:T(8,128)(2,1)S(1)} %collective-permute-done.z_ref), custom_call_target="tpu_custom_call" | custom-call | flops 1 | bytes 1 | tf_op jit(solution)/shard_map/pallas_call | solution.py:262
  30.4 0.4 collective-permute-done.7.y_ref
  30.8 1.9 %shard_map.62 = (s16[57,16,128]{2,1,0:T(8,128)(2,1)S(1)}, bf16[256,1792]{1,0:T(8,128)(2,1)S(1)}) custom-call(s32[1568]{0:T(1024)S(1)} %sub.7.place.place_ref, bf16[256,896]{1,0:T(8,128)(2,1)S(1)} %collective-permute-done.7.y_ref, bf16[256,1792]{1,0:T(8,128)(2,1)S(1)} %shard_map.61.z_dense, bf16[192,1792]{1,0:T(8,128)(2,1)S(1)} %constant_dynamic-update-slice_fusion.rows, ...), custom_call_target="tpu_custom_call" | custom-call | flops 1 | bytes 1 | tf_op jit(solution)/shard_map/pallas_call | solution.py:262
  32.8 2.8 %collective-permute-start.9 = (s16[57,16,128]{2,1,0:T(8,128)(2,1)S(1)}, s16[57,16,128]{2,1,0:T(8,128)(2,1)S(1)}, u32[]{:S(2)}, u32[]{:S(2)}) collective-permute-start(s16[57,16,128]{2,1,0:T(8,128)(2,1)S(1)} %get-tuple-element.27), channel_id=1, source_target_pairs={{0,8},{2,10},{4,12},{6,14},{8,0},{10,2},{12,4},{14,6},{1,9},{3,11}... | collective-permute-start | bytes 700424 | tf_op jit(solution)/shard_map/ppermute | solution.py:288
  35.6 0.9 %shard_map.63.acc = f32[64,1792]{1,0:T(8,128)S(1)} custom-call(bf16[896,1792]{1,0:T(8,128)(2,1)S(1)} %shard_map.57.raw, bf16[384,1792]{1,0:T(8,128)(2,1)S(1)} %shard_map.59.dense, bf16[64,1792]{1,0:T(8,128)(2,1)S(1)} %collective-permute-done.2.rows), custom_call_target="tpu_custom_call" | custom-call | flops 1 | bytes 1 | tf_op jit(solution)/shard_map/pallas_call | solution.py:262
  36.5 0.6 %shard_map.64._ = s16[57,16,128]{2,1,0:T(8,128)(2,1)S(1)} custom-call(bf16[256,1792]{1,0:T(8,128)(2,1)S(1)} %shard_map.61.z_dense, bf16[256,1792]{1,0:T(8,128)(2,1)S(1)} %get-tuple-element.25.y_dense, bf16[64,1792]{1,0:T(8,128)(2,1)S(1)} %collective-permute-done.2.rows, f32[64,1792]{1,0:T(8,128)S(1)} %shard_map.63.acc), custom_call_target="tpu_custom_call" | custom-call | flops 1 | bytes 1 | tf_op jit(solution)/shard_map/pallas_call | solution.py:262
  37.1 1.3 %collective-permute-start.8 = (s16[57,16,128]{2,1,0:T(8,128)(2,1)S(1)}, s16[57,16,128]{2,1,0:T(8,128)(2,1)S(1)}, u32[]{:S(2)}, u32[]{:S(2)}) collective-permute-start(s16[57,16,128]{2,1,0:T(8,128)(2,1)S(1)} %shard_map.64._), channel_id=1, source_target_pairs={{0,9},{1,8},{2,11},{3,10},{4,13},{5,12},{6,15},{7,14},{8,1},{9,0},... | collective-permute-start | bytes 700424 | tf_op jit(solution)/shard_map/ppermute | solution.py:286
  38.4 0.4 shard_map.65
  38.9 0.4 collective-permute-start.10
  39.3 1.7 %collective-permute-start.11 = (f32[32,1792]{1,0:T(8,128)S(1)}, f32[32,1792]{1,0:T(8,128)S(1)}, u32[]{:S(2)}, u32[]{:S(2)}) collective-permute-start(f32[32,1792]{1,0:T(8,128)S(1)} %get-tuple-element.30), channel_id=1, source_target_pairs={{0,1},{1,0},{2,3},{3,2},{4,5},{5,4},{6,7},{7,6},{8,9},{9,8},{10,11... | collective-permute-start | bytes 688136 | tf_op jit(solution)/shard_map/ppermute | solution.py:289
  41.0 11.3 %collective-permute-done.9.coded = s16[57,16,128]{2,1,0:T(8,128)(2,1)S(1)} collective-permute-done((s16[57,16,128]{2,1,0:T(8,128)(2,1)S(1)}, s16[57,16,128]{2,1,0:T(8,128)(2,1)S(1)}, u32[]{:S(2)}, u32[]{:S(2)}) %collective-permute-start.9) | collective-permute-done | bytes 233504 | tf_op jit(solution)/shard_map/ppermute | solution.py:288
  52.3 0.9 %shard_map.66.rest_0_ = f32[64,3584]{1,0:T(8,128)} custom-call(s16[57,16,128]{2,1,0:T(8,128)(2,1)S(1)} %collective-permute-done.9.coded, f32[64,1792]{1,0:T(8,128)S(1)} %get-tuple-element.28.rest_0_), custom_call_target="tpu_custom_call" | custom-call | flops 1 | bytes 1 | tf_op jit(solution)/shard_map/pallas_call | solution.py:262
  53.2 0.0 collective-permute-done.10.rest_1_
  53.2 0.0 collective-permute-done.11.rest_2_
  53.2 4.4 %collective-permute-done.8.coded = s16[57,16,128]{2,1,0:T(8,128)(2,1)S(1)} collective-permute-done((s16[57,16,128]{2,1,0:T(8,128)(2,1)S(1)}, s16[57,16,128]{2,1,0:T(8,128)(2,1)S(1)}, u32[]{:S(2)}, u32[]{:S(2)}) %collective-permute-start.8) | collective-permute-done | bytes 233504 | tf_op jit(solution)/shard_map/ppermute | solution.py:286
  57.6 0.9 %shard_map.67 = f32[64,3584]{1,0:T(8,128)} custom-call(s16[57,16,128]{2,1,0:T(8,128)(2,1)S(1)} %collective-permute-done.8.coded, f32[64,3584]{1,0:T(8,128)} %shard_map.66.rest_0_, f32[32,1792]{1,0:T(8,128)S(1)} %collective-permute-done.10.rest_1_, f32[32,1792]{1,0:T(8,128)S(1)} %collective-permute-done.11.rest_2_), custom_call_target="tpu_custom_call", output_to_operand_aliasing={{}: (1, {})} | custom-call | flops 1 | bytes 1 | tf_op jit(solution)/shard_map/pallas_call | solution.py:262
  (7 shorter events, 0.1 us)
Async XLA Ops:
  0.0 23.3 %collective-permute-start.3 = (bf16[448,1792]{1,0:T(8,128)(2,1)}, bf16[448,1792]{1,0:T(8,128)(2,1)S(1)}, u32[]{:S(2)}, u32[]{:S(2)}) collective-permute-start(bf16[448,1792]{1,0:T(8,128)(2,1)} %block_ref.3), channel_id=1, source_target_pairs={{0,2},{2,0},{4,6},{6,4},{8,10},{10,8},{12,14},{14,12},{1,3},{3,1},... | collective-permute-start | bytes 4816904 | tf_op jit(solution)/shard_map/ppermute | solution.py:288
  2.7 12.0 %copy-start.2 = (s32[56,2,14]{0,1,2:T(2,128)S(1)}, s32[56,2,14]{0,1,2:T(2,128)}, u32[]{:S(2)}) copy-start(s32[56,2,14]{0,1,2:T(2,128)} %param.9) | copy-start | bytes 18820
  2.7 16.7 %collective-permute-start.4 = (bf16[192,896]{1,0:T(8,128)(2,1)}, bf16[192,896]{1,0:T(8,128)(2,1)S(1)}, u32[]{:S(2)}, u32[]{:S(2)}) collective-permute-start(bf16[192,896]{1,0:T(8,128)(2,1)} %shard_map.58), channel_id=1, source_target_pairs={{0,4},{2,6},{4,0},{6,2},{8,12},{10,14},{12,8},{14,10},{1,5},{3,7},... | collective-permute-start | bytes 1032200 | tf_op jit(solution)/shard_map/ppermute | solution.py:288
  7.6 12.0 %copy-start.1 = (bf16[64,1792]{1,0:T(8,128)(2,1)S(1)}, bf16[64,1792]{1,0:T(8,128)(2,1)}, u32[]{:S(2)}) copy-start(bf16[64,1792]{1,0:T(8,128)(2,1)} %get-tuple-element.19) | copy-start | bytes 688132
  7.6 12.0 %collective-permute-start.1 = (bf16[64,1792]{1,0:T(8,128)(2,1)}, bf16[64,1792]{1,0:T(8,128)(2,1)S(1)}, u32[]{:S(2)}, u32[]{:S(2)}) collective-permute-start(bf16[64,1792]{1,0:T(8,128)(2,1)} %get-tuple-element.18), channel_id=1, source_target_pairs={{0,8},{2,10},{4,12},{6,14},{8,0},{10,2},{12,4},{14,6},{1,9},{3,11}... | collective-permute-start | bytes 688136 | tf_op jit(solution)/shard_map/ppermute | solution.py:288
  10.2 11.3 %collective-permute-start.6 = (bf16[64,1792]{1,0:T(8,128)(2,1)}, bf16[64,1792]{1,0:T(8,128)(2,1)S(1)}, u32[]{:S(2)}, u32[]{:S(2)}) collective-permute-start(bf16[64,1792]{1,0:T(8,128)(2,1)} %get-tuple-element.19), channel_id=1, source_target_pairs={{0,1},{1,0},{2,3},{3,2},{4,5},{5,4},{6,7},{7,6},{8,9},{9,8},{10,11... | collective-permute-start | bytes 688136 | tf_op jit(solution)/shard_map/ppermute | solution.py:289
  14.1 14.9 %collective-permute-start = (bf16[256,896]{1,0:T(8,128)(2,1)}, bf16[256,896]{1,0:T(8,128)(2,1)S(1)}, u32[]{:S(2)}, u32[]{:S(2)}) collective-permute-start(bf16[256,896]{1,0:T(8,128)(2,1)} %shard_map.55), channel_id=1, source_target_pairs={{0,4},{2,6},{4,0},{6,2},{8,12},{10,14},{12,8},{14,10},{1,5},{3,7},... | collective-permute-start | bytes 1376264 | tf_op jit(solution)/shard_map/ppermute | solution.py:288
  19.4 2.2 %collective-permute-start.5 = (bf16[192,896]{1,0:T(8,128)(2,1)S(1)}, bf16[192,896]{1,0:T(8,128)(2,1)S(1)}, u32[]{:S(2)}, u32[]{:S(2)}) collective-permute-start(bf16[192,896]{1,0:T(8,128)(2,1)S(1)} %collective-permute-done.4.z_ref), channel_id=1, source_target_pairs={{0,2},{2,0},{4,6},{6,4},{8,10},{10,8},{12,14},{14,12},{1,3},{3,1},... | collective-permute-start | bytes 1032200 | tf_op jit(solution)/shard_map/ppermute | solution.py:288
  19.6 3.7 %copy-start = (bf16[448,1792]{1,0:T(8,128)(2,1)S(1)}, bf16[448,1792]{1,0:T(8,128)(2,1)}, u32[]{:S(2)}) copy-start(bf16[448,1792]{1,0:T(8,128)(2,1)} %block_ref.3) | copy-start | bytes 4816900
  19.6 8.2 %collective-permute-start.2 = (bf16[64,1792]{1,0:T(8,128)(2,1)S(1)}, bf16[64,1792]{1,0:T(8,128)(2,1)S(1)}, u32[]{:S(2)}, u32[]{:S(2)}) collective-permute-start(bf16[64,1792]{1,0:T(8,128)(2,1)S(1)} %collective-permute-done.1), channel_id=1, source_target_pairs={{0,1},{1,0},{2,3},{3,2},{4,5},{5,4},{6,7},{7,6},{8,9},{9,8},{10,11... | collective-permute-start | bytes 688136 | tf_op jit(solution)/shard_map/ppermute | solution.py:289
  29.0 1.8 %collective-permute-start.7 = (bf16[256,896]{1,0:T(8,128)(2,1)S(1)}, bf16[256,896]{1,0:T(8,128)(2,1)S(1)}, u32[]{:S(2)}, u32[]{:S(2)}) collective-permute-start(bf16[256,896]{1,0:T(8,128)(2,1)S(1)} %collective-permute-done.z_ref), channel_id=1, source_target_pairs={{0,2},{2,0},{4,6},{6,4},{8,10},{10,8},{12,14},{14,12},{1,3},{3,1},... | collective-permute-start | bytes 1376264 | tf_op jit(solution)/shard_map/ppermute | solution.py:288
  32.8 19.5 %collective-permute-start.9 = (s16[57,16,128]{2,1,0:T(8,128)(2,1)S(1)}, s16[57,16,128]{2,1,0:T(8,128)(2,1)S(1)}, u32[]{:S(2)}, u32[]{:S(2)}) collective-permute-start(s16[57,16,128]{2,1,0:T(8,128)(2,1)S(1)} %get-tuple-element.27), channel_id=1, source_target_pairs={{0,8},{2,10},{4,12},{6,14},{8,0},{10,2},{12,4},{14,6},{1,9},{3,11}... | collective-permute-start | bytes 700424 | tf_op jit(solution)/shard_map/ppermute | solution.py:288
  37.1 20.4 %collective-permute-start.8 = (s16[57,16,128]{2,1,0:T(8,128)(2,1)S(1)}, s16[57,16,128]{2,1,0:T(8,128)(2,1)S(1)}, u32[]{:S(2)}, u32[]{:S(2)}) collective-permute-start(s16[57,16,128]{2,1,0:T(8,128)(2,1)S(1)} %shard_map.64._), channel_id=1, source_target_pairs={{0,9},{1,8},{2,11},{3,10},{4,13},{5,12},{6,15},{7,14},{8,1},{9,0},... | collective-permute-start | bytes 700424 | tf_op jit(solution)/shard_map/ppermute | solution.py:286
  38.9 14.3 %collective-permute-start.10 = (f32[32,1792]{1,0:T(8,128)S(1)}, f32[32,1792]{1,0:T(8,128)S(1)}, u32[]{:S(2)}, u32[]{:S(2)}) collective-permute-start(f32[32,1792]{1,0:T(8,128)S(1)} %get-tuple-element.29), channel_id=1, source_target_pairs={{0,1},{1,0},{2,3},{3,2},{4,5},{5,4},{6,7},{7,6},{8,9},{9,8},{10,11... | collective-permute-start | bytes 688136 | tf_op jit(solution)/shard_map/ppermute | solution.py:289
  39.3 13.9 %collective-permute-start.11 = (f32[32,1792]{1,0:T(8,128)S(1)}, f32[32,1792]{1,0:T(8,128)S(1)}, u32[]{:S(2)}, u32[]{:S(2)}) collective-permute-start(f32[32,1792]{1,0:T(8,128)S(1)} %get-tuple-element.30), channel_id=1, source_target_pairs={{0,1},{1,0},{2,3},{3,2},{4,5},{5,4},{6,7},{7,6},{8,9},{9,8},{10,11... | collective-permute-start | bytes 688136 | tf_op jit(solution)/shard_map/ppermute | solution.py:289
